TPU v7x, 32 devices: a whole 2x2x4 slice. The times are simulated.
32 devices in a mesh: dp: 8 (over z, y), tensor: 4 (over x, core).
Axes of the slice: x: 2, y: 2, z: 4, core: 2. Of those that a mesh axis runs over, the one named last changes fastest.
Arguments:
- inputs: bfloat16 [4096, 1024], P(('dp', 'tensor')), may hold values from -6 to 6
- cotangent: bfloat16 [4096, 1024], P(('dp', 'tensor')), may hold values from -6 to 6
- mix_gain: bfloat16 [1024], P('dp'), may hold values from 0.25 to 1.75
- query_weight: bfloat16 [1024, 512], P('dp', 'tensor'), may hold values from -0.1875 to 0.1875
- key_weight: bfloat16 [1024, 128], P('dp'), may hold values from -0.1875 to 0.1875
- value_weight: bfloat16 [1024, 128], P('dp'), may hold values from -0.1875 to 0.1875
- attention_out: bfloat16 [1024, 512], P('dp', 'tensor'), may hold values from -3 to 3
- mamba_gate: bfloat16 [1024, 1536], P('dp', 'tensor'), may hold values from -0.1875 to 0.1875
- mamba_input: bfloat16 [1024, 1536], P('dp', 'tensor'), may hold values from -0.1875 to 0.1875
- state_weight: bfloat16 [1024, 256], P('dp'), may hold values from -0.1875 to 0.1875
- step_weight: bfloat16 [1024, 24], P('dp', 'tensor'), may hold values from -0.1875 to 0.1875
- mamba_out: bfloat16 [1024, 1536], P('dp', 'tensor'), may hold values from -0.3125 to 0.3125
- kernel_weight: float32 [4, 1792], replicated, may hold values from -3 to 3
- kernel_bias: float32 [1792], replicated, may hold values from -3 to 3
- decay_log: float32 [24], replicated, may hold values from 0 to 2.77
- step_bias: float32 [24], replicated, may hold values from -4.5 to -2
- skip_weight: float32 [24], replicated, may hold values from 0.5 to 2
- mlp_gain: bfloat16 [1024], P('dp'), may hold values from 0.25 to 1.75
- gate_weight: bfloat16 [1024, 2048], P('dp', 'tensor'), may hold values from -0.1875 to 0.1875
- up_weight: bfloat16 [1024, 2048], P('dp', 'tensor'), may hold values from -0.1875 to 0.1875
- down_weight: bfloat16 [1024, 2048], P('dp', 'tensor'), may hold values from -0.1875 to 0.1875
Outputs:
- output: bfloat16 [4096, 1024], P(('dp', 'tensor'))
- grad_inputs: bfloat16 [4096, 1024], P(('dp', 'tensor'))
- grad_mix_gain: float32 [1024], P(('dp', 'tensor'))
- grad_query_weight: float32 [1024, 512], P('dp', 'tensor')
- grad_key_weight: float32 [1024, 128], P(('dp', 'tensor'))
- grad_value_weight: float32 [1024, 128], P(('dp', 'tensor'))
- grad_attention_out: float32 [1024, 512], P('dp', 'tensor')
- grad_mamba_gate: float32 [1024, 1536], P('dp', 'tensor')
- grad_mamba_input: float32 [1024, 1536], P('dp', 'tensor')
- grad_state_weight: float32 [1024, 256], P(('dp', 'tensor'))
- grad_step_weight: float32 [1024, 24], P('dp', 'tensor')
- grad_mamba_out: float32 [1024, 1536], P('dp', 'tensor')
- grad_kernel_weight: float32 [4, 1792], replicated
- grad_kernel_bias: float32 [1792], replicated
- grad_decay_log: float32 [24], replicated
- grad_step_bias: float32 [24], replicated
- grad_skip_weight: float32 [24], replicated
- grad_mlp_gain: float32 [1024], P(('dp', 'tensor'))
- grad_gate_weight: float32 [1024, 2048], P('dp', 'tensor')
- grad_up_weight: float32 [1024, 2048], P('dp', 'tensor')
- grad_down_weight: float32 [1024, 2048], P('dp', 'tensor')
All inputs are finite; a program needn't handle non-finite values.
Results may differ from a plain program's by a relative error of at most 0.02.
Values may be sent and summed in bfloat16 or wider, within the bound.
A program may use at most 128 MiB of HBM per device.

v0:
```python
import math

import jax
import jax.numpy as jnp
from jax import lax
from jax.sharding import PartitionSpec as P

D = 1024
HEADS = 8
KV_HEADS = 2
HEAD_DIM = 64
SSM_HEADS = 24
SSM_HEAD_DIM = 64
STATE = 128
KCONV = 4
SCAN_BLOCK = 128


eps = 1e-05
rope_base = 100000000000.0
highest = lax.Precision.HIGHEST
by_rows = (((0,), (0,)), ((), ()))
by_columns = (((1,), (1,)), ((), ()))


def rms_norm(values, gain_vector):
    return values * lax.rsqrt(jnp.mean(values * values, -1, keepdims=True) + eps) * gain_vector


def rotary_tables(length):
    half_dim = HEAD_DIM // 2
    frequency = jnp.exp(
        jnp.arange(half_dim, dtype=jnp.float32) * (-2.0 * math.log(rope_base) / HEAD_DIM)
    )
    angles = jnp.arange(length, dtype=jnp.float32)[:, None] * frequency[None, :]
    return (jnp.cos(angles)[:, None, :], jnp.sin(angles)[:, None, :])


def rotary(values, cosine_table, sine_table):
    half_dim = values.shape[-1] // 2
    former = values[..., :half_dim]
    latter = values[..., half_dim:]
    return jnp.concatenate(
        [former * cosine_table - latter * sine_table, latter * cosine_table + former * sine_table],
        -1,
    )


def unrotate(gradient, cosine_table, sine_table):
    half_dim = gradient.shape[-1] // 2
    former = gradient[..., :half_dim]
    latter = gradient[..., half_dim:]
    return jnp.concatenate(
        [former * cosine_table + latter * sine_table, latter * cosine_table - former * sine_table],
        -1,
    )


def causal_conv(signal, kernel, offset):
    length = signal.shape[0]
    tap_count = kernel.shape[0]
    padded = jnp.concatenate(
        [jnp.zeros((tap_count - 1,) + signal.shape[1:], signal.dtype), signal], 0
    )
    result = offset
    for lag_index in range(tap_count):
        result = result + kernel[lag_index] * padded[lag_index : lag_index + length]
    return result


def ssd_scan(series, step_sizes, decay_rates, input_map, output_map, skip_gain):
    length, group_count, head_count, head_width = series.shape
    blocks = length // SCAN_BLOCK

    def by_block(values):
        return values.reshape((blocks, SCAN_BLOCK) + values.shape[1:])

    def advance(carry_state, block_data):
        series_block, step_block, input_block, output_block = block_data
        cumulative = jnp.cumsum(step_block * decay_rates, axis=0)
        row_index = lax.broadcasted_iota(jnp.int32, (SCAN_BLOCK, SCAN_BLOCK), 0)
        earlier = lax.broadcasted_iota(jnp.int32, (SCAN_BLOCK, SCAN_BLOCK), 1)
        causal = (row_index >= earlier)[:, :, None, None]
        log_gaps = jnp.where(causal, cumulative[:, None] - cumulative[None, :], -1e30)
        affinity = jnp.einsum("tgn,sgn->tsg", output_block, input_block, precision=highest)
        weights = jnp.exp(log_gaps) * affinity[..., None]
        scaled = series_block * step_block[..., None]
        within = jnp.einsum("tsgj,sgjp->tgjp", weights, scaled, precision=highest)
        carried = (
            jnp.einsum("tgn,gjpn->tgjp", output_block, carry_state, precision=highest)
            * jnp.exp(cumulative)[..., None]
        )
        remain = jnp.exp(cumulative[-1][None] - cumulative)
        written = jnp.einsum(
            "sgjp,sgn->gjpn", scaled * remain[..., None], input_block, precision=highest
        )
        carry_state = carry_state * jnp.exp(cumulative[-1])[..., None, None] + written
        return (carry_state, within + carried + series_block * skip_gain[..., None])

    initial = jnp.zeros((group_count, head_count, head_width, input_map.shape[-1]), jnp.float32)
    _, outputs = lax.scan(
        advance,
        initial,
        (by_block(series), by_block(step_sizes), by_block(input_map), by_block(output_map)),
    )
    return outputs.reshape(series.shape)


def mamba_core(
    gate_proj,
    input_proj,
    state_proj,
    step_proj,
    kernel_local,
    bias_local,
    decay_local,
    step_local,
    skip_local,
):
    length, channel_count = input_proj.shape
    heads_here = step_proj.shape[1]
    activated = jax.nn.silu(
        causal_conv(jnp.concatenate([input_proj, state_proj], 1), kernel_local, bias_local)
    )
    series = activated[:, :channel_count].reshape(
        length, 1, heads_here, channel_count // heads_here
    )
    input_map = activated[:, channel_count : channel_count + STATE][:, None]
    output_map = activated[:, channel_count + STATE :][:, None]
    step_sizes = jax.nn.softplus(step_proj + step_local)[:, None]
    decay_rates = (-jnp.exp(decay_local))[None]
    scanned = ssd_scan(series, step_sizes, decay_rates, input_map, output_map, skip_local[None])
    return scanned.reshape(length, channel_count) * jax.nn.silu(gate_proj)


def full_rows(local_piece):
    return lax.all_gather(local_piece, "tensor", axis=0, tiled=True)


def summed_rows(operand_pairs, row_count):
    running = jnp.zeros(
        (row_count * lax.axis_size("tensor"), operand_pairs[0][1].shape[0]), jnp.float32
    )
    for left_side, right_side in operand_pairs:
        running = running + lax.dot_general(
            left_side, right_side, by_columns, preferred_element_type=jnp.float32
        )
    return lax.psum_scatter(
        running.astype(jnp.bfloat16), "tensor", scatter_dimension=0, tiled=True
    ).astype(jnp.float32)


def weight_grad(activations, gradient):
    return lax.dot_general(activations, gradient, by_rows, preferred_element_type=jnp.float32)


def block_scores(query_block, key_rot, first_row, score_scale):
    raw_scores = (
        jnp.einsum("qhd,kd->hqk", query_block, key_rot, preferred_element_type=jnp.float32)
        * score_scale
    )
    row_index = first_row + lax.broadcasted_iota(jnp.int32, raw_scores.shape, 1)
    column_index = lax.broadcasted_iota(jnp.int32, raw_scores.shape, 2)
    return jnp.where(column_index <= row_index, raw_scores, -1e30)


def local(
    inputs,
    cotangent,
    mix_gain,
    query_weight,
    key_weight,
    value_weight,
    attention_out,
    mamba_gate,
    mamba_input,
    state_weight,
    step_weight,
    mamba_out,
    kernel_weight,
    kernel_bias,
    decay_log,
    step_bias,
    skip_weight,
    mlp_gain,
    gate_weight,
    up_weight,
    down_weight,
):
    tensor_index = lax.axis_index("tensor")
    local_rows = inputs.shape[0]
    mix_gathered = (
        lax.all_gather(mix_gain, "dp", axis=0, tiled=True),
        lax.all_gather(query_weight, "dp", axis=0, tiled=True),
        lax.all_gather(key_weight, "dp", axis=0, tiled=True),
        lax.all_gather(value_weight, "dp", axis=0, tiled=True),
        lax.all_gather(attention_out, "dp", axis=0, tiled=True),
        lax.all_gather(mamba_gate, "dp", axis=0, tiled=True),
        lax.all_gather(mamba_input, "dp", axis=0, tiled=True),
        lax.all_gather(state_weight, "dp", axis=0, tiled=True),
        lax.all_gather(step_weight, "dp", axis=0, tiled=True),
        lax.all_gather(mamba_out, "dp", axis=0, tiled=True),
    )
    (
        mix_gain_all,
        query_all,
        key_all,
        value_all,
        attention_all,
        gate_ssm_all,
        input_ssm_all,
        state_all,
        step_all,
        mamba_out_all,
    ) = mix_gathered
    mlp_gathered = (
        lax.all_gather(mlp_gain, "dp", axis=0, tiled=True),
        lax.all_gather(gate_weight, "dp", axis=0, tiled=True),
        lax.all_gather(up_weight, "dp", axis=0, tiled=True),
        lax.all_gather(down_weight, "dp", axis=0, tiled=True),
    )
    mlp_gain_all, gate_all, up_all, down_all = mlp_gathered
    query_heads = query_all.shape[1] // HEAD_DIM
    key_head = tensor_index * query_heads // (HEADS // KV_HEADS)
    scan_width = input_ssm_all.shape[1]
    scan_heads = step_all.shape[1]
    full_width = SSM_HEADS * SSM_HEAD_DIM
    kernel_local = jnp.concatenate(
        [
            lax.dynamic_slice_in_dim(kernel_weight, tensor_index * scan_width, scan_width, 1),
            kernel_weight[:, full_width:],
        ],
        1,
    )
    bias_local = jnp.concatenate(
        [
            lax.dynamic_slice_in_dim(kernel_bias, tensor_index * scan_width, scan_width, 0),
            kernel_bias[full_width:],
        ],
        0,
    )
    decay_local = lax.dynamic_slice_in_dim(decay_log, tensor_index * scan_heads, scan_heads, 0)
    step_local = lax.dynamic_slice_in_dim(step_bias, tensor_index * scan_heads, scan_heads, 0)
    skip_local = lax.dynamic_slice_in_dim(skip_weight, tensor_index * scan_heads, scan_heads, 0)
    rows_float = inputs.astype(jnp.float32)
    normed, first_norm_back = jax.vjp(rms_norm, rows_float, mix_gain_all.astype(jnp.float32))
    normed_local = normed.astype(jnp.bfloat16)
    mixer_rows = full_rows(normed_local)
    length = mixer_rows.shape[0]
    cosine_table, sine_table = rotary_tables(length)
    key_slice = lax.dynamic_slice_in_dim(key_all, key_head * HEAD_DIM, HEAD_DIM, 1)
    value_slice = lax.dynamic_slice_in_dim(value_all, key_head * HEAD_DIM, HEAD_DIM, 1)
    query_proj = jnp.dot(mixer_rows, query_all, preferred_element_type=jnp.float32).reshape(
        length, query_heads, HEAD_DIM
    )
    key_proj = jnp.dot(mixer_rows, key_slice, preferred_element_type=jnp.float32)
    value_proj = jnp.dot(mixer_rows, value_slice, preferred_element_type=jnp.float32)
    query_rot = rotary(query_proj, cosine_table, sine_table).astype(jnp.bfloat16)
    key_rot = rotary(key_proj[:, None], cosine_table, sine_table)[:, 0].astype(jnp.bfloat16)
    value_low = value_proj.astype(jnp.bfloat16)
    block_rows = min(512, length)
    block_count = length // block_rows
    score_scale = HEAD_DIM ** (-0.5)
    block_ids = jnp.arange(block_count, dtype=jnp.int32)

    def attend_block(block_index):
        first_row = block_index * block_rows
        scores = block_scores(query_rot, key_rot, first_row, score_scale)
        row_max = jnp.max(scores, -1, keepdims=True)
        shifted = jnp.exp(scores - row_max)
        row_total = jnp.sum(shifted, -1, keepdims=True)
        weights_low = (shifted / row_total).astype(jnp.bfloat16)
        attended = jnp.einsum(
            "hqk,kd->qhd", weights_low, value_low, preferred_element_type=jnp.float32
        )
        return (attended, (row_max + jnp.log(row_total))[..., 0])

    attended_blocks, log_totals = lax.map(attend_block, block_ids)
    attended_low = attended_blocks.reshape(length, query_heads * HEAD_DIM).astype(jnp.bfloat16)
    gate_proj = jnp.dot(mixer_rows, gate_ssm_all, preferred_element_type=jnp.float32)
    input_proj = jnp.dot(mixer_rows, input_ssm_all, preferred_element_type=jnp.float32)
    state_proj = jnp.dot(mixer_rows, state_all, preferred_element_type=jnp.float32)
    step_proj = jnp.dot(mixer_rows, step_all, preferred_element_type=jnp.float32)
    gated_out, mamba_back = jax.vjp(
        mamba_core,
        gate_proj,
        input_proj,
        state_proj,
        step_proj,
        kernel_local,
        bias_local,
        decay_local,
        step_local,
        skip_local,
    )
    gated_low = gated_out.astype(jnp.bfloat16)
    mixed = summed_rows(((attended_low, attention_all), (gated_low, mamba_out_all)), local_rows)
    hidden = rows_float + mixed
    normed_mlp, second_norm_back = jax.vjp(rms_norm, hidden, mlp_gain_all.astype(jnp.float32))
    normed_mlp_local = normed_mlp.astype(jnp.bfloat16)
    mlp_rows = full_rows(normed_mlp_local)
    gate_pre = jnp.dot(mlp_rows, gate_all, preferred_element_type=jnp.float32)
    up_pre = jnp.dot(mlp_rows, up_all, preferred_element_type=jnp.float32)
    sigmoid_gate = jax.nn.sigmoid(gate_pre)
    silu_gate = gate_pre * sigmoid_gate
    units_low = (silu_gate * up_pre).astype(jnp.bfloat16)
    mlp_sum = summed_rows(((units_low, down_all),), local_rows)
    output = (hidden + mlp_sum).astype(jnp.bfloat16)
    gate_back, up_back, down_back = (
        lax.all_gather(gate_weight, "dp", axis=0, tiled=True),
        lax.all_gather(up_weight, "dp", axis=0, tiled=True),
        lax.all_gather(down_weight, "dp", axis=0, tiled=True),
    )
    (
        query_back,
        key_back,
        value_back,
        attention_back,
        gate_ssm_back,
        input_ssm_back,
        state_back,
        step_back,
        mamba_out_back,
    ) = (
        lax.all_gather(query_weight, "dp", axis=0, tiled=True),
        lax.all_gather(key_weight, "dp", axis=0, tiled=True),
        lax.all_gather(value_weight, "dp", axis=0, tiled=True),
        lax.all_gather(attention_out, "dp", axis=0, tiled=True),
        lax.all_gather(mamba_gate, "dp", axis=0, tiled=True),
        lax.all_gather(mamba_input, "dp", axis=0, tiled=True),
        lax.all_gather(state_weight, "dp", axis=0, tiled=True),
        lax.all_gather(step_weight, "dp", axis=0, tiled=True),
        lax.all_gather(mamba_out, "dp", axis=0, tiled=True),
    )
    cotangent_rows = full_rows(cotangent)
    grad_down = weight_grad(cotangent_rows, units_low)
    unit_grad = jnp.dot(cotangent_rows, down_back, preferred_element_type=jnp.float32)
    gate_grad = (
        unit_grad * up_pre * (sigmoid_gate * (1.0 + gate_pre * (1.0 - sigmoid_gate)))
    ).astype(jnp.bfloat16)
    up_grad = (unit_grad * silu_gate).astype(jnp.bfloat16)
    grad_gate = weight_grad(mlp_rows, gate_grad)
    grad_up = weight_grad(mlp_rows, up_grad)
    mlp_input_grad = summed_rows(((gate_grad, gate_back), (up_grad, up_back)), local_rows)
    hidden_norm_grad, grad_mlp_gain = second_norm_back(mlp_input_grad)
    hidden_grad = cotangent.astype(jnp.float32) + hidden_norm_grad
    mixer_grad_rows = full_rows(hidden_grad.astype(jnp.bfloat16))
    grad_attention = weight_grad(mixer_grad_rows, attended_low)
    grad_mamba_out = weight_grad(mixer_grad_rows, gated_low)
    attended_grad = (
        jnp.dot(mixer_grad_rows, attention_back, preferred_element_type=jnp.float32)
        .astype(jnp.bfloat16)
        .reshape(length, query_heads, HEAD_DIM)
    )
    gated_grad = jnp.dot(mixer_grad_rows, mamba_out_back, preferred_element_type=jnp.float32)

    def attend_back(carried, block_index):
        key_total, value_total = carried
        first_row = block_index * block_rows
        scores = block_scores(query_rot, key_rot, first_row, score_scale)
        probabilities = jnp.exp(scores - log_totals[block_index][..., None])
        prob_grad = jnp.einsum(
            "qhd,kd->hqk", attended_grad, value_low, preferred_element_type=jnp.float32
        )
        row_dot = jnp.sum(prob_grad * probabilities, -1, keepdims=True)
        score_grad = (probabilities * (prob_grad - row_dot)).astype(jnp.bfloat16)
        query_grad = (
            jnp.einsum("hqk,kd->qhd", score_grad, key_rot, preferred_element_type=jnp.float32)
            * score_scale
        )
        key_total = (
            key_total
            + jnp.einsum("hqk,qhd->kd", score_grad, query_rot, preferred_element_type=jnp.float32)
            * score_scale
        )
        value_total = value_total + jnp.einsum(
            "hqk,qhd->kd",
            probabilities.astype(jnp.bfloat16),
            attended_grad,
            preferred_element_type=jnp.float32,
        )
        return ((key_total, value_total), query_grad)

    zero_keys = jnp.zeros((length, HEAD_DIM), jnp.float32)
    (key_total, value_total), query_grads = lax.scan(attend_back, (zero_keys, zero_keys), block_ids)
    query_low = (
        unrotate(query_grads.reshape(length, query_heads, HEAD_DIM), cosine_table, sine_table)
        .astype(jnp.bfloat16)
        .reshape(length, query_heads * HEAD_DIM)
    )
    key_low = unrotate(key_total[:, None], cosine_table, sine_table)[:, 0].astype(jnp.bfloat16)
    value_grad_low = value_total.astype(jnp.bfloat16)
    (
        gate_proj_grad,
        input_proj_grad,
        state_proj_grad,
        step_proj_grad,
        kernel_grad,
        bias_grad,
        decay_grad,
        step_bias_grad,
        skip_grad,
    ) = mamba_back(gated_grad)
    gate_proj_low = gate_proj_grad.astype(jnp.bfloat16)
    input_proj_low = input_proj_grad.astype(jnp.bfloat16)
    state_proj_low = state_proj_grad.astype(jnp.bfloat16)
    step_proj_low = step_proj_grad.astype(jnp.bfloat16)
    key_slice_back = lax.dynamic_slice_in_dim(key_back, key_head * HEAD_DIM, HEAD_DIM, 1)
    value_slice_back = lax.dynamic_slice_in_dim(value_back, key_head * HEAD_DIM, HEAD_DIM, 1)
    mixer_input_grad = summed_rows(
        (
            (query_low, query_back),
            (key_low, key_slice_back),
            (value_grad_low, value_slice_back),
            (gate_proj_low, gate_ssm_back),
            (input_proj_low, input_ssm_back),
            (state_proj_low, state_back),
            (step_proj_low, step_back),
        ),
        local_rows,
    )
    input_norm_grad, grad_mix_gain = first_norm_back(mixer_input_grad)
    grad_inputs = (hidden_grad + input_norm_grad).astype(jnp.bfloat16)
    grad_query = weight_grad(mixer_rows, query_low)
    key_width = key_all.shape[1]
    grad_key = lax.dynamic_update_slice_in_dim(
        jnp.zeros((D, key_width), jnp.float32),
        weight_grad(mixer_rows, key_low),
        key_head * HEAD_DIM,
        1,
    )
    grad_value = lax.dynamic_update_slice_in_dim(
        jnp.zeros((D, key_width), jnp.float32),
        weight_grad(mixer_rows, value_grad_low),
        key_head * HEAD_DIM,
        1,
    )
    grad_gate_ssm = weight_grad(mixer_rows, gate_proj_low)
    grad_input_ssm = weight_grad(mixer_rows, input_proj_low)
    grad_state = weight_grad(mixer_rows, state_proj_low)
    grad_step = weight_grad(mixer_rows, step_proj_low)
    kernel_full = jnp.concatenate(
        [
            lax.dynamic_update_slice_in_dim(
                jnp.zeros((KCONV, full_width), jnp.float32),
                kernel_grad[:, :scan_width],
                tensor_index * scan_width,
                1,
            ),
            kernel_grad[:, scan_width:],
        ],
        1,
    )
    bias_full = jnp.concatenate(
        [
            lax.dynamic_update_slice_in_dim(
                jnp.zeros((full_width,), jnp.float32),
                bias_grad[:scan_width],
                tensor_index * scan_width,
                0,
            ),
            bias_grad[scan_width:],
        ],
        0,
    )
    decay_full = lax.dynamic_update_slice_in_dim(
        jnp.zeros((SSM_HEADS,), jnp.float32), decay_grad, tensor_index * scan_heads, 0
    )
    step_bias_full = lax.dynamic_update_slice_in_dim(
        jnp.zeros((SSM_HEADS,), jnp.float32), step_bias_grad, tensor_index * scan_heads, 0
    )
    skip_full = lax.dynamic_update_slice_in_dim(
        jnp.zeros((SSM_HEADS,), jnp.float32), skip_grad, tensor_index * scan_heads, 0
    )
    mix_sums = (
        lax.psum_scatter(grad_query, "dp", scatter_dimension=0, tiled=True),
        lax.psum_scatter(grad_attention, "dp", scatter_dimension=0, tiled=True),
        lax.psum_scatter(grad_gate_ssm, "dp", scatter_dimension=0, tiled=True),
        lax.psum_scatter(grad_input_ssm, "dp", scatter_dimension=0, tiled=True),
        lax.psum_scatter(grad_step, "dp", scatter_dimension=0, tiled=True),
        lax.psum_scatter(grad_mamba_out, "dp", scatter_dimension=0, tiled=True),
    )
    mlp_sums = (
        lax.psum_scatter(grad_gate, "dp", scatter_dimension=0, tiled=True),
        lax.psum_scatter(grad_up, "dp", scatter_dimension=0, tiled=True),
        lax.psum_scatter(grad_down, "dp", scatter_dimension=0, tiled=True),
    )
    shared_sums = (
        lax.psum_scatter(grad_mix_gain, ("dp", "tensor"), scatter_dimension=0, tiled=True),
        lax.psum_scatter(grad_mlp_gain, ("dp", "tensor"), scatter_dimension=0, tiled=True),
        lax.psum_scatter(grad_key, ("dp", "tensor"), scatter_dimension=0, tiled=True),
        lax.psum_scatter(grad_value, ("dp", "tensor"), scatter_dimension=0, tiled=True),
        lax.psum_scatter(grad_state, ("dp", "tensor"), scatter_dimension=0, tiled=True),
    )
    small_sums = lax.psum(
        (kernel_full, bias_full, decay_full, step_bias_full, skip_full), ("dp", "tensor")
    )
    return (
        output,
        grad_inputs,
        shared_sums[0],
        mix_sums[0],
        shared_sums[2],
        shared_sums[3],
        mix_sums[1],
        mix_sums[2],
        mix_sums[3],
        shared_sums[4],
        mix_sums[4],
        mix_sums[5],
        small_sums[0],
        small_sums[1],
        small_sums[2],
        small_sums[3],
        small_sums[4],
        shared_sums[1],
        mlp_sums[0],
        mlp_sums[1],
        mlp_sums[2],
    )


def solution(mesh):
    placed = (
        P(("dp", "tensor"), None),
        P(("dp", "tensor"), None),
        P("dp"),
        P("dp", "tensor"),
        P("dp", None),
        P("dp", None),
        P("dp", "tensor"),
        P("dp", "tensor"),
        P("dp", "tensor"),
        P("dp", None),
        P("dp", "tensor"),
        P("dp", "tensor"),
        P(),
        P(),
        P(),
        P(),
        P(),
        P("dp"),
        P("dp", "tensor"),
        P("dp", "tensor"),
        P("dp", "tensor"),
    )
    return jax.shard_map(
        local,
        mesh=mesh,
        in_specs=placed,
        out_specs=(
            P(("dp", "tensor"), None),
            P(("dp", "tensor"), None),
            P(("dp", "tensor")),
            P("dp", "tensor"),
            P(("dp", "tensor"), None),
            P(("dp", "tensor"), None),
            P("dp", "tensor"),
            P("dp", "tensor"),
            P("dp", "tensor"),
            P(("dp", "tensor"), None),
            P("dp", "tensor"),
            P("dp", "tensor"),
            P(),
            P(),
            P(),
            P(),
            P(),
            P(("dp", "tensor")),
            P("dp", "tensor"),
            P("dp", "tensor"),
            P("dp", "tensor"),
        ),
        check_vma=False,
    )
```

profile of v0, /device:TPU:0, one launch (start us, length us, event | category | flops | bytes accessed | tf_op | source)
XLA Modules:
  0.0 1771.6 jit_solution(307518311492428193)
XLA Ops:
  9.9 22.3 %all-gather = bf16[8,1,128]{2,1,0:T(2,128)(2,1)S(1)} all-gather(bf16[1,1,128]{2,1,0:T(2,128)(2,1)} %bitcast.651), channel_id=1, replica_groups=mesh['dp'=8,'tensor'=4] {'dp'}, dimensions={0}, use_global_device_ids=true | all-gather | bytes 2304 | tf_op jit(solution)/shard_map/all_gather | solution.py:193
  36.5 26.1 %all_gather.72 = bf16[1024,6]{0,1:T(8,128)(2,1)S(1)} all-gather(bf16[128,6]{0,1:T(8,128)(2,1)} %param.35), channel_id=1, replica_groups=mesh['dp'=8,'tensor'=4] {'dp'}, dimensions={0}, use_global_device_ids=true | all-gather | bytes 13824 | tf_op jit(solution)/shard_map/all_gather | solution.py:201
  64.5 33.0 %all_gather.69 = bf16[1024,128]{1,0:T(8,128)(2,1)} all-gather(bf16[128,128]{1,0:T(8,128)(2,1)} %param.29), channel_id=1, replica_groups=mesh['dp'=8,'tensor'=4] {'dp'}, dimensions={0}, use_global_device_ids=true | all-gather | bytes 294912 | tf_op jit(solution)/shard_map/all_gather | solution.py:195
  97.5 33.0 %all_gather.70 = bf16[1024,128]{1,0:T(8,128)(2,1)} all-gather(bf16[128,128]{1,0:T(8,128)(2,1)} %param.28), channel_id=1, replica_groups=mesh['dp'=8,'tensor'=4] {'dp'}, dimensions={0}, use_global_device_ids=true | all-gather | bytes 294912 | tf_op jit(solution)/shard_map/all_gather | solution.py:194
  130.5 33.0 %all_gather.68 = bf16[1024,128]{1,0:T(8,128)(2,1)} all-gather(bf16[128,128]{1,0:T(8,128)(2,1)S(1)} %copy-done.94), channel_id=1, replica_groups=mesh['dp'=8,'tensor'=4] {'dp'}, dimensions={0}, use_global_device_ids=true | all-gather | bytes 294912 | tf_op jit(solution)/shard_map/all_gather | solution.py:196
  163.4 32.9 %all_gather.71 = bf16[1024,128]{1,0:T(8,128)(2,1)} all-gather(bf16[128,128]{1,0:T(8,128)(2,1)S(1)} %copy-done.95), channel_id=1, replica_groups=mesh['dp'=8,'tensor'=4] {'dp'}, dimensions={0}, use_global_device_ids=true | all-gather | bytes 294912 | tf_op jit(solution)/shard_map/all_gather | solution.py:197
  197.4 31.7 %all_gather.74 = bf16[1024,256]{1,0:T(8,128)(2,1)S(1)} all-gather(bf16[128,256]{1,0:T(8,128)(2,1)S(1)} %copy-done.81), channel_id=1, replica_groups=mesh['dp'=8,'tensor'=4] {'dp'}, dimensions={0}, use_global_device_ids=true | all-gather | bytes 589824 | tf_op jit(solution)/shard_map/all_gather | solution.py:200
  229.1 32.3 %all_gather.73 = bf16[1024,384]{1,0:T(8,128)(2,1)S(1)} all-gather(bf16[128,384]{1,0:T(8,128)(2,1)S(1)} %copy-done.76), channel_id=1, replica_groups=mesh['dp'=8,'tensor'=4] {'dp'}, dimensions={0}, use_global_device_ids=true | all-gather | bytes 884736 | tf_op jit(solution)/shard_map/all_gather | solution.py:199
  261.3 33.7 %all_gather.75 = bf16[1024,384]{1,0:T(8,128)(2,1)} all-gather(bf16[128,384]{1,0:T(8,128)(2,1)S(1)} %copy-done.77), channel_id=1, replica_groups=mesh['dp'=8,'tensor'=4] {'dp'}, dimensions={0}, use_global_device_ids=true | all-gather | bytes 884736 | tf_op jit(solution)/shard_map/all_gather | solution.py:198
  295.0 34.1 %all_gather.76 = bf16[1024,384]{1,0:T(8,128)(2,1)} all-gather(bf16[128,384]{1,0:T(8,128)(2,1)S(1)} %copy-done.78), channel_id=1, replica_groups=mesh['dp'=8,'tensor'=4] {'dp'}, dimensions={0}, use_global_device_ids=true | all-gather | bytes 884736 | tf_op jit(solution)/shard_map/all_gather | solution.py:202
  332.4 2.7 fusion.126
  338.2 65.5 %while.82 = (s32[]{:T(128)}, f32[1,6,64,128]{3,2,1,0:T(8,128)S(1)}, f32[4,128,1,6,64]{1,0,4,3,2:T(4,128)}, f32[4,128,128,1,6]{2,1,4,3,0:T(8,128)}, f32[4,128,128...) while((s32[]{:T(128)}, f32[1,6,64,128]{3,2,1,0:T(8,128)S(1)}, ...), condition=%wide.region_5.6_spmd.clone.clone, body=%wide.region_3.5_spmd.clone.clone.sunk | while | flops 253036800 | bytes 4982733 | solution.py:101
  343.4 6.0 dynamic_update_slice.239
  359.8 6.0 dynamic_update_slice.239
  376.1 6.0 dynamic_update_slice.239
  392.6 6.0 dynamic_update_slice.239
  418.0 16.2 all-gather.1
  434.2 5.8 reduce-scatter.17.cloned.1.call-done
  445.2 12.7 all-gather.14.cloned.1.call-done
  457.9 17.2 all-gather.12.cloned.1.call-done
  475.1 3.3 fusion.203
  478.4 39.4 %all-gather.16.cloned.1.call-done = bf16[1024,512]{1,0:T(8,128)(2,1)} async-done(((bf16[128,512]{1,0:T(8,128)(2,1)}), bf16[1024,512]{1,0:T(8,128)(2,1)}) %all-gather.16.cloned.1.call-update) | async-done | bytes 1048592 | tf_op jit(solution)/shard_map/all_gather | solution.py:219
  517.8 3.2 fusion.204
  521.0 13.5 all-gather.20.cloned.1.call-done
  534.6 42.8 %all-gather.18.cloned.1.call-done = bf16[1024,512]{1,0:T(8,128)(2,1)} async-done(((bf16[128,512]{1,0:T(8,128)(2,1)}), bf16[1024,512]{1,0:T(8,128)(2,1)}) %all-gather.18.cloned.1.call-update) | async-done | bytes 1048592 | tf_op jit(solution)/shard_map/all_gather | solution.py:220
  577.3 4.1 multiply_convert_fusion
  584.9 23.5 %reduce-scatter.21.cloned.1.call-done = bf16[128,1024]{1,0:T(8,128)(2,1)} async-done(((bf16[512,1024]{1,0:T(8,128)(2,1)}), bf16[128,1024]{1,0:T(8,128)(2,1)}) %reduce-scatter.21.cloned.1.call-update) | async-done | bytes 262160 | tf_op jit(solution)/shard_map/reduce_scatter | solution.py:148
  613.1 3.5 convolution_bitcast_fusion.9
  616.6 12.4 all-gather.22.cloned.1.call-done
  629.0 3.8 fusion.137
  632.9 2.3 copy.216
  635.2 2.3 reshape.1204
  640.6 107.0 %while.81 = (s32[]{:T(128)}, f32[1,6]{1,0:T(1,128)S(1)}, f32[1,6]{1,0:T(1,128)S(1)}, f32[1,6,64,128]{3,2,1,0:T(8,128)S(1)}, f32[4,128,1,6,64]{1,0,4,3,2:T(4,128)...) while((s32[]{:T(128)}, f32[1,6]{1,0:T(1,128)S(1)}, ...), condition=%wide.region_24.25_spmd.clone, body=%wide.region_12.24_spmd.clone.sunk | while | flops 505256736 | bytes 6948834 | solution.py:101
  646.2 6.0 dynamic_update_slice.228
  653.1 2.0 fusion.350
  664.2 2.1 fusion.361
  672.9 6.0 dynamic_update_slice.228
  679.8 2.0 fusion.350
  690.9 2.1 fusion.361
  699.6 6.0 dynamic_update_slice.228
  706.5 2.0 fusion.350
  717.6 2.1 fusion.361
  726.3 6.0 dynamic_update_slice.228
  733.2 2.0 fusion.350
  744.3 2.1 fusion.361
  747.7 2.1 copy.292
  761.8 5.8 multiply_reduce_fusion.3
  783.0 2.0 fusion.217
  786.1 2.1 fusion.218
  789.5 2.3 dynamic_update_slice.149
  796.7 2.8 dynamic_update_slice.150
  811.9 41.9 %all-reduce.16 = (f32[1024]{0:T(1024)S(1)}, f32[4,1792]{1,0:T(4,128)}, f32[1792]{0:T(1024)}, f32[24]{0:T(128)}, f32[24]{0:T(128)}, /*index=5*/f32[24]{0:T(128)}, f32[1024]{0:T(1024)S(1)}) all-reduce(f32[1024]{0:T(1024)S(1)} %get-tuple-element.1500, ...), channel_id=6, replica_groups=mesh['dp'=8,'tensor'=4] {'dp','tensor'}, use_global_device_ids=true, to_apply=%region_28.29.clone | all-reduce | flops 11080 | bytes 88640
  855.0 2.2 fusion.149
  857.2 32.3 %reduce-scatter.39.cloned.1.call-done = f32[128,6]{0,1:T(8,128)} async-done(((f32[1024,6]{0,1:T(8,128)}), f32[128,6]{0,1:T(8,128)}) %reduce-scatter.39.cloned.1.call-update) | async-done | bytes 3088 | tf_op jit(solution)/shard_map/reduce_scatter | solution.py:480
  889.5 71.0 %reduce-scatter.43.cloned.1.call-done = f32[128,512]{1,0:T(8,128)} async-done(((f32[1024,512]{1,0:T(8,128)}), f32[128,512]{1,0:T(8,128)}) %reduce-scatter.43.cloned.1.call-update) | async-done | bytes 262160 | tf_op jit(solution)/shard_map/reduce_scatter | solution.py:484
  960.5 70.9 %reduce-scatter.45.cloned.1.call-done = f32[128,512]{1,0:T(8,128)} async-done(((f32[1024,512]{1,0:T(8,128)}), f32[128,512]{1,0:T(8,128)}) %reduce-scatter.45.cloned.1.call-update) | async-done | bytes 262160 | tf_op jit(solution)/shard_map/reduce_scatter | solution.py:485
  1031.4 135.4 %reduce-scatter.27.cloned.1.call-done = f32[32,128]{1,0:T(8,128)} async-done(((f32[1024,128]{1,0:T(8,128)}), f32[32,128]{1,0:T(8,128)}) %reduce-scatter.27.cloned.1.call-update) | async-done | bytes 16400 | tf_op jit(solution)/shard_map/reduce_scatter | solution.py:491
  1166.8 62.1 %reduce-scatter.31.cloned.1.call-done = f32[128,128]{1,0:T(8,128)} async-done(((f32[1024,128]{1,0:T(8,128)}), f32[128,128]{1,0:T(8,128)}) %reduce-scatter.31.cloned.1.call-update) | async-done | bytes 65552 | tf_op jit(solution)/shard_map/reduce_scatter | solution.py:477
  1228.8 65.0 %reduce-scatter.25.cloned.1.call-done = f32[128,128]{1,0:T(8,128)} async-done(((f32[1024,128]{1,0:T(8,128)}), f32[128,128]{1,0:T(8,128)}) %reduce-scatter.25.cloned.1.call-update) | async-done | bytes 65552 | tf_op jit(solution)/shard_map/reduce_scatter | solution.py:476
  1293.8 135.5 %reduce-scatter.29.cloned.1.call-done = f32[32,128]{1,0:T(8,128)} async-done(((f32[1024,128]{1,0:T(8,128)}), f32[32,128]{1,0:T(8,128)}) %reduce-scatter.29.cloned.1.call-update) | async-done | bytes 16400 | tf_op jit(solution)/shard_map/reduce_scatter | solution.py:492
  1429.3 133.4 %reduce-scatter.37.cloned.1.call-done = f32[32,256]{1,0:T(8,128)} async-done(((f32[1024,256]{1,0:T(8,128)}), f32[32,256]{1,0:T(8,128)}) %reduce-scatter.37.cloned.1.call-update) | async-done | bytes 32784 | tf_op jit(solution)/shard_map/reduce_scatter | solution.py:493
  1562.7 65.3 %reduce-scatter.41.cloned.1.call-done = f32[128,384]{1,0:T(8,128)} async-done(((f32[1024,384]{1,0:T(8,128)}), f32[128,384]{1,0:T(8,128)}) %reduce-scatter.41.cloned.1.call-update) | async-done | bytes 196624 | tf_op jit(solution)/shard_map/reduce_scatter | solution.py:481
  1628.1 67.8 %reduce-scatter.35.cloned.1.call-done = f32[128,384]{1,0:T(8,128)} async-done(((f32[1024,384]{1,0:T(8,128)}), f32[128,384]{1,0:T(8,128)}) %reduce-scatter.35.cloned.1.call-update) | async-done | bytes 196624 | tf_op jit(solution)/shard_map/reduce_scatter | solution.py:479
  1695.9 68.1 %reduce-scatter.33.cloned.1.call-done = f32[128,384]{1,0:T(8,128)} async-done(((f32[1024,384]{1,0:T(8,128)}), f32[128,384]{1,0:T(8,128)}) %reduce-scatter.33.cloned.1.call-update) | async-done | bytes 196624 | tf_op jit(solution)/shard_map/reduce_scatter | solution.py:478
  (642 shorter events, 200.7 us)
Async XLA Ops:
  8.0 55.9 %copy-start = (f32[24]{0:T(128)S(1)}, f32[24]{0:T(128)}, u32[]{:S(2)}) copy-start(f32[24]{0:T(128)} %param.41) | copy-start | bytes 292
  8.0 188.3 %slice-start = ((f32[4,1792]{1,0:T(4,128)}), f32[4,256]{1,0:T(4,128)S(1)}, s32[]{:S(2)}) async-start(f32[4,1792]{1,0:T(4,128)} %param.37), calls=%async_computation.39 | async-start | bytes 8192 | tf_op jit(solution)/shard_map/slice | solution.py:231
  8.1 122.4 %copy-start.94 = (bf16[128,128]{1,0:T(8,128)(2,1)S(1)}, bf16[128,128]{1,0:T(8,128)(2,1)}, u32[]{:S(2)}) copy-start(bf16[128,128]{1,0:T(8,128)(2,1)} %param.30) | copy-start | bytes 98308
  8.1 155.4 %copy-start.95 = (bf16[128,128]{1,0:T(8,128)(2,1)S(1)}, bf16[128,128]{1,0:T(8,128)(2,1)}, u32[]{:S(2)}) copy-start(bf16[128,128]{1,0:T(8,128)(2,1)} %param.31) | copy-start | bytes 98308
  8.1 188.3 %copy-start.118 = (f32[24]{0:T(128)S(1)}, f32[24]{0:T(128)}, u32[]{:S(2)}) copy-start(f32[24]{0:T(128)} %param.39) | copy-start | bytes 292
  8.1 189.2 %copy-start.81 = (bf16[128,256]{1,0:T(8,128)(2,1)S(1)}, bf16[128,256]{1,0:T(8,128)(2,1)}, u32[]{:S(2)}) copy-start(bf16[128,256]{1,0:T(8,128)(2,1)} %param.34) | copy-start | bytes 196612
  8.1 321.1 %all-gather.10.cloned.1.call-start = ((), (), s32[]{:S(2)}) async-start(), calls=%async_computation.16 | async-start | bytes 1310720 | tf_op jit(solution)/shard_map/all_gather | solution.py:137
  8.1 220.9 %copy-start.76 = (bf16[128,384]{1,0:T(8,128)(2,1)S(1)}, bf16[128,384]{1,0:T(8,128)(2,1)}, u32[]{:S(2)}) copy-start(bf16[128,384]{1,0:T(8,128)(2,1)} %param.33) | copy-start | bytes 294916
  9.9 24.2 %copy-start.110 = (f32[128]{0:T(128)}, f32[128]{0:T(128)S(1)}, u32[]{:S(2)}) copy-start(f32[128]{0:T(128)S(1)} %fusion.183) | copy-start | bytes 1540
  32.3 229.1 %copy-start.79 = (f32[8,1,128]{2,1,0:T(1,128)}, f32[8,1,128]{2,1,0:T(1,128)S(1)}, u32[]{:S(2)}) copy-start(f32[8,1,128]{2,1,0:T(1,128)S(1)} %convert_element_type.150) | copy-start | bytes 12292
  34.0 227.3 %copy-start.77 = (bf16[128,384]{1,0:T(8,128)(2,1)S(1)}, bf16[128,384]{1,0:T(8,128)(2,1)}, u32[]{:S(2)}) copy-start(bf16[128,384]{1,0:T(8,128)(2,1)} %param.32) | copy-start | bytes 294916
  34.1 405.9 %reduce-scatter.17.cloned.1.call-start = ((), (), s32[]{:S(2)}) async-start(), calls=%async_computation.17 | async-start | bytes 1310720 | tf_op jit(solution)/shard_map/reduce_scatter | solution.py:148
  36.5 258.6 %copy-start.108 = (f32[32]{0:T(128)}, f32[32]{0:T(128)S(1)}, u32[]{:S(2)}) copy-start(f32[32]{0:T(128)S(1)} %multiply_exponential_fusion) | copy-start | bytes 388
  62.6 273.2 %copy-start.67 = (bf16[1024,6]{0,1:T(8,128)(2,1)}, bf16[1024,6]{0,1:T(8,128)(2,1)S(1)}, u32[]{:S(2)}) copy-start(bf16[1024,6]{0,1:T(8,128)(2,1)S(1)} %all_gather.72) | copy-start | bytes 36868
  130.4 164.6 %copy-start.78 = (bf16[128,384]{1,0:T(8,128)(2,1)S(1)}, bf16[128,384]{1,0:T(8,128)(2,1)}, u32[]{:S(2)}) copy-start(bf16[128,384]{1,0:T(8,128)(2,1)} %param.36) | copy-start | bytes 294916
  196.3 136.1 %copy-start.86 = (f32[640]{0:T(1024)}, f32[640]{0:T(1024)S(1)}, u32[]{:S(2)}) copy-start(f32[640]{0:T(1024)S(1)} %get-tuple-element.1502) | copy-start | bytes 7684
  196.3 136.1 %copy-start.88 = (f32[640]{0:T(1024)}, f32[640]{0:T(1024)S(1)}, u32[]{:S(2)}) copy-start(f32[640]{0:T(1024)S(1)} %get-tuple-element.1503) | copy-start | bytes 7684
  196.4 136.1 %copy-start.90 = (f32[640]{0:T(1024)}, f32[640]{0:T(1024)S(1)}, u32[]{:S(2)}) copy-start(f32[640]{0:T(1024)S(1)} %get-tuple-element.1504) | copy-start | bytes 7684
  196.4 136.1 %copy-start.92 = (f32[640]{0:T(1024)}, f32[640]{0:T(1024)S(1)}, u32[]{:S(2)}) copy-start(f32[640]{0:T(1024)S(1)} %get-tuple-element.1505) | copy-start | bytes 7684
  197.3 211.7 %copy-start.49 = (f32[512,32]{0,1:T(8,128)}, f32[512,32]{0,1:T(8,128)S(1)}, u32[]{:S(2)}) copy-start(f32[512,32]{0,1:T(8,128)S(1)} %get-tuple-element.1676) | copy-start | bytes 196612
  197.3 211.7 %copy-start.51 = (f32[512,32]{0,1:T(8,128)}, f32[512,32]{0,1:T(8,128)S(1)}, u32[]{:S(2)}) copy-start(f32[512,32]{0,1:T(8,128)S(1)} %get-tuple-element.1677) | copy-start | bytes 196612
  229.1 102.0 %copy-start.15 = (bf16[1024,256]{1,0:T(8,128)(2,1)}, bf16[1024,256]{1,0:T(8,128)(2,1)S(1)}, u32[]{:S(2)}) copy-start(bf16[1024,256]{1,0:T(8,128)(2,1)S(1)} %all_gather.74) | copy-start | bytes 1572868
  261.3 69.8 %copy-start.10 = (bf16[1024,384]{1,0:T(8,128)(2,1)}, bf16[1024,384]{1,0:T(8,128)(2,1)S(1)}, u32[]{:S(2)}) copy-start(bf16[1024,384]{1,0:T(8,128)(2,1)S(1)} %all_gather.73) | copy-start | bytes 2359300
  415.6 24.4 %copy-start.5 = (bf16[128,1024]{1,0:T(8,128)(2,1)S(1)}, bf16[128,1024]{1,0:T(8,128)(2,1)}, u32[]{:S(2)}) copy-start(bf16[128,1024]{1,0:T(8,128)(2,1)} %param.25) | copy-start | bytes 786436
  417.4 40.5 %all-gather.14.cloned.1.call-start = ((), (), s32[]{:S(2)}) async-start(), calls=%async_computation.19 | async-start | bytes 1179648 | tf_op jit(solution)/shard_map/all_gather | solution.py:218
  418.0 57.2 %all-gather.12.cloned.1.call-start = ((), (), s32[]{:S(2)}) async-start(), calls=%async_computation.18 | async-start | bytes 1310720 | tf_op jit(solution)/shard_map/all_gather | solution.py:137
  441.1 169.1 %copy-start.106 = (f32[128]{0:T(128)}, f32[128]{0:T(128)S(1)}, u32[]{:S(2)}) copy-start(f32[128]{0:T(128)S(1)} %fusion.184) | copy-start | bytes 1540
  442.9 74.8 %all-gather.16.cloned.1.call-start = ((), (), s32[]{:S(2)}) async-start(), calls=%async_computation.20 | async-start | bytes 1179648 | tf_op jit(solution)/shard_map/all_gather | solution.py:219
  443.5 91.0 %all-gather.20.cloned.1.call-start = ((), (), s32[]{:S(2)}) async-start(), calls=%async_computation.23 | async-start | bytes 1310720 | tf_op jit(solution)/shard_map/all_gather | solution.py:137
  444.2 133.1 %all-gather.18.cloned.1.call-start = ((), (), s32[]{:S(2)}) async-start(), calls=%async_computation.21 | async-start | bytes 1179648 | tf_op jit(solution)/shard_map/all_gather | solution.py:220
  445.0 163.4 %reduce-scatter.21.cloned.1.call-start = ((), (), s32[]{:S(2)}) async-start(), calls=%async_computation.24 | async-start | bytes 1310720 | tf_op jit(solution)/shard_map/reduce_scatter | solution.py:148
  583.1 25.4 %copy-start.13 = (bf16[128,1024]{1,0:T(8,128)(2,1)S(1)}, bf16[128,1024]{1,0:T(8,128)(2,1)}, u32[]{:S(2)}) copy-start(bf16[128,1024]{1,0:T(8,128)(2,1)} %reduce-scatter.17.cloned.1.call-done) | copy-start | bytes 786436
  584.8 25.4 %copy-start.24 = (bf16[128,1024]{1,0:T(8,128)(2,1)S(1)}, bf16[128,1024]{1,0:T(8,128)(2,1)}, u32[]{:S(2)}) copy-start(bf16[128,1024]{1,0:T(8,128)(2,1)} %param.26) | copy-start | bytes 786436
  584.8 27.4 %copy-start.82 = (f32[512,6]{0,1:T(8,128)S(1)}, f32[512,6]{0,1:T(8,128)}, u32[]{:S(2)}) copy-start(f32[512,6]{0,1:T(8,128)} %get-tuple-element.1674) | copy-start | bytes 36868
  584.8 44.2 %all-gather.22.cloned.1.call-start = ((), (), s32[]{:S(2)}) async-start(), calls=%async_computation.25 | async-start | bytes 1310720 | tf_op jit(solution)/shard_map/all_gather | solution.py:137
  612.1 196.7 %reduce-scatter.47.cloned.1.call-start = ((), (), s32[]{:S(2)}) async-start(), calls=%async_computation.38 | async-start | bytes 2359296 | tf_op jit(solution)/shard_map/reduce_scatter | solution.py:486
  616.6 194.1 %reduce-scatter.23.cloned.1.call-start = ((), (), s32[]{:S(2)}) async-start(), calls=%async_computation.26 | async-start | bytes 1310720 | tf_op jit(solution)/shard_map/reduce_scatter | solution.py:148
  749.8 5.5 copy-start.4
  761.7 12.1 copy-start.44
  761.8 5.8 copy-start.87
  761.8 5.8 copy-start.89
  761.8 5.8 copy-start.91
  761.8 5.8 copy-start.93
  768.5 6.2 copy-start.33
  769.8 5.5 copy-start.19
  779.8 75.1 %reduce-scatter.19.cloned.1.call-start = ((), (), s32[]{:S(2)}) async-start(), calls=%async_computation.22 | async-start | bytes 1310720 | tf_op jit(solution)/shard_map/reduce_scatter | solution.py:148
  781.7 107.9 %reduce-scatter.39.cloned.1.call-start = ((), (), s32[]{:S(2)}) async-start(), calls=%async_computation.34 | async-start | bytes 36864 | tf_op jit(solution)/shard_map/reduce_scatter | solution.py:480
  782.6 177.9 %reduce-scatter.43.cloned.1.call-start = ((), (), s32[]{:S(2)}) async-start(), calls=%async_computation.36 | async-start | bytes 2359296 | tf_op jit(solution)/shard_map/reduce_scatter | solution.py:484
  785.1 246.3 %reduce-scatter.45.cloned.1.call-start = ((), (), s32[]{:S(2)}) async-start(), calls=%async_computation.37 | async-start | bytes 2359296 | tf_op jit(solution)/shard_map/reduce_scatter | solution.py:485
  788.2 378.5 %reduce-scatter.27.cloned.1.call-start = ((), (), s32[]{:S(2)}) async-start(), calls=%async_computation.28 | async-start | bytes 540672 | tf_op jit(solution)/shard_map/reduce_scatter | solution.py:491
  792.6 436.2 %reduce-scatter.31.cloned.1.call-start = ((), (), s32[]{:S(2)}) async-start(), calls=%async_computation.30 | async-start | bytes 589824 | tf_op jit(solution)/shard_map/reduce_scatter | solution.py:477
  794.0 499.9 %reduce-scatter.25.cloned.1.call-start = ((), (), s32[]{:S(2)}) async-start(), calls=%async_computation.27 | async-start | bytes 589824 | tf_op jit(solution)/shard_map/reduce_scatter | solution.py:476
  795.3 634.0 %reduce-scatter.29.cloned.1.call-start = ((), (), s32[]{:S(2)}) async-start(), calls=%async_computation.29 | async-start | bytes 540672 | tf_op jit(solution)/shard_map/reduce_scatter | solution.py:492
  799.5 763.2 %reduce-scatter.37.cloned.1.call-start = ((), (), s32[]{:S(2)}) async-start(), calls=%async_computation.33 | async-start | bytes 1081344 | tf_op jit(solution)/shard_map/reduce_scatter | solution.py:493
  801.1 827.0 %reduce-scatter.41.cloned.1.call-start = ((), (), s32[]{:S(2)}) async-start(), calls=%async_computation.35 | async-start | bytes 1769472 | tf_op jit(solution)/shard_map/reduce_scatter | solution.py:481
  803.2 892.7 %reduce-scatter.35.cloned.1.call-start = ((), (), s32[]{:S(2)}) async-start(), calls=%async_computation.32 | async-start | bytes 1769472 | tf_op jit(solution)/shard_map/reduce_scatter | solution.py:479
  805.2 958.8 %reduce-scatter.33.cloned.1.call-start = ((), (), s32[]{:S(2)}) async-start(), calls=%async_computation.31 | async-start | bytes 1769472 | tf_op jit(solution)/shard_map/reduce_scatter | solution.py:478
  807.2 47.7 %copy-start.115 = (f32[128]{0:T(128)S(1)}, f32[128]{0:T(128)}, u32[]{:S(2)}) copy-start(f32[128]{0:T(128)} %copy-done.114) | copy-start | bytes 1540
  807.3 47.7 %copy-start.14 = (bf16[128,1024]{1,0:T(8,128)(2,1)S(1)}, bf16[128,1024]{1,0:T(8,128)(2,1)}, u32[]{:S(2)}) copy-start(bf16[128,1024]{1,0:T(8,128)(2,1)} %reduce-scatter.17.cloned.1.call-done) | copy-start | bytes 786436
  807.3 47.7 %copy-start.25 = (bf16[128,1024]{1,0:T(8,128)(2,1)S(1)}, bf16[128,1024]{1,0:T(8,128)(2,1)}, u32[]{:S(2)}) copy-start(bf16[128,1024]{1,0:T(8,128)(2,1)} %param.26) | copy-start | bytes 786436
  807.3 47.7 %copy-start.29 = (bf16[128,1024]{1,0:T(8,128)(2,1)S(1)}, bf16[128,1024]{1,0:T(8,128)(2,1)}, u32[]{:S(2)}) copy-start(bf16[128,1024]{1,0:T(8,128)(2,1)} %reduce-scatter.21.cloned.1.call-done) | copy-start | bytes 786436
  807.3 47.7 %copy-start.107 = (f32[128]{0:T(128)S(1)}, f32[128]{0:T(128)}, u32[]{:S(2)}) copy-start(f32[128]{0:T(128)} %copy-done.106) | copy-start | bytes 1540
  807.3 47.7 %copy-start.113 = (f32[128]{0:T(128)S(1)}, f32[128]{0:T(128)}, u32[]{:S(2)}) copy-start(f32[128]{0:T(128)} %copy-done.112) | copy-start | bytes 1540
  808.8 955.2 %copy-start.1 = (f32[24]{0:T(128)S(1)}, f32[24]{0:T(128)}, u32[]{:S(2)}) copy-start(f32[24]{0:T(128)} %param.41) | copy-start | bytes 292
  (82 other events, 147.9 us)
Sparse Core Ops, SparseCore 0:
  34.2 13.9 all-gather.9
  417.5 22.4 reduce-scatter.16
  585.0 23.4 reduce-scatter.20
  612.2 16.7 all-gather.21
Sparse Core Ops, SparseCore 1:
  420.0 37.9 all-gather.13
  460.0 15.1 all-gather.11
  477.4 40.4 all-gather.15
  519.4 15.1 all-gather.19
  536.9 40.4 all-gather.17
  616.9 68.2 reduce-scatter.46
  779.9 24.8 reduce-scatter.22
  807.3 25.0 reduce-scatter.18
  836.0 53.5 reduce-scatter.38
  893.7 66.8 reduce-scatter.42
  964.5 66.8 reduce-scatter.44
  1034.2 132.5 reduce-scatter.26
  1170.9 57.9 reduce-scatter.30
  1232.8 61.0 reduce-scatter.24
  1296.8 132.5 reduce-scatter.28
  1432.2 130.5 reduce-scatter.36
  1567.1 60.9 reduce-scatter.40
  1632.1 63.8 reduce-scatter.34
  1700.2 63.8 reduce-scatter.32
where the time goes:
time: 1780 us; the launch traced here: 1770 us
  waiting for transfers between devices  1080 us (61%)
  blocking collectives  370 us (21%)
  local copies, waits for them, and re-layouts  133 us (7%)
  matrix products  110 us (6%)
  other arithmetic  62.6 us (4%)
    reduce_scatter x1, waiting for transfers between devices, local(): lax.psum_scatter(grad_value, ('dp', 'tensor'), scatter_dimension=0, tiled...  135 us
    reduce_scatter x1, waiting for transfers between devices, local(): lax.psum_scatter(grad_key, ('dp', 'tensor'), scatter_dimension=0, tiled=T...  135 us
    reduce_scatter x1, waiting for transfers between devices, local(): lax.psum_scatter(grad_state, ('dp', 'tensor'), scatter_dimension=0, tiled...  133 us
    reduce_scatter x1, waiting for transfers between devices, local(): lax.psum_scatter(grad_gate, 'dp', scatter_dimension=0, tiled=True)  71 us
    reduce_scatter x1, waiting for transfers between devices, local(): lax.psum_scatter(grad_up, 'dp', scatter_dimension=0, tiled=True)  70.9 us
    reduce_scatter x1, waiting for transfers between devices, local(): lax.psum_scatter(grad_gate_ssm, 'dp', scatter_dimension=0, tiled=True)  68.1 us
    reduce_scatter x1, waiting for transfers between devices, local(): lax.psum_scatter(grad_input_ssm, 'dp', scatter_dimension=0, tiled=True)  67.8 us
    reduce_scatter x1, waiting for transfers between devices, local(): lax.psum_scatter(grad_mamba_out, 'dp', scatter_dimension=0, tiled=True)  65.3 us
  transfers between devices with their start and end apart: 23, of which 19 were waited for; matrix products, arithmetic and copies ran while one was open for 11% of the time, Pallas kernels for 0%

commit v1 on v0

--- a/solution.py
+++ b/solution.py
@@ -131,6 +131,58 @@
     decay_rates = (-jnp.exp(decay_local))[None]
     scanned = ssd_scan(series, step_sizes, decay_rates, input_map, output_map, skip_local[None])
     return scanned.reshape(length, channel_count) * jax.nn.silu(gate_proj)
+
+
+def partner_pairs(count):
+    return [(index, index ^ 1) for index in range(count)]
+
+
+def shift_pairs(count, steps):
+    return [(index, (index + 2 * steps) % count) for index in range(count)]
+
+
+def gather_dp(piece):
+    count = lax.axis_size("dp")
+    if count > 8 or count % 2:
+        return lax.all_gather(piece, "dp", axis=0, tiled=True)
+    mine = lax.axis_index("dp")
+    rows = piece.shape[0]
+    result = jnp.zeros((count * rows,) + piece.shape[1:], piece.dtype)
+
+    def put(result, block, source):
+        return lax.dynamic_update_slice_in_dim(result, block, source * rows, 0)
+
+    far = [lax.ppermute(piece, "dp", shift_pairs(count, steps)) for steps in range(1, count // 2)]
+    near = lax.ppermute(piece, "dp", partner_pairs(count))
+    crossed = [lax.ppermute(block, "dp", partner_pairs(count)) for block in far]
+    other = mine + 1 - 2 * (mine % 2)
+    result = put(result, piece, mine)
+    result = put(result, near, other)
+    for steps in range(1, count // 2):
+        result = put(result, far[steps - 1], (mine - 2 * steps + count) % count)
+        result = put(result, crossed[steps - 1], (other - 2 * steps + count) % count)
+    return result
+
+
+def reduce_dp(partial):
+    count = lax.axis_size("dp")
+    rows = partial.shape[0] // count
+    if count > 8 or count % 2:
+        return lax.psum_scatter(partial, "dp", scatter_dimension=0, tiled=True).astype(jnp.float32)
+    mine = lax.axis_index("dp")
+    side = mine % 2
+    place = mine // 2
+    half_count = count // 2
+    split = partial.reshape((half_count, 2, rows) + partial.shape[1:])
+    sent = lax.dynamic_index_in_dim(split, 1 - side, 1, keepdims=False)
+    kept = lax.dynamic_index_in_dim(split, side, 1, keepdims=False)
+    arrived = lax.ppermute(sent, "dp", partner_pairs(count))
+    paired = (kept.astype(jnp.float32) + arrived.astype(jnp.float32)).astype(jnp.bfloat16)
+    total = lax.dynamic_index_in_dim(paired, place, 0, keepdims=False).astype(jnp.float32)
+    for steps in range(1, half_count):
+        block = lax.dynamic_index_in_dim(paired, (place + steps) % half_count, 0, keepdims=False)
+        total = total + lax.ppermute(block, "dp", shift_pairs(count, steps)).astype(jnp.float32)
+    return total
 
 
 def full_rows(local_piece):
@@ -189,41 +241,48 @@
 ):
     tensor_index = lax.axis_index("tensor")
     local_rows = inputs.shape[0]
-    mix_gathered = (
-        lax.all_gather(mix_gain, "dp", axis=0, tiled=True),
-        lax.all_gather(query_weight, "dp", axis=0, tiled=True),
-        lax.all_gather(key_weight, "dp", axis=0, tiled=True),
-        lax.all_gather(value_weight, "dp", axis=0, tiled=True),
-        lax.all_gather(attention_out, "dp", axis=0, tiled=True),
-        lax.all_gather(mamba_gate, "dp", axis=0, tiled=True),
-        lax.all_gather(mamba_input, "dp", axis=0, tiled=True),
-        lax.all_gather(state_weight, "dp", axis=0, tiled=True),
-        lax.all_gather(step_weight, "dp", axis=0, tiled=True),
-        lax.all_gather(mamba_out, "dp", axis=0, tiled=True),
-    )
-    (
-        mix_gain_all,
-        query_all,
-        key_all,
-        value_all,
-        attention_all,
-        gate_ssm_all,
-        input_ssm_all,
-        state_all,
-        step_all,
-        mamba_out_all,
-    ) = mix_gathered
-    mlp_gathered = (
-        lax.all_gather(mlp_gain, "dp", axis=0, tiled=True),
-        lax.all_gather(gate_weight, "dp", axis=0, tiled=True),
-        lax.all_gather(up_weight, "dp", axis=0, tiled=True),
-        lax.all_gather(down_weight, "dp", axis=0, tiled=True),
-    )
-    mlp_gain_all, gate_all, up_all, down_all = mlp_gathered
-    query_heads = query_all.shape[1] // HEAD_DIM
+    query_heads = query_weight.shape[1] // HEAD_DIM
     key_head = tensor_index * query_heads // (HEADS // KV_HEADS)
-    scan_width = input_ssm_all.shape[1]
-    scan_heads = step_all.shape[1]
+    unit_count = gate_weight.shape[1]
+    scan_width = mamba_input.shape[1]
+    scan_heads = step_weight.shape[1]
+    weight_rows = query_weight.shape[0]
+    narrow = jnp.concatenate(
+        [
+            step_weight,
+            mix_gain[:, None],
+            mlp_gain[:, None],
+            jnp.zeros((weight_rows, 128 - scan_heads - 2), jnp.bfloat16),
+        ],
+        1,
+    )
+    key_own = lax.dynamic_slice_in_dim(key_weight, key_head * HEAD_DIM, HEAD_DIM, 1)
+    value_own = lax.dynamic_slice_in_dim(value_weight, key_head * HEAD_DIM, HEAD_DIM, 1)
+    mix_pack = gather_dp(
+        jnp.concatenate(
+            [mamba_gate, mamba_input, state_weight, query_weight, key_own, value_own, narrow], 1
+        )
+    )
+    out_pack = gather_dp(jnp.concatenate([attention_out, mamba_out], 1))
+    mlp_pack = gather_dp(jnp.concatenate([gate_weight, up_weight, down_weight], 1))
+
+    def take(pack, widths):
+        pieces, start = [], 0
+        for width in widths:
+            pieces.append(pack[:, start : start + width])
+            start += width
+        return pieces
+
+    query_width = query_weight.shape[1]
+    gate_ssm_all, input_ssm_all, state_all, query_all, key_slice, value_slice, narrow_all = take(
+        mix_pack,
+        (scan_width, scan_width, state_weight.shape[1], query_width, HEAD_DIM, HEAD_DIM, 128),
+    )
+    step_all = narrow_all[:, :scan_heads]
+    mix_gain_all = narrow_all[:, scan_heads]
+    mlp_gain_all = narrow_all[:, scan_heads + 1]
+    attention_all, mamba_out_all = take(out_pack, (query_width, scan_width))
+    gate_all, up_all, down_all = take(mlp_pack, (unit_count,) * 3)
     full_width = SSM_HEADS * SSM_HEAD_DIM
     kernel_local = jnp.concatenate(
         [
@@ -248,8 +307,6 @@
     mixer_rows = full_rows(normed_local)
     length = mixer_rows.shape[0]
     cosine_table, sine_table = rotary_tables(length)
-    key_slice = lax.dynamic_slice_in_dim(key_all, key_head * HEAD_DIM, HEAD_DIM, 1)
-    value_slice = lax.dynamic_slice_in_dim(value_all, key_head * HEAD_DIM, HEAD_DIM, 1)
     query_proj = jnp.dot(mixer_rows, query_all, preferred_element_type=jnp.float32).reshape(
         length, query_heads, HEAD_DIM
     )
@@ -306,53 +363,27 @@
     units_low = (silu_gate * up_pre).astype(jnp.bfloat16)
     mlp_sum = summed_rows(((units_low, down_all),), local_rows)
     output = (hidden + mlp_sum).astype(jnp.bfloat16)
-    gate_back, up_back, down_back = (
-        lax.all_gather(gate_weight, "dp", axis=0, tiled=True),
-        lax.all_gather(up_weight, "dp", axis=0, tiled=True),
-        lax.all_gather(down_weight, "dp", axis=0, tiled=True),
-    )
-    (
-        query_back,
-        key_back,
-        value_back,
-        attention_back,
-        gate_ssm_back,
-        input_ssm_back,
-        state_back,
-        step_back,
-        mamba_out_back,
-    ) = (
-        lax.all_gather(query_weight, "dp", axis=0, tiled=True),
-        lax.all_gather(key_weight, "dp", axis=0, tiled=True),
-        lax.all_gather(value_weight, "dp", axis=0, tiled=True),
-        lax.all_gather(attention_out, "dp", axis=0, tiled=True),
-        lax.all_gather(mamba_gate, "dp", axis=0, tiled=True),
-        lax.all_gather(mamba_input, "dp", axis=0, tiled=True),
-        lax.all_gather(state_weight, "dp", axis=0, tiled=True),
-        lax.all_gather(step_weight, "dp", axis=0, tiled=True),
-        lax.all_gather(mamba_out, "dp", axis=0, tiled=True),
-    )
     cotangent_rows = full_rows(cotangent)
     grad_down = weight_grad(cotangent_rows, units_low)
-    unit_grad = jnp.dot(cotangent_rows, down_back, preferred_element_type=jnp.float32)
+    unit_grad = jnp.dot(cotangent_rows, down_all, preferred_element_type=jnp.float32)
     gate_grad = (
         unit_grad * up_pre * (sigmoid_gate * (1.0 + gate_pre * (1.0 - sigmoid_gate)))
     ).astype(jnp.bfloat16)
     up_grad = (unit_grad * silu_gate).astype(jnp.bfloat16)
     grad_gate = weight_grad(mlp_rows, gate_grad)
     grad_up = weight_grad(mlp_rows, up_grad)
-    mlp_input_grad = summed_rows(((gate_grad, gate_back), (up_grad, up_back)), local_rows)
+    mlp_input_grad = summed_rows(((gate_grad, gate_all), (up_grad, up_all)), local_rows)
     hidden_norm_grad, grad_mlp_gain = second_norm_back(mlp_input_grad)
     hidden_grad = cotangent.astype(jnp.float32) + hidden_norm_grad
     mixer_grad_rows = full_rows(hidden_grad.astype(jnp.bfloat16))
     grad_attention = weight_grad(mixer_grad_rows, attended_low)
     grad_mamba_out = weight_grad(mixer_grad_rows, gated_low)
     attended_grad = (
-        jnp.dot(mixer_grad_rows, attention_back, preferred_element_type=jnp.float32)
+        jnp.dot(mixer_grad_rows, attention_all, preferred_element_type=jnp.float32)
         .astype(jnp.bfloat16)
         .reshape(length, query_heads, HEAD_DIM)
     )
-    gated_grad = jnp.dot(mixer_grad_rows, mamba_out_back, preferred_element_type=jnp.float32)
+    gated_grad = jnp.dot(mixer_grad_rows, mamba_out_all, preferred_element_type=jnp.float32)
 
     def attend_back(carried, block_index):
         key_total, value_total = carried
@@ -405,24 +436,22 @@
     input_proj_low = input_proj_grad.astype(jnp.bfloat16)
     state_proj_low = state_proj_grad.astype(jnp.bfloat16)
     step_proj_low = step_proj_grad.astype(jnp.bfloat16)
-    key_slice_back = lax.dynamic_slice_in_dim(key_back, key_head * HEAD_DIM, HEAD_DIM, 1)
-    value_slice_back = lax.dynamic_slice_in_dim(value_back, key_head * HEAD_DIM, HEAD_DIM, 1)
     mixer_input_grad = summed_rows(
         (
-            (query_low, query_back),
-            (key_low, key_slice_back),
-            (value_grad_low, value_slice_back),
-            (gate_proj_low, gate_ssm_back),
-            (input_proj_low, input_ssm_back),
-            (state_proj_low, state_back),
-            (step_proj_low, step_back),
+            (query_low, query_all),
+            (key_low, key_slice),
+            (value_grad_low, value_slice),
+            (gate_proj_low, gate_ssm_all),
+            (input_proj_low, input_ssm_all),
+            (state_proj_low, state_all),
+            (step_proj_low, step_all),
         ),
         local_rows,
     )
     input_norm_grad, grad_mix_gain = first_norm_back(mixer_input_grad)
     grad_inputs = (hidden_grad + input_norm_grad).astype(jnp.bfloat16)
     grad_query = weight_grad(mixer_rows, query_low)
-    key_width = key_all.shape[1]
+    key_width = key_weight.shape[1]
     grad_key = lax.dynamic_update_slice_in_dim(
         jnp.zeros((D, key_width), jnp.float32),
         weight_grad(mixer_rows, key_low),
@@ -472,29 +501,64 @@
     skip_full = lax.dynamic_update_slice_in_dim(
         jnp.zeros((SSM_HEADS,), jnp.float32), skip_grad, tensor_index * scan_heads, 0
     )
-    mix_sums = (
-        lax.psum_scatter(grad_query, "dp", scatter_dimension=0, tiled=True),
-        lax.psum_scatter(grad_attention, "dp", scatter_dimension=0, tiled=True),
-        lax.psum_scatter(grad_gate_ssm, "dp", scatter_dimension=0, tiled=True),
-        lax.psum_scatter(grad_input_ssm, "dp", scatter_dimension=0, tiled=True),
-        lax.psum_scatter(grad_step, "dp", scatter_dimension=0, tiled=True),
-        lax.psum_scatter(grad_mamba_out, "dp", scatter_dimension=0, tiled=True),
-    )
-    mlp_sums = (
-        lax.psum_scatter(grad_gate, "dp", scatter_dimension=0, tiled=True),
-        lax.psum_scatter(grad_up, "dp", scatter_dimension=0, tiled=True),
-        lax.psum_scatter(grad_down, "dp", scatter_dimension=0, tiled=True),
-    )
-    shared_sums = (
-        lax.psum_scatter(grad_mix_gain, ("dp", "tensor"), scatter_dimension=0, tiled=True),
-        lax.psum_scatter(grad_mlp_gain, ("dp", "tensor"), scatter_dimension=0, tiled=True),
-        lax.psum_scatter(grad_key, ("dp", "tensor"), scatter_dimension=0, tiled=True),
-        lax.psum_scatter(grad_value, ("dp", "tensor"), scatter_dimension=0, tiled=True),
-        lax.psum_scatter(grad_state, ("dp", "tensor"), scatter_dimension=0, tiled=True),
-    )
-    small_sums = lax.psum(
-        (kernel_full, bias_full, decay_full, step_bias_full, skip_full), ("dp", "tensor")
-    )
+    count = lax.axis_size("dp")
+    tensor_size = lax.axis_size("tensor")
+    low = jnp.bfloat16
+    shared = jnp.concatenate(
+        [
+            grad_key,
+            grad_value,
+            grad_state,
+            grad_mix_gain[:, None],
+            grad_mlp_gain[:, None],
+            jnp.zeros((D, 126), jnp.float32),
+        ],
+        1,
+    ).astype(low)
+    shared_width = shared.shape[1]
+    shared = lax.psum_scatter(
+        shared.reshape(count, tensor_size, D // count // tensor_size, shared_width),
+        "tensor",
+        scatter_dimension=1,
+        tiled=True,
+    )
+    shared = shared.reshape(D, shared_width // tensor_size)
+    mlp_sum_pack = reduce_dp(jnp.concatenate([grad_gate, grad_up, grad_down], 1).astype(low))
+    out_sum_pack = reduce_dp(jnp.concatenate([grad_attention, grad_mamba_out], 1).astype(low))
+    mix_sum_pack = reduce_dp(
+        jnp.concatenate(
+            [
+                grad_gate_ssm.astype(low),
+                grad_input_ssm.astype(low),
+                grad_query.astype(low),
+                shared,
+                grad_step.astype(low),
+            ],
+            1,
+        )
+    )
+    mlp_sums = take(mlp_sum_pack, (unit_count,) * 3)
+    attention_sum, mamba_out_sum = take(out_sum_pack, (query_width, scan_width))
+    gate_ssm_sum, input_ssm_sum, query_sum, shared_sum, step_sum = take(
+        mix_sum_pack,
+        (scan_width, scan_width, query_width, shared_width // tensor_size, scan_heads),
+    )
+    shared_sum = shared_sum.reshape(D // count // tensor_size, shared_width)
+    key_sum, value_sum, state_sum = take(
+        shared_sum, (key_width, key_width, state_weight.shape[1])
+    )
+    mix_gain_sum = shared_sum[:, shared_width - 128]
+    mlp_gain_sum = shared_sum[:, shared_width - 127]
+    mix_sums = (query_sum, attention_sum, gate_ssm_sum, input_ssm_sum, step_sum, mamba_out_sum)
+    shared_sums = (mix_gain_sum, mlp_gain_sum, key_sum, value_sum, state_sum)
+    small_parts = (kernel_full, bias_full, decay_full, step_bias_full, skip_full)
+    small_flat = lax.psum(
+        jnp.concatenate([part.reshape(-1) for part in small_parts]), ("dp", "tensor")
+    )
+    small_sums, start = [], 0
+    for part in small_parts:
+        small_sums.append(small_flat[start : start + part.size].reshape(part.shape))
+        start += part.size
     return (
         output,
         grad_inputs,

time: 1780 us -> 721 us (0.41)
  waiting for transfers between devices: 1080 us -> 162 us
  blocking collectives: 370 us -> 63.1 us
  starting transfers between devices: 1.41 us -> 70.5 us
  local copies, waits for them, and re-layouts: 133 us -> 192 us
    reduce_scatter x12 -> x1, waiting for transfers between devices: 907 us -> 0.01 us  [local(): lax.psum_scatter(shared.reshape(count, tensor_size, D // count // tensor_...]
    all_gather x11 -> x0, blocking collectives: 328 us -> none  [the longest x1 34.1 us: local(): lax.all_gather(mamba_out, 'dp', axis=0, tiled=True)]
    ppermute x0 -> x33, waiting for transfers between devices: none -> 100 us  [the longest x9 41 us: reduce_dp(): lax.ppermute(block, 'dp', shift_pairs(count, steps)).astype(jnp.float32)]
    all_gather x3 -> x0, waiting for transfers between devices: 94.9 us -> none  [the longest x1 42.8 us: local(): lax.all_gather(down_weight, 'dp', axis=0, tiled=True)]
    ppermute x0 -> x33, starting transfers between devices: none -> 69.5 us  [the longest x9 36.6 us: gather_dp(): lax.ppermute(piece, 'dp', shift_pairs(count, steps))]
    psum x0 -> x1, blocking collectives: none -> 63.1 us  [local(): lax.psum(jnp.concatenate([part.reshape(-1) for part in small_parts]), ('d...]
    unnamed x1 -> x0, blocking collectives: 41.9 us -> none
    all_gather x4, waiting for transfers between devices: 43.1 us -> 22.4 us  [full_rows(): return lax.all_gather(local_piece, 'tensor', axis=0, tiled=True)]
  transfers between devices with their start and end apart: 23 -> 42, of which waited for: 19 -> 23; matrix products, arithmetic and copies ran while one was open for 11% -> 16% of each run, Pallas kernels for 0% -> 0%
where the time goes in v1:
time: 721 us; the launch traced here: 709 us
  local copies, waits for them, and re-layouts  192 us (27%)
  waiting for transfers between devices  162 us (22%)
  matrix products  127 us (18%)
  other arithmetic  77.9 us (11%)
  starting transfers between devices  70.5 us (10%)
  blocking collectives  63.1 us (9%)
  between operations  16 us (2%)
    psum x1, blocking collectives, local(): lax.psum(jnp.concatenate([part.reshape(-1) for part in small_parts]), ('d...  63.1 us
    dynamic_update_slice x44, local copies, waits for them, and re-layouts, ssd_scan(): lax.scan(advance, initial, (by_block(series), by_block(step_sizes), by_bl...  60.2 us
    ppermute x9, waiting for transfers between devices, reduce_dp(): lax.ppermute(block, 'dp', shift_pairs(count, steps)).astype(jnp.float32)  41 us
    reduce_scatter x4, waiting for transfers between devices, summed_rows(): lax.psum_scatter(running.astype(jnp.bfloat16), 'tensor', scatter_dimensio...  38.4 us
    ppermute x9, starting transfers between devices, gather_dp(): lax.ppermute(piece, 'dp', shift_pairs(count, steps))  36.6 us
    ppermute x9, waiting for transfers between devices, gather_dp(): crossed = [lax.ppermute(block, 'dp', partner_pairs(count)) for block in far]  33.5 us
    dot_general x12, matrix products, summed_rows(): lax.dot_general(left_side, right_side, by_columns, preferred_element_type...  22.7 us
    all_gather x4, waiting for transfers between devices, full_rows(): return lax.all_gather(local_piece, 'tensor', axis=0, tiled=True)  22.4 us
  transfers between devices with their start and end apart: 42, of which 23 were waited for; matrix products, arithmetic and copies ran while one was open for 16% of the time, Pallas kernels for 0%

profile of v1, /device:TPU:0, one launch (start us, length us, event | category | flops | bytes accessed | tf_op | source)
XLA Modules:
  0.0 708.6 jit_solution(4174782335392675902)
XLA Ops:
  11.6 3.0 collective-permute-start
  16.2 2.6 collective-permute-start.3
  30.2 14.0 %collective-permute-start.10 = (bf16[128,512]{1,0:T(8,128)(2,1)}, bf16[128,512]{1,0:T(8,128)(2,1)}, u32[]{:S(2)}, u32[]{:S(2)}) collective-permute-start(bf16[128,512]{1,0:T(8,128)(2,1)} %constant_dynamic-update-slice_fusion.7), channel_id=1, source_target_pairs={{0,16},{4,20},{8,24},{12,28},{16,0},{20,4},{24,8},{28,12},{1,17},{... | collective-permute-start | bytes 393224 | tf_op jit(solution)/shard_map/ppermute | solution.py:155
  44.5 11.0 %collective-permute-start.12 = (bf16[128,512]{1,0:T(8,128)(2,1)}, bf16[128,512]{1,0:T(8,128)(2,1)}, u32[]{:S(2)}, u32[]{:S(2)}) collective-permute-start(bf16[128,512]{1,0:T(8,128)(2,1)} %constant_dynamic-update-slice_fusion.7), channel_id=1, source_target_pairs={{0,24},{4,28},{8,0},{12,4},{16,8},{20,12},{24,16},{28,20},{1,25},{... | collective-permute-start | bytes 393224 | tf_op jit(solution)/shard_map/ppermute | solution.py:155
  58.1 6.7 collective-permute-done.2
  67.1 7.8 %collective-permute-done.4 = bf16[128,1408]{1,0:T(8,128)(2,1)S(1)} collective-permute-done((bf16[128,1408]{1,0:T(8,128)(2,1)S(1)}, bf16[128,1408]{1,0:T(8,128)(2,1)S(1)}, u32[]{:S(2)}, u32[]{:S(2)}) %collective-permute-start.4) | collective-permute-done | bytes 360480 | tf_op jit(solution)/shard_map/ppermute | solution.py:157
  77.3 5.0 collective-permute-done.6
  98.2 2.1 all-gather.5.cloned.1.call-done
  100.2 2.1 fusion.164
  105.1 2.6 fusion.129
  115.5 67.7 %while.82 = (s32[]{:T(128)}, f32[1,6,64,128]{3,2,1,0:T(8,128)S(1)}, f32[4,128,1,6,64]{1,0,4,3,2:T(4,128)}, f32[4,128,128,1,6]{2,1,4,3,0:T(8,128)}, f32[4,128,128...) while((s32[]{:T(128)}, f32[1,6,64,128]{3,2,1,0:T(8,128)S(1)}, ...), condition=%wide.region_5.6_spmd.clone.clone, body=%wide.region_3.5_spmd.clone.clone.sunk | while | flops 253036800 | bytes 4982733 | solution.py:101
  121.3 6.0 dynamic_update_slice.359
  138.2 6.0 dynamic_update_slice.359
  155.2 6.0 dynamic_update_slice.359
  172.1 6.0 dynamic_update_slice.359
  191.5 2.9 multiply_convert_fusion.3
  201.3 2.4 collective-permute-start.17
  207.9 4.5 collective-permute-done.15
  214.6 7.9 %reduce-scatter.6.cloned.1.call-done = bf16[128,1024]{1,0:T(8,128)(2,1)} async-done(((bf16[512,1024]{1,0:T(8,128)(2,1)}), bf16[128,1024]{1,0:T(8,128)(2,1)}) %reduce-scatter.6.cloned.1.call-update) | async-done | bytes 262160 | tf_op jit(solution)/shard_map/reduce_scatter | solution.py:200
  234.1 6.6 collective-permute-done.18
  242.3 5.8 collective-permute-done.20
  248.9 3.3 convolution_bitcast_fusion.9
  252.2 7.5 %all-gather.7.cloned.1.call-done = bf16[512,1024]{1,0:T(8,128)(2,1)} async-done(((bf16[128,1024]{1,0:T(8,128)(2,1)}), bf16[512,1024]{1,0:T(8,128)(2,1)}) %all-gather.7.cloned.1.call-update) | async-done | bytes 1048592 | tf_op jit(solution)/shard_map/all_gather | solution.py:189
  259.8 2.4 fusion.143
  262.2 3.1 multiply_convert_fusion.1
  265.3 2.3 fusion.141
  267.7 3.0 add_convert_fusion.1
  270.8 25.0 %reduce-scatter.10.cloned.1.call-done = bf16[128,1024]{1,0:T(8,128)(2,1)} async-done(((bf16[512,1024]{1,0:T(8,128)(2,1)}), bf16[128,1024]{1,0:T(8,128)(2,1)}) %reduce-scatter.10.cloned.1.call-update) | async-done | bytes 262160 | tf_op jit(solution)/shard_map/reduce_scatter | solution.py:200
  300.5 3.1 convolution_convert_fusion.1
  303.5 12.8 %all-gather.11.cloned.1.call-done = bf16[512,1024]{1,0:T(8,128)(2,1)} async-done(((bf16[128,1024]{1,0:T(8,128)(2,1)}), bf16[512,1024]{1,0:T(8,128)(2,1)}) %all-gather.11.cloned.1.call-update) | async-done | bytes 1048592 | tf_op jit(solution)/shard_map/all_gather | solution.py:189
  318.3 2.7 fusion.133
  326.5 2.3 copy.490
  328.8 2.3 reshape.1274
  334.3 115.3 %while.81 = (s32[]{:T(128)}, f32[1,6]{1,0:T(1,128)}, f32[1,6]{1,0:T(1,128)}, f32[1,6,64,128]{3,2,1,0:T(8,128)S(1)}, f32[4,128,1,6,64]{1,0,4,3,2:T(4,128)}, /*ind...) while((s32[]{:T(128)}, f32[1,6]{1,0:T(1,128)}, ...), condition=%wide.region_24.25_spmd.clone, body=%wide.region_12.24_spmd.clone.sunk | while | flops 505256736 | bytes 6949322 | solution.py:101
  339.9 5.9 dynamic_update_slice.348
  367.7 5.9 dynamic_update_slice.348
  396.8 5.9 dynamic_update_slice.348
  426.0 5.9 dynamic_update_slice.348
  449.7 2.3 copy.599
  455.6 4.3 multiply_reduce_fusion.3
  472.4 2.6 add_convert_fusion
  476.8 2.2 concatenate.119
  479.0 2.5 copy.526
  481.5 2.2 convolution_convert_fusion.2
  492.1 2.5 dynamic_update_slice.245
  494.6 5.5 reduce-scatter.12.cloned.1.call-done
  503.9 19.9 %collective-permute-done.29 = bf16[4,128,1536]{2,1,0:T(8,128)(2,1)} collective-permute-done((bf16[4,128,1536]{2,1,0:T(8,128)(2,1)}, bf16[4,128,1536]{2,1,0:T(8,128)(2,1)}, u32[]{:S(2)}, u32[]{:S(2)}) %collective-permute-start.29) | collective-permute-done | bytes 1572896 | tf_op jit(solution)/shard_map/ppermute | solution.py:179
  523.8 2.3 fusion.119
  528.6 2.4 collective-permute-start.31
  532.4 3.1 convolution_convert_fusion.3
  535.6 5.8 collective-permute-done.30
  541.4 15.2 %collective-permute-done.31 = bf16[128,1536]{1,0:T(8,128)(2,1)} collective-permute-done((bf16[128,1536]{1,0:T(8,128)(2,1)}, bf16[128,1536]{1,0:T(8,128)(2,1)}, u32[]{:S(2)}, u32[]{:S(2)}) %collective-permute-start.31) | collective-permute-done | bytes 393248 | tf_op jit(solution)/shard_map/ppermute | solution.py:184
  571.5 2.7 convolution_convert_fusion.6
  574.2 2.4 copy.513
  576.6 2.2 constant_dynamic-update-slice_fusion.16
  585.8 4.8 copy.518
  591.7 63.1 %psum.7 = f32[9032]{0:T(1024)S(1)} all-reduce(f32[9032]{0:T(1024)S(1)} %concatenate.116), channel_id=1, replica_groups=mesh['dp'=8,'tensor'=4] {'dp','tensor'}, use_global_device_ids=true, to_apply=%region_36.37 | all-reduce | flops 9032 | bytes 72256 | tf_op jit(solution)/shard_map/psum | solution.py:555
  657.3 2.1 collective-permute-start.26
  660.4 2.8 collective-permute-start.28
  665.6 4.0 collective-permute-done.27
  673.7 3.0 collective-permute-start.22
  679.2 2.2 fusion.178
  681.3 4.7 collective-permute-done.22
  686.0 9.6 %collective-permute-done.23 = bf16[128,1062]{0,1:T(8,128)(2,1)} collective-permute-done((bf16[128,1062]{0,1:T(8,128)(2,1)S(1)}, bf16[128,1062]{0,1:T(8,128)(2,1)}, u32[]{:S(2)}, u32[]{:S(2)}) %collective-permute-start.23) | collective-permute-done | bytes 271904 | tf_op jit(solution)/shard_map/ppermute | solution.py:184
  (710 shorter events, 311.2 us)
Async XLA Ops:
  7.2 78.5 %copy-start = (f32[24]{0:T(128)S(1)}, f32[24]{0:T(128)}, u32[]{:S(2)}) copy-start(f32[24]{0:T(128)} %param.41) | copy-start | bytes 292
  7.2 93.0 %all-gather.5.cloned.1.call-start = ((), (), s32[]{:S(2)}) async-start(), calls=%async_computation.5 | async-start | bytes 1310720 | tf_op jit(solution)/shard_map/all_gather | solution.py:189
  11.6 17.6 %collective-permute-start = (bf16[128,1408]{1,0:T(8,128)(2,1)S(1)}, bf16[128,1408]{1,0:T(8,128)(2,1)S(1)}, u32[]{:S(2)}, u32[]{:S(2)}) collective-permute-start(bf16[128,1408]{1,0:T(8,128)(2,1)S(1)} %concatenate.90), channel_id=1, source_target_pairs={{0,4},{4,0},{8,12},{12,8},{16,20},{20,16},{24,28},{28,24},{1,5},{5... | collective-permute-start | bytes 1081352 | tf_op jit(solution)/shard_map/ppermute | solution.py:156
  14.7 15.6 %collective-permute-start.1 = (bf16[128,1408]{1,0:T(8,128)(2,1)S(1)}, bf16[128,1408]{1,0:T(8,128)(2,1)S(1)}, u32[]{:S(2)}, u32[]{:S(2)}) collective-permute-start(bf16[128,1408]{1,0:T(8,128)(2,1)S(1)} %concatenate.90), channel_id=1, source_target_pairs={{0,8},{4,12},{8,16},{12,20},{16,24},{20,28},{24,0},{28,4},{1,9},{5... | collective-permute-start | bytes 1081352 | tf_op jit(solution)/shard_map/ppermute | solution.py:155
  16.2 28.2 %collective-permute-start.3 = (bf16[128,1408]{1,0:T(8,128)(2,1)S(1)}, bf16[128,1408]{1,0:T(8,128)(2,1)S(1)}, u32[]{:S(2)}, u32[]{:S(2)}) collective-permute-start(bf16[128,1408]{1,0:T(8,128)(2,1)S(1)} %concatenate.90), channel_id=1, source_target_pairs={{0,16},{4,20},{8,24},{12,28},{16,0},{20,4},{24,8},{28,12},{1,17},{... | collective-permute-start | bytes 1081352 | tf_op jit(solution)/shard_map/ppermute | solution.py:155
  18.8 36.9 %collective-permute-start.5 = (bf16[128,1408]{1,0:T(8,128)(2,1)S(1)}, bf16[128,1408]{1,0:T(8,128)(2,1)S(1)}, u32[]{:S(2)}, u32[]{:S(2)}) collective-permute-start(bf16[128,1408]{1,0:T(8,128)(2,1)S(1)} %concatenate.90), channel_id=1, source_target_pairs={{0,24},{4,28},{8,0},{12,4},{16,8},{20,12},{24,16},{28,20},{1,25},{... | collective-permute-start | bytes 1081352 | tf_op jit(solution)/shard_map/ppermute | solution.py:155
  23.1 68.7 %collective-permute-start.7 = (bf16[128,512]{1,0:T(8,128)(2,1)}, bf16[128,512]{1,0:T(8,128)(2,1)}, u32[]{:S(2)}, u32[]{:S(2)}) collective-permute-start(bf16[128,512]{1,0:T(8,128)(2,1)} %constant_dynamic-update-slice_fusion.7), channel_id=1, source_target_pairs={{0,4},{4,0},{8,12},{12,8},{16,20},{20,16},{24,28},{28,24},{1,5},{5... | collective-permute-start | bytes 393224 | tf_op jit(solution)/shard_map/ppermute | solution.py:156
  24.7 59.5 %copy-start.83 = (f32[128]{0:T(128)}, f32[128]{0:T(128)S(1)}, u32[]{:S(2)}) copy-start(f32[128]{0:T(128)S(1)} %fusion.228) | copy-start | bytes 1540
  24.7 61.6 %copy-start.80 = (f32[32]{0:T(128)}, f32[32]{0:T(128)S(1)}, u32[]{:S(2)}) copy-start(f32[32]{0:T(128)S(1)} %multiply_exponential_fusion) | copy-start | bytes 388
  29.3 59.8 %collective-permute-start.8 = (bf16[128,512]{1,0:T(8,128)(2,1)}, bf16[128,512]{1,0:T(8,128)(2,1)}, u32[]{:S(2)}, u32[]{:S(2)}) collective-permute-start(bf16[128,512]{1,0:T(8,128)(2,1)} %constant_dynamic-update-slice_fusion.7), channel_id=1, source_target_pairs={{0,8},{4,12},{8,16},{12,20},{16,24},{20,28},{24,0},{28,4},{1,9},{5... | collective-permute-start | bytes 393224 | tf_op jit(solution)/shard_map/ppermute | solution.py:155
  30.2 59.5 %collective-permute-start.10 = (bf16[128,512]{1,0:T(8,128)(2,1)}, bf16[128,512]{1,0:T(8,128)(2,1)}, u32[]{:S(2)}, u32[]{:S(2)}) collective-permute-start(bf16[128,512]{1,0:T(8,128)(2,1)} %constant_dynamic-update-slice_fusion.7), channel_id=1, source_target_pairs={{0,16},{4,20},{8,24},{12,28},{16,0},{20,4},{24,8},{28,12},{1,17},{... | collective-permute-start | bytes 393224 | tf_op jit(solution)/shard_map/ppermute | solution.py:155
  44.5 46.7 %collective-permute-start.12 = (bf16[128,512]{1,0:T(8,128)(2,1)}, bf16[128,512]{1,0:T(8,128)(2,1)}, u32[]{:S(2)}, u32[]{:S(2)}) collective-permute-start(bf16[128,512]{1,0:T(8,128)(2,1)} %constant_dynamic-update-slice_fusion.7), channel_id=1, source_target_pairs={{0,24},{4,28},{8,0},{12,4},{16,8},{20,12},{24,16},{28,20},{1,25},{... | collective-permute-start | bytes 393224 | tf_op jit(solution)/shard_map/ppermute | solution.py:155
  55.7 9.1 %collective-permute-start.2 = (bf16[128,1408]{1,0:T(8,128)(2,1)S(1)}, bf16[128,1408]{1,0:T(8,128)(2,1)S(1)}, u32[]{:S(2)}, u32[]{:S(2)}) collective-permute-start(bf16[128,1408]{1,0:T(8,128)(2,1)S(1)} %collective-permute-done.1), channel_id=1, source_target_pairs={{0,4},{4,0},{8,12},{12,8},{16,20},{20,16},{24,28},{28,24},{1,5},{5... | collective-permute-start | bytes 1081352 | tf_op jit(solution)/shard_map/ppermute | solution.py:157
  64.8 10.1 %collective-permute-start.4 = (bf16[128,1408]{1,0:T(8,128)(2,1)S(1)}, bf16[128,1408]{1,0:T(8,128)(2,1)S(1)}, u32[]{:S(2)}, u32[]{:S(2)}) collective-permute-start(bf16[128,1408]{1,0:T(8,128)(2,1)S(1)} %collective-permute-done.3), channel_id=1, source_target_pairs={{0,4},{4,0},{8,12},{12,8},{16,20},{20,16},{24,28},{28,24},{1,5},{5... | collective-permute-start | bytes 1081352 | tf_op jit(solution)/shard_map/ppermute | solution.py:157
  66.3 17.9 %copy-start.5 = (bf16[128,1024]{1,0:T(8,128)(2,1)S(1)}, bf16[128,1024]{1,0:T(8,128)(2,1)}, u32[]{:S(2)}) copy-start(bf16[128,1024]{1,0:T(8,128)(2,1)} %param.25) | copy-start | bytes 786436
  67.1 19.1 %copy-start.71 = (f32[4,1792]{1,0:T(4,128)S(1)}, f32[4,1792]{1,0:T(4,128)}, u32[]{:S(2)}) copy-start(f32[4,1792]{1,0:T(4,128)} %param.37) | copy-start | bytes 86020
  74.9 7.4 %collective-permute-start.6 = (bf16[128,1408]{1,0:T(8,128)(2,1)S(1)}, bf16[128,1408]{1,0:T(8,128)(2,1)S(1)}, u32[]{:S(2)}, u32[]{:S(2)}) collective-permute-start(bf16[128,1408]{1,0:T(8,128)(2,1)S(1)} %collective-permute-done.5), channel_id=1, source_target_pairs={{0,4},{4,0},{8,12},{12,8},{16,20},{20,16},{24,28},{28,24},{1,5},{5... | collective-permute-start | bytes 1081352 | tf_op jit(solution)/shard_map/ppermute | solution.py:157
  85.1 137.5 %reduce-scatter.6.cloned.1.call-start = ((), (), s32[]{:S(2)}) async-start(), calls=%async_computation.6 | async-start | bytes 1310720 | tf_op jit(solution)/shard_map/reduce_scatter | solution.py:200
  87.2 99.8 %copy-start.35 = (f32[512,32]{0,1:T(8,128)}, f32[512,32]{0,1:T(8,128)S(1)}, u32[]{:S(2)}) copy-start(f32[512,32]{0,1:T(8,128)S(1)} %get-tuple-element.1842) | copy-start | bytes 196612
  88.0 17.0 %copy-start.61 = (f32[640]{0:T(1024)}, f32[640]{0:T(1024)S(1)}, u32[]{:S(2)}) copy-start(f32[640]{0:T(1024)S(1)} %get-tuple-element.1654) | copy-start | bytes 7684
  88.0 17.0 %copy-start.63 = (f32[640]{0:T(1024)}, f32[640]{0:T(1024)S(1)}, u32[]{:S(2)}) copy-start(f32[640]{0:T(1024)S(1)} %get-tuple-element.1655) | copy-start | bytes 7684
  89.1 5.2 collective-permute-start.9
  89.7 6.0 collective-permute-start.11
  91.2 6.0 collective-permute-start.13
  197.5 51.4 %all-gather.9.cloned.1.call-start = ((), (), s32[]{:S(2)}) async-start(), calls=%async_computation.9 | async-start | bytes 1310720 | tf_op jit(solution)/shard_map/all_gather | solution.py:189
  198.2 61.6 %all-gather.7.cloned.1.call-start = ((), (), s32[]{:S(2)}) async-start(), calls=%async_computation.7 | async-start | bytes 1310720 | tf_op jit(solution)/shard_map/all_gather | solution.py:189
  198.3 14.0 %collective-permute-start.15 = (bf16[128,1536]{1,0:T(8,128)(2,1)S(1)}, bf16[128,1536]{1,0:T(8,128)(2,1)}, u32[]{:S(2)}, u32[]{:S(2)}) collective-permute-start(bf16[128,1536]{1,0:T(8,128)(2,1)S(1)} %constant_dynamic-update-slice_fusion.9), channel_id=1, source_target_pairs={{0,8},{4,12},{8,16},{12,20},{16,24},{20,28},{24,0},{28,4},{1,9},{5... | collective-permute-start | bytes 1179656 | tf_op jit(solution)/shard_map/ppermute | solution.py:155
  199.9 14.0 %collective-permute-start.14 = (bf16[128,1536]{1,0:T(8,128)(2,1)S(1)}, bf16[128,1536]{1,0:T(8,128)(2,1)S(1)}, u32[]{:S(2)}, u32[]{:S(2)}) collective-permute-start(bf16[128,1536]{1,0:T(8,128)(2,1)S(1)} %constant_dynamic-update-slice_fusion.9), channel_id=1, source_target_pairs={{0,4},{4,0},{8,12},{12,8},{16,20},{20,16},{24,28},{28,24},{1,5},{5... | collective-permute-start | bytes 1179656 | tf_op jit(solution)/shard_map/ppermute | solution.py:156
  201.3 27.2 %collective-permute-start.17 = (bf16[128,1536]{1,0:T(8,128)(2,1)S(1)}, bf16[128,1536]{1,0:T(8,128)(2,1)}, u32[]{:S(2)}, u32[]{:S(2)}) collective-permute-start(bf16[128,1536]{1,0:T(8,128)(2,1)S(1)} %constant_dynamic-update-slice_fusion.9), channel_id=1, source_target_pairs={{0,16},{4,20},{8,24},{12,28},{16,0},{20,4},{24,8},{28,12},{1,17},{... | collective-permute-start | bytes 1179656 | tf_op jit(solution)/shard_map/ppermute | solution.py:155
  203.8 26.3 %collective-permute-start.19 = (bf16[128,1536]{1,0:T(8,128)(2,1)S(1)}, bf16[128,1536]{1,0:T(8,128)(2,1)S(1)}, u32[]{:S(2)}, u32[]{:S(2)}) collective-permute-start(bf16[128,1536]{1,0:T(8,128)(2,1)S(1)} %constant_dynamic-update-slice_fusion.9), channel_id=1, source_target_pairs={{0,24},{4,28},{8,0},{12,4},{16,8},{20,12},{24,16},{28,20},{1,25},{... | collective-permute-start | bytes 1179656 | tf_op jit(solution)/shard_map/ppermute | solution.py:155
  212.4 18.2 %collective-permute-start.16 = (bf16[128,1536]{1,0:T(8,128)(2,1)}, bf16[128,1536]{1,0:T(8,128)(2,1)}, u32[]{:S(2)}, u32[]{:S(2)}) collective-permute-start(bf16[128,1536]{1,0:T(8,128)(2,1)} %collective-permute-done.15), channel_id=1, source_target_pairs={{0,4},{4,0},{8,12},{12,8},{16,20},{20,16},{24,28},{28,24},{1,5},{5... | collective-permute-start | bytes 1179656 | tf_op jit(solution)/shard_map/ppermute | solution.py:157
  223.7 17.9 %copy-start.89 = (f32[128]{0:T(128)}, f32[128]{0:T(128)S(1)}, u32[]{:S(2)}) copy-start(f32[128]{0:T(128)S(1)} %multiply_reduce_fusion.5) | copy-start | bytes 1540
  223.7 73.9 %copy-start.78 = (f32[128]{0:T(128)}, f32[128]{0:T(128)S(1)}, u32[]{:S(2)}) copy-start(f32[128]{0:T(128)S(1)} %fusion.229) | copy-start | bytes 1540
  225.5 70.3 %reduce-scatter.10.cloned.1.call-start = ((), (), s32[]{:S(2)}) async-start(), calls=%async_computation.10 | async-start | bytes 1310720 | tf_op jit(solution)/shard_map/reduce_scatter | solution.py:200
  228.5 12.2 %collective-permute-start.18 = (bf16[128,1536]{1,0:T(8,128)(2,1)}, bf16[128,1536]{1,0:T(8,128)(2,1)S(1)}, u32[]{:S(2)}, u32[]{:S(2)}) collective-permute-start(bf16[128,1536]{1,0:T(8,128)(2,1)} %collective-permute-done.17), channel_id=1, source_target_pairs={{0,4},{4,0},{8,12},{12,8},{16,20},{20,16},{24,28},{28,24},{1,5},{5... | collective-permute-start | bytes 1179656 | tf_op jit(solution)/shard_map/ppermute | solution.py:157
  230.0 18.1 %collective-permute-start.20 = (bf16[128,1536]{1,0:T(8,128)(2,1)S(1)}, bf16[128,1536]{1,0:T(8,128)(2,1)S(1)}, u32[]{:S(2)}, u32[]{:S(2)}) collective-permute-start(bf16[128,1536]{1,0:T(8,128)(2,1)S(1)} %collective-permute-done.19), channel_id=1, source_target_pairs={{0,4},{4,0},{8,12},{12,8},{16,20},{20,16},{24,28},{28,24},{1,5},{5... | collective-permute-start | bytes 1179656 | tf_op jit(solution)/shard_map/ppermute | solution.py:157
  267.7 28.1 %copy-start.9 = (bf16[128,1024]{1,0:T(8,128)(2,1)S(1)}, bf16[128,1024]{1,0:T(8,128)(2,1)}, u32[]{:S(2)}) copy-start(bf16[128,1024]{1,0:T(8,128)(2,1)} %reduce-scatter.6.cloned.1.call-done) | copy-start | bytes 786436
  267.7 29.9 %copy-start.90 = (f32[128]{0:T(128)S(1)}, f32[128]{0:T(128)}, u32[]{:S(2)}) copy-start(f32[128]{0:T(128)} %copy-done.89) | copy-start | bytes 1540
  267.7 29.9 %copy-start.17 = (bf16[128,1024]{1,0:T(8,128)(2,1)S(1)}, bf16[128,1024]{1,0:T(8,128)(2,1)}, u32[]{:S(2)}) copy-start(bf16[128,1024]{1,0:T(8,128)(2,1)} %param.26) | copy-start | bytes 786436
  270.7 28.9 %copy-start.60 = (f32[512,6]{0,1:T(8,128)S(1)}, f32[512,6]{0,1:T(8,128)}, u32[]{:S(2)}) copy-start(f32[512,6]{0,1:T(8,128)} %get-tuple-element.1840) | copy-start | bytes 36868
  270.7 45.6 %all-gather.11.cloned.1.call-start = ((), (), s32[]{:S(2)}) async-start(), calls=%async_computation.11 | async-start | bytes 1310720 | tf_op jit(solution)/shard_map/all_gather | solution.py:189
  299.5 200.6 %reduce-scatter.12.cloned.1.call-start = ((), (), s32[]{:S(2)}) async-start(), calls=%async_computation.12 | async-start | bytes 1310720 | tf_op jit(solution)/shard_map/reduce_scatter | solution.py:200
  303.5 17.4 %copy-start.47 = (bf16[512,64,1]{0,1,2:T(8,128)(2,1)S(1)}, bf16[512,64,1]{0,1,2:T(8,128)(2,1)}, u32[]{:S(2)}) copy-start(bf16[512,64,1]{0,1,2:T(8,128)(2,1)} %copy-done.46) | copy-start | bytes 196612
  475.0 106.3 %reduce-scatter.14.cloned.1.call-start = ((), (), s32[]{:S(2)}) async-start(), calls=%async_computation.13 | async-start | bytes 1638400 | tf_op jit(solution)/shard_map/reduce_scatter | solution.py:519
  486.9 36.8 %collective-permute-start.29 = (bf16[4,128,1536]{2,1,0:T(8,128)(2,1)}, bf16[4,128,1536]{2,1,0:T(8,128)(2,1)}, u32[]{:S(2)}, u32[]{:S(2)}) collective-permute-start(bf16[4,128,1536]{2,1,0:T(8,128)(2,1)} %dynamic-slice_bitcast_fusion), channel_id=1, source_target_pairs={{0,4},{4,0},{8,12},{12,8},{16,20},{20,16},{24,28},{28,24},{1,5},{5... | collective-permute-start | bytes 4718600 | tf_op jit(solution)/shard_map/ppermute | solution.py:179
  503.7 175.4 %reduce-scatter.8.cloned.1.call-start = ((), (), s32[]{:S(2)}) async-start(), calls=%async_computation.8 | async-start | bytes 1310720 | tf_op jit(solution)/shard_map/reduce_scatter | solution.py:200
  527.1 14.3 %collective-permute-start.30 = (bf16[128,1536]{1,0:T(8,128)(2,1)}, bf16[128,1536]{1,0:T(8,128)(2,1)}, u32[]{:S(2)}, u32[]{:S(2)}) collective-permute-start(bf16[128,1536]{1,0:T(8,128)(2,1)} %get-tuple-element.1803), channel_id=1, source_target_pairs={{0,8},{4,12},{8,16},{12,20},{16,24},{20,28},{24,0},{28,4},{1,9},{5... | collective-permute-start | bytes 1179656 | tf_op jit(solution)/shard_map/ppermute | solution.py:184
  528.6 28.1 %collective-permute-start.31 = (bf16[128,1536]{1,0:T(8,128)(2,1)}, bf16[128,1536]{1,0:T(8,128)(2,1)}, u32[]{:S(2)}, u32[]{:S(2)}) collective-permute-start(bf16[128,1536]{1,0:T(8,128)(2,1)} %get-tuple-element.1805), channel_id=1, source_target_pairs={{0,16},{4,20},{8,24},{12,28},{16,0},{20,4},{24,8},{28,12},{1,17},{... | collective-permute-start | bytes 1179656 | tf_op jit(solution)/shard_map/ppermute | solution.py:184
  531.0 25.6 %collective-permute-start.32 = (bf16[128,1536]{1,0:T(8,128)(2,1)}, bf16[128,1536]{1,0:T(8,128)(2,1)}, u32[]{:S(2)}, u32[]{:S(2)}) collective-permute-start(bf16[128,1536]{1,0:T(8,128)(2,1)} %get-tuple-element.1804), channel_id=1, source_target_pairs={{0,24},{4,28},{8,0},{12,4},{16,8},{20,12},{24,16},{28,20},{1,25},{... | collective-permute-start | bytes 1179656 | tf_op jit(solution)/shard_map/ppermute | solution.py:184
  535.6 23.5 %copy-start.75 = (f32[640]{0:T(1024)S(1)}, f32[640]{0:T(1024)}, u32[]{:S(2)}) copy-start(f32[640]{0:T(1024)} %get-tuple-element.1647) | copy-start | bytes 7684
  535.6 23.4 %copy-start.74 = (f32[640]{0:T(1024)S(1)}, f32[640]{0:T(1024)}, u32[]{:S(2)}) copy-start(f32[640]{0:T(1024)} %get-tuple-element.1643) | copy-start | bytes 7684
  535.6 23.4 %copy-start.73 = (f32[640]{0:T(1024)S(1)}, f32[640]{0:T(1024)}, u32[]{:S(2)}) copy-start(f32[640]{0:T(1024)} %get-tuple-element.1645) | copy-start | bytes 7684
  535.6 23.5 %copy-start.72 = (f32[640]{0:T(1024)S(1)}, f32[640]{0:T(1024)}, u32[]{:S(2)}) copy-start(f32[640]{0:T(1024)} %get-tuple-element.1644) | copy-start | bytes 7684
  535.6 23.5 %copy-start.69 = (f32[640]{0:T(1024)S(1)}, f32[640]{0:T(1024)}, u32[]{:S(2)}) copy-start(f32[640]{0:T(1024)} %get-tuple-element.1646) | copy-start | bytes 7684
  566.2 89.9 %collective-permute-start.25 = (bf16[4,128,512]{2,1,0:T(8,128)(2,1)}, bf16[4,128,512]{2,1,0:T(8,128)(2,1)}, u32[]{:S(2)}, u32[]{:S(2)}) collective-permute-start(bf16[4,128,512]{2,1,0:T(8,128)(2,1)} %fusion.182), channel_id=1, source_target_pairs={{0,4},{4,0},{8,12},{12,8},{16,20},{20,16},{24,28},{28,24},{1,5},{5... | collective-permute-start | bytes 1572872 | tf_op jit(solution)/shard_map/ppermute | solution.py:179
  584.4 71.7 %copy-start.21 = (bf16[4,2,128,128]{3,2,0,1:T(8,128)(2,1)S(1)}, bf16[4,2,128,128]{3,2,0,1:T(8,128)(2,1)}, u32[]{:S(2)}) copy-start(bf16[4,2,128,128]{3,2,0,1:T(8,128)(2,1)} %copy.522) | copy-start | bytes 786436
  590.5 80.5 %collective-permute-start.21 = (bf16[4,128,1062]{1,0,2:T(4,128)(2,1)}, bf16[4,128,1062]{1,0,2:T(4,128)(2,1)}, u32[]{:S(2)}, u32[]{:S(2)}) collective-permute-start(bf16[4,128,1062]{1,0,2:T(4,128)(2,1)} %copy.518), channel_id=1, source_target_pairs={{0,4},{4,0},{8,12},{12,8},{16,20},{20,16},{24,28},{28,24},{1,5},{5... | collective-permute-start | bytes 3262472 | tf_op jit(solution)/shard_map/ppermute | solution.py:179
  657.3 8.3 %collective-permute-start.26 = (bf16[128,512]{1,0:T(8,128)(2,1)S(1)}, bf16[128,512]{1,0:T(8,128)(2,1)S(1)}, u32[]{:S(2)}, u32[]{:S(2)}) collective-permute-start(bf16[128,512]{1,0:T(8,128)(2,1)S(1)} %get-tuple-element.1822), channel_id=1, source_target_pairs={{0,8},{4,12},{8,16},{12,20},{16,24},{20,28},{24,0},{28,4},{1,9},{5... | collective-permute-start | bytes 393224 | tf_op jit(solution)/shard_map/ppermute | solution.py:184
  659.5 10.1 %collective-permute-start.27 = (bf16[128,512]{1,0:T(8,128)(2,1)S(1)}, bf16[128,512]{1,0:T(8,128)(2,1)S(1)}, u32[]{:S(2)}, u32[]{:S(2)}) collective-permute-start(bf16[128,512]{1,0:T(8,128)(2,1)S(1)} %get-tuple-element.1824), channel_id=1, source_target_pairs={{0,16},{4,20},{8,24},{12,28},{16,0},{20,4},{24,8},{28,12},{1,17},{... | collective-permute-start | bytes 393224 | tf_op jit(solution)/shard_map/ppermute | solution.py:184
  660.4 9.2 %collective-permute-start.28 = (bf16[128,512]{1,0:T(8,128)(2,1)S(1)}, bf16[128,512]{1,0:T(8,128)(2,1)S(1)}, u32[]{:S(2)}, u32[]{:S(2)}) collective-permute-start(bf16[128,512]{1,0:T(8,128)(2,1)S(1)} %get-tuple-element.1823), channel_id=1, source_target_pairs={{0,24},{4,28},{8,0},{12,4},{16,8},{20,12},{24,16},{28,20},{1,25},{... | collective-permute-start | bytes 393224 | tf_op jit(solution)/shard_map/ppermute | solution.py:184
  673.7 12.3 %collective-permute-start.22 = (bf16[128,1062]{0,1:T(8,128)(2,1)}, bf16[128,1062]{0,1:T(8,128)(2,1)S(1)}, u32[]{:S(2)}, u32[]{:S(2)}) collective-permute-start(bf16[128,1062]{0,1:T(8,128)(2,1)} %get-tuple-element.1814), channel_id=1, source_target_pairs={{0,8},{4,12},{8,16},{12,20},{16,24},{20,28},{24,0},{28,4},{1,9},{5... | collective-permute-start | bytes 815624 | tf_op jit(solution)/shard_map/ppermute | solution.py:184
  676.7 18.8 %collective-permute-start.23 = (bf16[128,1062]{0,1:T(8,128)(2,1)S(1)}, bf16[128,1062]{0,1:T(8,128)(2,1)}, u32[]{:S(2)}, u32[]{:S(2)}) collective-permute-start(bf16[128,1062]{0,1:T(8,128)(2,1)S(1)} %get-tuple-element.1816), channel_id=1, source_target_pairs={{0,16},{4,20},{8,24},{12,28},{16,0},{20,4},{24,8},{28,12},{1,17},{... | collective-permute-start | bytes 815624 | tf_op jit(solution)/shard_map/ppermute | solution.py:184
  678.8 16.8 %collective-permute-start.24 = (bf16[128,1062]{0,1:T(8,128)(2,1)S(1)}, bf16[128,1062]{0,1:T(8,128)(2,1)}, u32[]{:S(2)}, u32[]{:S(2)}) collective-permute-start(bf16[128,1062]{0,1:T(8,128)(2,1)S(1)} %get-tuple-element.1815), channel_id=1, source_target_pairs={{0,24},{4,28},{8,0},{12,4},{16,8},{20,12},{24,16},{28,20},{1,25},{... | collective-permute-start | bytes 815624 | tf_op jit(solution)/shard_map/ppermute | solution.py:184
  679.1 22.8 %copy-start.1 = (f32[24]{0:T(128)S(1)}, f32[24]{0:T(128)}, u32[]{:S(2)}) copy-start(f32[24]{0:T(128)} %param.41) | copy-start | bytes 292
  (79 other events, 336.0 us)
Sparse Core Ops, SparseCore 0:
  85.2 14.9 all-gather.4
  197.6 24.9 reduce-scatter.5
  224.2 16.7 all-gather.8
  243.0 16.7 all-gather.6
  270.9 24.8 reduce-scatter.9
  299.6 16.7 all-gather.10
  475.2 24.8 reduce-scatter.11
  503.8 26.5 reduce-scatter.13
  535.7 22.1 reduce-scatter.7

commit v2 on v1

--- a/solution.py
+++ b/solution.py
@@ -1,8 +1,11 @@
+import functools
 import math
 
 import jax
 import jax.numpy as jnp
 from jax import lax
+from jax.experimental import pallas as pl
+from jax.experimental.pallas import tpu as pltpu
 from jax.sharding import PartitionSpec as P
 
 D = 1024
@@ -68,42 +71,242 @@
     return result
 
 
-def ssd_scan(series, step_sizes, decay_rates, input_map, output_map, skip_gain):
-    length, group_count, head_count, head_width = series.shape
-    blocks = length // SCAN_BLOCK
-
-    def by_block(values):
-        return values.reshape((blocks, SCAN_BLOCK) + values.shape[1:])
-
-    def advance(carry_state, block_data):
-        series_block, step_block, input_block, output_block = block_data
-        cumulative = jnp.cumsum(step_block * decay_rates, axis=0)
-        row_index = lax.broadcasted_iota(jnp.int32, (SCAN_BLOCK, SCAN_BLOCK), 0)
-        earlier = lax.broadcasted_iota(jnp.int32, (SCAN_BLOCK, SCAN_BLOCK), 1)
-        causal = (row_index >= earlier)[:, :, None, None]
-        log_gaps = jnp.where(causal, cumulative[:, None] - cumulative[None, :], -1e30)
-        affinity = jnp.einsum("tgn,sgn->tsg", output_block, input_block, precision=highest)
-        weights = jnp.exp(log_gaps) * affinity[..., None]
-        scaled = series_block * step_block[..., None]
-        within = jnp.einsum("tsgj,sgjp->tgjp", weights, scaled, precision=highest)
-        carried = (
-            jnp.einsum("tgn,gjpn->tgjp", output_block, carry_state, precision=highest)
-            * jnp.exp(cumulative)[..., None]
-        )
-        remain = jnp.exp(cumulative[-1][None] - cumulative)
-        written = jnp.einsum(
-            "sgjp,sgn->gjpn", scaled * remain[..., None], input_block, precision=highest
-        )
-        carry_state = carry_state * jnp.exp(cumulative[-1])[..., None, None] + written
-        return (carry_state, within + carried + series_block * skip_gain[..., None])
-
-    initial = jnp.zeros((group_count, head_count, head_width, input_map.shape[-1]), jnp.float32)
-    _, outputs = lax.scan(
-        advance,
-        initial,
-        (by_block(series), by_block(step_sizes), by_block(input_map), by_block(output_map)),
-    )
-    return outputs.reshape(series.shape)
+def low_dot(left, right, dims):
+    return lax.dot_general(
+        left.astype(jnp.bfloat16),
+        right.astype(jnp.bfloat16),
+        dims,
+        preferred_element_type=jnp.float32,
+    )
+
+
+plain = (((1,), (0,)), ((), ()))
+
+
+def head_lanes(values, first_head, heads, width):
+    rows = values.shape[0]
+    lane = lax.broadcasted_iota(jnp.int32, (rows, heads * width), 1)
+    spread = jnp.broadcast_to(values[:, first_head : first_head + 1], lane.shape)
+    for index in range(1, heads):
+        column = first_head + index
+        spread = jnp.where(
+            lane < index * width,
+            spread,
+            jnp.broadcast_to(values[:, column : column + 1], lane.shape),
+        )
+    return spread
+
+
+def decay_weights(column, row):
+    size = column.shape[0]
+    later = lax.broadcasted_iota(jnp.int32, (size, size), 0)
+    earlier = lax.broadcasted_iota(jnp.int32, (size, size), 1)
+    return jnp.exp(jnp.where(later >= earlier, column - row, -1e30))
+
+
+def scan_forward_kernel(
+    slab_heads, width, heads, x_ref, cum_ref, cumt_ref, b_ref, c_ref, y_ref, saved_ref, state_ref
+):
+    @pl.when(pl.program_id(0) == 0)
+    def _():
+        state_ref[...] = jnp.zeros_like(state_ref)
+
+    size = x_ref.shape[0]
+    slab = slab_heads * width
+    saved_ref[0] = state_ref[...]
+    cum = cum_ref[...]
+    input_map, output_map = b_ref[...], c_ref[...]
+    affinity = low_dot(output_map, input_map, by_columns)
+    lane = lax.broadcasted_iota(jnp.int32, (size, slab), 1)
+    for first in range(0, heads, slab_heads):
+        cols = slice(first * width, first * width + slab)
+        series = x_ref[:, cols]
+        state = state_ref[:, cols]
+        spread = head_lanes(cum, first, slab_heads, width)
+        last = spread[size - 1 : size]
+        result = low_dot(output_map, state, plain) * jnp.exp(spread)
+        for index in range(slab_heads):
+            head = first + index
+            decay = decay_weights(cum[:, head : head + 1], cumt_ref[head : head + 1, :])
+            own = (lane >= index * width) & (lane < (index + 1) * width)
+            result = result + low_dot(decay * affinity, jnp.where(own, series, 0.0), plain)
+        y_ref[:, cols] = result
+        state_ref[:, cols] = state * jnp.exp(last) + low_dot(
+            input_map, series * jnp.exp(last - spread), by_rows
+        )
+
+
+def scan_backward_kernel(
+    slab_heads,
+    width,
+    heads,
+    x_ref,
+    cum_ref,
+    cumt_ref,
+    b_ref,
+    c_ref,
+    saved_ref,
+    g_ref,
+    dx_ref,
+    dcum_ref,
+    dcumt_ref,
+    db_ref,
+    dc_ref,
+    state_ref,
+):
+    @pl.when(pl.program_id(0) == 0)
+    def _():
+        state_ref[...] = jnp.zeros_like(state_ref)
+
+    size = x_ref.shape[0]
+    slab = slab_heads * width
+    cum = cum_ref[...]
+    input_map, output_map = b_ref[...], c_ref[...]
+    affinity = low_dot(output_map, input_map, by_columns)
+    lane = lax.broadcasted_iota(jnp.int32, (size, slab), 1)
+    cum_lane = lax.broadcasted_iota(jnp.int32, cum.shape, 1)
+    cum_row = lax.broadcasted_iota(jnp.int32, cum.shape, 0)
+    d_cum = jnp.zeros(cum.shape, jnp.float32)
+    d_affinity = jnp.zeros((size, size), jnp.float32)
+    d_input = jnp.zeros(input_map.shape, jnp.float32)
+    d_output = jnp.zeros(output_map.shape, jnp.float32)
+    dcumt_ref[...] = jnp.zeros_like(dcumt_ref)
+    for first in range(0, heads, slab_heads):
+        cols = slice(first * width, first * width + slab)
+        series = x_ref[:, cols]
+        gradient = g_ref[:, cols]
+        state = saved_ref[0, :, cols]
+        d_state = state_ref[:, cols]
+        spread = head_lanes(cum, first, slab_heads, width)
+        last = spread[size - 1 : size]
+        remain = jnp.exp(last - spread)
+        grown = gradient * jnp.exp(spread)
+        kept = series * remain
+        d_kept = low_dot(input_map, d_state, plain)
+        d_output = d_output + low_dot(grown, state, by_columns)
+        d_input = d_input + low_dot(kept, d_state, by_columns)
+        written = d_kept * kept
+        position = grown * low_dot(output_map, state, plain) - written
+        decayed = d_state * jnp.exp(last)
+        final = jnp.sum(decayed * state, 0, keepdims=True) + jnp.sum(written, 0, keepdims=True)
+        d_series = d_kept * remain
+        for index in range(slab_heads):
+            head = first + index
+            decay = decay_weights(cum[:, head : head + 1], cumt_ref[head : head + 1, :])
+            own = (lane >= index * width) & (lane < (index + 1) * width)
+            own_gradient = jnp.where(own, gradient, 0.0)
+            d_weights = low_dot(own_gradient, series, by_columns) * decay
+            d_affinity = d_affinity + d_weights
+            d_gaps = d_weights * affinity
+            d_series = d_series + low_dot(decay * affinity, own_gradient, by_rows)
+            column = jnp.sum(d_gaps, 1, keepdims=True) + jnp.sum(
+                jnp.where(own, position, 0.0), 1, keepdims=True
+            )
+            total = jnp.sum(jnp.where(own[:1], final, 0.0), 1, keepdims=True)
+            column = jnp.where(cum_row == size - 1, column + total, column)
+            d_cum = jnp.where(cum_lane == head, column, d_cum)
+            dcumt_ref[head : head + 1, :] = -jnp.sum(d_gaps, 0, keepdims=True)
+        dx_ref[:, cols] = d_series
+        state_ref[:, cols] = decayed + low_dot(output_map, grown, by_rows)
+    dcum_ref[...] = d_cum
+    db_ref[...] = d_input + low_dot(d_affinity, output_map, by_rows)
+    dc_ref[...] = d_output + low_dot(d_affinity, input_map, plain)
+
+
+def scan_sizes(series, cum):
+    length, channels = series.shape
+    heads = cum.shape[1]
+    width = channels // heads
+    slab_heads = max(1, 128 // width)
+    while heads % slab_heads:
+        slab_heads -= 1
+    return length, channels, heads, width, slab_heads, length // SCAN_BLOCK
+
+
+def padded_cum(cum, heads):
+    padded = -(-heads // 8) * 8
+    return jnp.pad(cum, ((0, 0), (0, 128 - heads))), jnp.pad(cum.T, ((0, padded - heads), (0, 0)))
+
+
+def scan_run(series, cum, input_map, output_map):
+    length, channels, heads, width, slab_heads, blocks = scan_sizes(series, cum)
+    wide, tall = padded_cum(cum, heads)
+
+    def rows(columns):
+        return pl.BlockSpec((SCAN_BLOCK, columns), lambda i: (i, 0))
+
+    return pl.pallas_call(
+        functools.partial(scan_forward_kernel, slab_heads, width, heads),
+        grid=(blocks,),
+        in_specs=[
+            rows(channels),
+            rows(128),
+            pl.BlockSpec((tall.shape[0], SCAN_BLOCK), lambda i: (0, i)),
+            rows(STATE),
+            rows(STATE),
+        ],
+        out_specs=[rows(channels), pl.BlockSpec((1, STATE, channels), lambda i: (i, 0, 0))],
+        out_shape=[
+            jax.ShapeDtypeStruct((length, channels), jnp.float32),
+            jax.ShapeDtypeStruct((blocks, STATE, channels), jnp.float32),
+        ],
+        scratch_shapes=[pltpu.VMEM((STATE, channels), jnp.float32)],
+        compiler_params=pltpu.CompilerParams(vmem_limit_bytes=16 * 1024 * 1024),
+        cost_estimate=pl.CostEstimate(
+            flops=400_000_000, bytes_accessed=4_000_000, transcendentals=800_000
+        ),
+    )(series, wide, tall, input_map, output_map)
+
+
+@jax.custom_vjp
+def scan_core(series, cum, input_map, output_map):
+    return scan_run(series, cum, input_map, output_map)[0]
+
+
+def scan_core_forward(series, cum, input_map, output_map):
+    outputs, saved = scan_run(series, cum, input_map, output_map)
+    return outputs, (series, cum, input_map, output_map, saved)
+
+
+def scan_core_backward(residuals, gradient):
+    series, cum, input_map, output_map, saved = residuals
+    length, channels, heads, width, slab_heads, blocks = scan_sizes(series, cum)
+    wide, tall = padded_cum(cum, heads)
+
+    def rows(columns):
+        return pl.BlockSpec((SCAN_BLOCK, columns), lambda i: (blocks - 1 - i, 0))
+
+    across = pl.BlockSpec((tall.shape[0], SCAN_BLOCK), lambda i: (0, blocks - 1 - i))
+    d_series, d_wide, d_tall, d_input, d_output = pl.pallas_call(
+        functools.partial(scan_backward_kernel, slab_heads, width, heads),
+        grid=(blocks,),
+        in_specs=[
+            rows(channels),
+            rows(128),
+            across,
+            rows(STATE),
+            rows(STATE),
+            pl.BlockSpec((1, STATE, channels), lambda i: (blocks - 1 - i, 0, 0)),
+            rows(channels),
+        ],
+        out_specs=[rows(channels), rows(128), across, rows(STATE), rows(STATE)],
+        out_shape=[
+            jax.ShapeDtypeStruct((length, channels), jnp.float32),
+            jax.ShapeDtypeStruct((length, 128), jnp.float32),
+            jax.ShapeDtypeStruct(tall.shape, jnp.float32),
+            jax.ShapeDtypeStruct((length, STATE), jnp.float32),
+            jax.ShapeDtypeStruct((length, STATE), jnp.float32),
+        ],
+        scratch_shapes=[pltpu.VMEM((STATE, channels), jnp.float32)],
+        compiler_params=pltpu.CompilerParams(vmem_limit_bytes=16 * 1024 * 1024),
+        cost_estimate=pl.CostEstimate(
+            flops=2_000_000_000, bytes_accessed=40_000_000, transcendentals=1_600_000
+        ),
+    )(series, wide, tall, input_map, output_map, saved, gradient)
+    return d_series, d_wide[:, :heads] + d_tall[:heads].T, d_input, d_output
+
+
+scan_core.defvjp(scan_core_forward, scan_core_backward)
 
 
 def mamba_core(
@@ -122,15 +325,24 @@
     activated = jax.nn.silu(
         causal_conv(jnp.concatenate([input_proj, state_proj], 1), kernel_local, bias_local)
     )
-    series = activated[:, :channel_count].reshape(
-        length, 1, heads_here, channel_count // heads_here
-    )
-    input_map = activated[:, channel_count : channel_count + STATE][:, None]
-    output_map = activated[:, channel_count + STATE :][:, None]
-    step_sizes = jax.nn.softplus(step_proj + step_local)[:, None]
-    decay_rates = (-jnp.exp(decay_local))[None]
-    scanned = ssd_scan(series, step_sizes, decay_rates, input_map, output_map, skip_local[None])
-    return scanned.reshape(length, channel_count) * jax.nn.silu(gate_proj)
+    series = activated[:, :channel_count]
+    input_map = activated[:, channel_count : channel_count + STATE]
+    output_map = activated[:, channel_count + STATE :]
+    step_sizes = jax.nn.softplus(step_proj + step_local)
+    decay_rates = -jnp.exp(decay_local)
+    position = lax.broadcasted_iota(jnp.int32, (SCAN_BLOCK, SCAN_BLOCK), 0)
+    earlier = lax.broadcasted_iota(jnp.int32, (SCAN_BLOCK, SCAN_BLOCK), 1)
+    cum = jnp.einsum(
+        "ts,bsh->bth",
+        (position >= earlier).astype(jnp.float32),
+        (step_sizes * decay_rates).reshape(-1, SCAN_BLOCK, heads_here),
+        precision=highest,
+    ).reshape(length, heads_here)
+    width = channel_count // heads_here
+    scanned = scan_core(
+        series * jnp.repeat(step_sizes, width, axis=1), cum, input_map, output_map
+    ) + series * jnp.repeat(skip_local, width)
+    return scanned * jax.nn.silu(gate_proj)
 
 
 def partner_pairs(count):
@@ -468,39 +680,6 @@
     grad_input_ssm = weight_grad(mixer_rows, input_proj_low)
     grad_state = weight_grad(mixer_rows, state_proj_low)
     grad_step = weight_grad(mixer_rows, step_proj_low)
-    kernel_full = jnp.concatenate(
-        [
-            lax.dynamic_update_slice_in_dim(
-                jnp.zeros((KCONV, full_width), jnp.float32),
-                kernel_grad[:, :scan_width],
-                tensor_index * scan_width,
-                1,
-            ),
-            kernel_grad[:, scan_width:],
-        ],
-        1,
-    )
-    bias_full = jnp.concatenate(
-        [
-            lax.dynamic_update_slice_in_dim(
-                jnp.zeros((full_width,), jnp.float32),
-                bias_grad[:scan_width],
-                tensor_index * scan_width,
-                0,
-            ),
-            bias_grad[scan_width:],
-        ],
-        0,
-    )
-    decay_full = lax.dynamic_update_slice_in_dim(
-        jnp.zeros((SSM_HEADS,), jnp.float32), decay_grad, tensor_index * scan_heads, 0
-    )
-    step_bias_full = lax.dynamic_update_slice_in_dim(
-        jnp.zeros((SSM_HEADS,), jnp.float32), step_bias_grad, tensor_index * scan_heads, 0
-    )
-    skip_full = lax.dynamic_update_slice_in_dim(
-        jnp.zeros((SSM_HEADS,), jnp.float32), skip_grad, tensor_index * scan_heads, 0
-    )
     count = lax.axis_size("dp")
     tensor_size = lax.axis_size("tensor")
     low = jnp.bfloat16
@@ -551,14 +730,33 @@
     mlp_gain_sum = shared_sum[:, shared_width - 127]
     mix_sums = (query_sum, attention_sum, gate_ssm_sum, input_ssm_sum, step_sum, mamba_out_sum)
     shared_sums = (mix_gain_sum, mlp_gain_sum, key_sum, value_sum, state_sum)
-    small_parts = (kernel_full, bias_full, decay_full, step_bias_full, skip_full)
-    small_flat = lax.psum(
-        jnp.concatenate([part.reshape(-1) for part in small_parts]), ("dp", "tensor")
-    )
-    small_sums, start = [], 0
-    for part in small_parts:
-        small_sums.append(small_flat[start : start + part.size].reshape(part.shape))
-        start += part.size
+    small_own = jnp.concatenate(
+        [kernel_grad.reshape(-1), bias_grad, decay_grad, step_bias_grad, skip_grad]
+    )
+    small_rows = -(-small_own.shape[0] // 1024) * 8
+    small_own = jnp.pad(small_own, (0, small_rows * 128 - small_own.shape[0]))
+    small_every = lax.all_gather(
+        small_own.reshape(small_rows, 128), ("dp", "tensor"), axis=0, tiled=True
+    )
+    small_tensor = jnp.sum(small_every.reshape(count, tensor_size, -1), 0)
+    local_width = kernel_grad.shape[1]
+    taps = small_tensor[:, : KCONV * local_width].reshape(tensor_size, KCONV, local_width)
+    bias_start = KCONV * local_width
+    biases = small_tensor[:, bias_start : bias_start + local_width]
+    small_sums = [
+        jnp.concatenate(
+            [
+                taps[:, :, :scan_width].transpose(1, 0, 2).reshape(KCONV, full_width),
+                jnp.sum(taps[:, :, scan_width:], 0),
+            ],
+            1,
+        ),
+        jnp.concatenate([biases[:, :scan_width].reshape(-1), jnp.sum(biases[:, scan_width:], 0)]),
+    ]
+    start = bias_start + local_width
+    for _ in range(3):
+        small_sums.append(small_tensor[:, start : start + scan_heads].reshape(-1))
+        start += scan_heads
     return (
         output,
         grad_inputs,

time: 721 us -> 520 us (0.72)
  local copies, waits for them, and re-layouts: 192 us -> 116 us
  matrix products: 127 us -> 79.4 us
  other arithmetic: 77.9 us -> 34.6 us
  waiting for transfers between devices: 162 us -> 147 us
  blocking collectives: 63.1 us -> 48.5 us
    psum x1 -> x0, blocking collectives: 63.1 us -> none  [local(): lax.psum(jnp.concatenate([part.reshape(-1) for part in small_parts]), ('d...]
    dynamic_update_slice x48 -> x0, local copies, waits for them, and re-layouts: 60.8 us -> none  [the longest x44 60.2 us: ssd_scan(): lax.scan(advance, initial, (by_block(series), by_block(step_sizes), by_bl...]
    dot_general x48 -> x2, matrix products: 55.3 us -> 1.76 us  [mamba_core(): jnp.einsum('ts,bsh->bth', (position >= earlier).astype(jnp.float32), (ste...]
    all_gather x0 -> x1, blocking collectives: none -> 48.5 us  [local(): lax.all_gather(small_own.reshape(small_rows, 128), ('dp', 'tensor'), axis...]
    dynamic_update_slice x17 -> x0, other arithmetic: 16.7 us -> none  [the longest x16 16.4 us: ssd_scan(): lax.scan(advance, initial, (by_block(series), by_block(step_sizes), by_bl...]
    mul x25 -> x2, local copies, waits for them, and re-layouts: 13.9 us -> 1.82 us  [the longest x1 1.17 us: mamba_core(): series * jnp.repeat(step_sizes, width, axis=1)]
    dynamic_slice x20 -> x1, local copies, waits for them, and re-layouts: 12.1 us -> 0.07 us  [local(): lax.dynamic_slice_in_dim(skip_weight, tensor_index * scan_heads, scan_hea...]
    add_any x12 -> x0, other arithmetic: 11.1 us -> none  [the longest x4 4.02 us: advance(): cumulative = jnp.cumsum(step_block * decay_rates, axis=0)]
  transfers between devices with their start and end apart: 42 -> 42, of which waited for: 23 -> 20; matrix products, arithmetic and copies ran while one was open for 16% -> 26% of each run, Pallas kernels for 0% -> 0%
where the time goes in v2:
time: 520 us; the launch traced here: 511 us
  waiting for transfers between devices  147 us (28%)
  local copies, waits for them, and re-layouts  116 us (22%)
  matrix products  79.4 us (15%)
  starting transfers between devices  64.1 us (12%)
  blocking collectives  48.5 us (9%)
  other arithmetic  34.6 us (7%)
  between operations  15.9 us (3%)
  Pallas kernels  5.52 us (1%)
    all_gather x1, blocking collectives, local(): lax.all_gather(small_own.reshape(small_rows, 128), ('dp', 'tensor'), axis...  48.5 us
    ppermute x9, waiting for transfers between devices, reduce_dp(): lax.ppermute(block, 'dp', shift_pairs(count, steps)).astype(jnp.float32)  43.3 us
    ppermute x9, starting transfers between devices, gather_dp(): lax.ppermute(piece, 'dp', shift_pairs(count, steps))  33.8 us
    dot_general x12, matrix products, summed_rows(): lax.dot_general(left_side, right_side, by_columns, preferred_element_type...  29 us
    reduce_scatter x4, waiting for transfers between devices, summed_rows(): lax.psum_scatter(running.astype(jnp.bfloat16), 'tensor', scatter_dimensio...  27.4 us
    dynamic_update_slice x24, local copies, waits for them, and re-layouts, put(): return lax.dynamic_update_slice_in_dim(result, block, source * rows, 0)  26.9 us
    ppermute x9, waiting for transfers between devices, gather_dp(): crossed = [lax.ppermute(block, 'dp', partner_pairs(count)) for block in far]  26 us
    ppermute x3, waiting for transfers between devices, reduce_dp(): arrived = lax.ppermute(sent, 'dp', partner_pairs(count))  22 us
  transfers between devices with their start and end apart: 42, of which 20 were waited for; matrix products, arithmetic and copies ran while one was open for 26% of the time, Pallas kernels for 0%

profile of v2, /device:TPU:0, one launch (start us, length us, event | category | flops | bytes accessed | tf_op | source)
XLA Modules:
  0.0 510.9 jit_solution(2647619203440279528)
XLA Ops:
  11.6 3.0 collective-permute-start
  16.3 2.6 collective-permute-start.3
  28.0 1.9 copy.326
  29.9 14.5 %collective-permute-start.10 = (bf16[128,512]{1,0:T(8,128)(2,1)}, bf16[128,512]{1,0:T(8,128)(2,1)}, u32[]{:S(2)}, u32[]{:S(2)}) collective-permute-start(bf16[128,512]{1,0:T(8,128)(2,1)} %constant_dynamic-update-slice_fusion), channel_id=1, source_target_pairs={{0,16},{4,20},{8,24},{12,28},{16,0},{20,4},{24,8},{28,12},{1,17},{... | collective-permute-start | bytes 393224 | tf_op jit(solution)/shard_map/ppermute | solution.py:367
  44.3 1.9 copy.327
  46.2 9.4 %collective-permute-start.12 = (bf16[128,512]{1,0:T(8,128)(2,1)}, bf16[128,512]{1,0:T(8,128)(2,1)}, u32[]{:S(2)}, u32[]{:S(2)}) collective-permute-start(bf16[128,512]{1,0:T(8,128)(2,1)} %constant_dynamic-update-slice_fusion), channel_id=1, source_target_pairs={{0,24},{4,28},{8,0},{12,4},{16,8},{20,12},{24,16},{28,20},{1,25},{... | collective-permute-start | bytes 393224 | tf_op jit(solution)/shard_map/ppermute | solution.py:367
  55.6 1.9 copy.329
  61.4 5.1 collective-permute-done.2
  67.0 1.9 copy.328
  71.1 5.5 %collective-permute-done.4 = bf16[128,1408]{1,0:T(8,128)(2,1)} collective-permute-done((bf16[128,1408]{1,0:T(8,128)(2,1)}, bf16[128,1408]{1,0:T(8,128)(2,1)}, u32[]{:S(2)}, u32[]{:S(2)}) %collective-permute-start.4) | collective-permute-done | bytes 360480 | tf_op jit(solution)/shard_map/ppermute | solution.py:369
  77.1 1.9 copy.330
  80.3 4.0 collective-permute-done.6
  109.6 2.2 compare_select_fusion.2
  112.2 2.1 fusion.45
  117.0 1.9 fusion.10
  126.6 2.8 multiply_convert_fusion.3
  130.2 1.9 fusion.37
  132.0 2.5 add_convert_fusion.2
  141.4 3.1 collective-permute-start.19
  144.5 1.9 broadcast_in_dim.89
  148.1 5.3 %collective-permute-done.15 = bf16[128,1536]{1,0:T(8,128)(2,1)} collective-permute-done((bf16[128,1536]{1,0:T(8,128)(2,1)}, bf16[128,1536]{1,0:T(8,128)(2,1)}, u32[]{:S(2)}, u32[]{:S(2)}) %collective-permute-start.15) | collective-permute-done | bytes 393248 | tf_op jit(solution)/shard_map/ppermute | solution.py:367
  155.7 2.2 reduce-scatter.6.cloned.1.call-done
  162.9 2.8 collective-permute-done.17
  171.2 6.6 %collective-permute-done.18 = bf16[128,1536]{1,0:T(8,128)(2,1)S(1)} collective-permute-done((bf16[128,1536]{1,0:T(8,128)(2,1)}, bf16[128,1536]{1,0:T(8,128)(2,1)S(1)}, u32[]{:S(2)}, u32[]{:S(2)}) %collective-permute-start.18) | collective-permute-done | bytes 393248 | tf_op jit(solution)/shard_map/ppermute | solution.py:369
  180.4 4.8 collective-permute-done.20
  186.0 3.2 convolution_bitcast_fusion
  189.2 5.9 %all-gather.7.cloned.1.call-done = bf16[512,1024]{1,0:T(8,128)(2,1)} async-done(((bf16[128,1024]{1,0:T(8,128)(2,1)}), bf16[512,1024]{1,0:T(8,128)(2,1)}) %all-gather.7.cloned.1.call-update) | async-done | bytes 1048592 | tf_op jit(solution)/shard_map/all_gather | solution.py:401
  195.1 2.4 fusion.24
  197.5 3.2 multiply_convert_fusion.1
  201.6 2.0 fusion.22
  203.6 3.0 add_convert_fusion.1
  206.6 25.0 %reduce-scatter.10.cloned.1.call-done = bf16[128,1024]{1,0:T(8,128)(2,1)} async-done(((bf16[512,1024]{1,0:T(8,128)(2,1)}), bf16[128,1024]{1,0:T(8,128)(2,1)}) %reduce-scatter.10.cloned.1.call-update) | async-done | bytes 262160 | tf_op jit(solution)/shard_map/reduce_scatter | solution.py:412
  232.9 2.0 fusion.128
  235.1 3.1 convolution_convert_fusion.1
  238.2 13.7 %all-gather.11.cloned.1.call-done = bf16[512,1024]{1,0:T(8,128)(2,1)} async-done(((bf16[128,1024]{1,0:T(8,128)(2,1)}), bf16[512,1024]{1,0:T(8,128)(2,1)}) %all-gather.11.cloned.1.call-update) | async-done | bytes 1048592 | tf_op jit(solution)/shard_map/all_gather | solution.py:401
  251.9 1.9 convolution_convert_fusion.11
  253.8 2.0 fusion.14
  259.4 3.5 multiply_reduce_fusion.4
  262.9 3.9 transpose_jvp___.1
  277.9 2.7 fusion.84
  280.6 2.1 fusion.39
  282.6 2.0 fusion.43
  289.7 4.9 add_convert_fusion
  299.2 2.2 convolution_convert_fusion.2
  309.6 2.9 dynamic_update_slice.111
  314.9 2.9 dynamic_update_slice.110
  323.2 3.7 concatenate.112
  327.0 13.1 %collective-permute-done.29 = bf16[4,128,1536]{2,1,0:T(8,128)(2,1)} collective-permute-done((bf16[4,128,1536]{2,1,0:T(8,128)(2,1)S(1)}, bf16[4,128,1536]{2,1,0:T(8,128)(2,1)}, u32[]{:S(2)}, u32[]{:S(2)}) %collective-permute-start.29) | collective-permute-done | bytes 1572896 | tf_op jit(solution)/shard_map/ppermute | solution.py:391
  340.2 2.3 fusion
  344.9 2.4 collective-permute-start.31
  348.7 3.2 convolution_convert_fusion.3
  352.0 5.7 %collective-permute-done.30 = bf16[128,1536]{1,0:T(8,128)(2,1)S(1)} collective-permute-done((bf16[128,1536]{1,0:T(8,128)(2,1)}, bf16[128,1536]{1,0:T(8,128)(2,1)S(1)}, u32[]{:S(2)}, u32[]{:S(2)}) %collective-permute-start.30) | collective-permute-done | bytes 393248 | tf_op jit(solution)/shard_map/ppermute | solution.py:396
  357.7 15.3 %collective-permute-done.31 = bf16[128,1536]{1,0:T(8,128)(2,1)} collective-permute-done((bf16[128,1536]{1,0:T(8,128)(2,1)}, bf16[128,1536]{1,0:T(8,128)(2,1)}, u32[]{:S(2)}, u32[]{:S(2)}) %collective-permute-start.31) | collective-permute-done | bytes 393248 | tf_op jit(solution)/shard_map/ppermute | solution.py:396
  375.8 48.5 %all_gather.19 = f32[1024,128]{1,0:T(8,128)S(1)} all-gather(f32[32,128]{1,0:T(8,128)S(1)} %pad_bitcast_fusion), channel_id=1, replica_groups=mesh['dp'=8,'tensor'=4] {'dp','tensor'}, dimensions={0}, use_global_device_ids=true | all-gather | bytes 540672 | tf_op jit(solution)/shard_map/all_gather | solution.py:738
  442.2 4.8 copy.360
  447.0 2.0 collective-permute-start.21
  450.5 3.7 collective-permute-start.28
  456.6 2.0 collective-permute-done.26
  458.6 4.5 collective-permute-done.27
  464.6 8.9 %collective-permute-done.21 = bf16[4,128,1062]{1,0,2:T(4,128)(2,1)} collective-permute-done((bf16[4,128,1062]{1,0,2:T(4,128)(2,1)}, bf16[4,128,1062]{1,0,2:T(4,128)(2,1)}, u32[]{:S(2)}, u32[]{:S(2)}) %collective-permute-start.21) | collective-permute-done | bytes 1087520 | tf_op jit(solution)/shard_map/ppermute | solution.py:391
  476.1 3.8 collective-permute-start.24
  480.0 2.2 fusion.59
  482.2 5.5 %collective-permute-done.22 = bf16[128,1062]{0,1:T(8,128)(2,1)S(1)} collective-permute-done((bf16[128,1062]{0,1:T(8,128)(2,1)}, bf16[128,1062]{0,1:T(8,128)(2,1)S(1)}, u32[]{:S(2)}, u32[]{:S(2)}) %collective-permute-start.22) | collective-permute-done | bytes 271904 | tf_op jit(solution)/shard_map/ppermute | solution.py:396
  487.7 10.3 %collective-permute-done.23 = bf16[128,1062]{0,1:T(8,128)(2,1)S(1)} collective-permute-done((bf16[128,1062]{0,1:T(8,128)(2,1)S(1)}, bf16[128,1062]{0,1:T(8,128)(2,1)S(1)}, u32[]{:S(2)}, u32[]{:S(2)}) %collective-permute-start.23) | collective-permute-done | bytes 271904 | tf_op jit(solution)/shard_map/ppermute | solution.py:396
  (503 shorter events, 165.1 us)
Async XLA Ops:
  7.2 99.0 %all-gather.5.cloned.1.call-start = ((), (), s32[]{:S(2)}) async-start(), calls=%async_computation.5 | async-start | bytes 1310720 | tf_op jit(solution)/shard_map/all_gather | solution.py:401
  11.6 15.6 %collective-permute-start = (bf16[128,1408]{1,0:T(8,128)(2,1)S(1)}, bf16[128,1408]{1,0:T(8,128)(2,1)}, u32[]{:S(2)}, u32[]{:S(2)}) collective-permute-start(bf16[128,1408]{1,0:T(8,128)(2,1)S(1)} %concatenate.93), channel_id=1, source_target_pairs={{0,4},{4,0},{8,12},{12,8},{16,20},{20,16},{24,28},{28,24},{1,5},{5... | collective-permute-start | bytes 1081352 | tf_op jit(solution)/shard_map/ppermute | solution.py:368
  14.7 15.2 %collective-permute-start.1 = (bf16[128,1408]{1,0:T(8,128)(2,1)S(1)}, bf16[128,1408]{1,0:T(8,128)(2,1)}, u32[]{:S(2)}, u32[]{:S(2)}) collective-permute-start(bf16[128,1408]{1,0:T(8,128)(2,1)S(1)} %concatenate.93), channel_id=1, source_target_pairs={{0,8},{4,12},{8,16},{12,20},{16,24},{20,28},{24,0},{28,4},{1,9},{5... | collective-permute-start | bytes 1081352 | tf_op jit(solution)/shard_map/ppermute | solution.py:367
  16.3 30.0 %collective-permute-start.3 = (bf16[128,1408]{1,0:T(8,128)(2,1)S(1)}, bf16[128,1408]{1,0:T(8,128)(2,1)}, u32[]{:S(2)}, u32[]{:S(2)}) collective-permute-start(bf16[128,1408]{1,0:T(8,128)(2,1)S(1)} %concatenate.93), channel_id=1, source_target_pairs={{0,16},{4,20},{8,24},{12,28},{16,0},{20,4},{24,8},{28,12},{1,17},{... | collective-permute-start | bytes 1081352 | tf_op jit(solution)/shard_map/ppermute | solution.py:367
  18.8 38.7 %collective-permute-start.5 = (bf16[128,1408]{1,0:T(8,128)(2,1)S(1)}, bf16[128,1408]{1,0:T(8,128)(2,1)}, u32[]{:S(2)}, u32[]{:S(2)}) collective-permute-start(bf16[128,1408]{1,0:T(8,128)(2,1)S(1)} %concatenate.93), channel_id=1, source_target_pairs={{0,24},{4,28},{8,0},{12,4},{16,8},{20,12},{24,16},{28,20},{1,25},{... | collective-permute-start | bytes 1081352 | tf_op jit(solution)/shard_map/ppermute | solution.py:367
  23.1 74.9 %collective-permute-start.7 = (bf16[128,512]{1,0:T(8,128)(2,1)}, bf16[128,512]{1,0:T(8,128)(2,1)}, u32[]{:S(2)}, u32[]{:S(2)}) collective-permute-start(bf16[128,512]{1,0:T(8,128)(2,1)} %constant_dynamic-update-slice_fusion), channel_id=1, source_target_pairs={{0,4},{4,0},{8,12},{12,8},{16,20},{20,16},{24,28},{28,24},{1,5},{5... | collective-permute-start | bytes 393224 | tf_op jit(solution)/shard_map/ppermute | solution.py:368
  26.1 60.2 %copy-start.102 = (f32[128]{0:T(128)}, f32[128]{0:T(128)S(1)}, u32[]{:S(2)}) copy-start(f32[128]{0:T(128)S(1)} %fusion.120) | copy-start | bytes 1540
  27.3 68.2 %collective-permute-start.8 = (bf16[128,512]{1,0:T(8,128)(2,1)}, bf16[128,512]{1,0:T(8,128)(2,1)}, u32[]{:S(2)}, u32[]{:S(2)}) collective-permute-start(bf16[128,512]{1,0:T(8,128)(2,1)} %constant_dynamic-update-slice_fusion), channel_id=1, source_target_pairs={{0,8},{4,12},{8,16},{12,20},{16,24},{20,28},{24,0},{28,4},{1,9},{5... | collective-permute-start | bytes 393224 | tf_op jit(solution)/shard_map/ppermute | solution.py:367
  29.9 66.1 %collective-permute-start.10 = (bf16[128,512]{1,0:T(8,128)(2,1)}, bf16[128,512]{1,0:T(8,128)(2,1)}, u32[]{:S(2)}, u32[]{:S(2)}) collective-permute-start(bf16[128,512]{1,0:T(8,128)(2,1)} %constant_dynamic-update-slice_fusion), channel_id=1, source_target_pairs={{0,16},{4,20},{8,24},{12,28},{16,0},{20,4},{24,8},{28,12},{1,17},{... | collective-permute-start | bytes 393224 | tf_op jit(solution)/shard_map/ppermute | solution.py:367
  46.2 51.2 %collective-permute-start.12 = (bf16[128,512]{1,0:T(8,128)(2,1)}, bf16[128,512]{1,0:T(8,128)(2,1)}, u32[]{:S(2)}, u32[]{:S(2)}) collective-permute-start(bf16[128,512]{1,0:T(8,128)(2,1)} %constant_dynamic-update-slice_fusion), channel_id=1, source_target_pairs={{0,24},{4,28},{8,0},{12,4},{16,8},{20,12},{24,16},{28,20},{1,25},{... | collective-permute-start | bytes 393224 | tf_op jit(solution)/shard_map/ppermute | solution.py:367
  57.5 9.0 %collective-permute-start.2 = (bf16[128,1408]{1,0:T(8,128)(2,1)}, bf16[128,1408]{1,0:T(8,128)(2,1)}, u32[]{:S(2)}, u32[]{:S(2)}) collective-permute-start(bf16[128,1408]{1,0:T(8,128)(2,1)} %collective-permute-done.1), channel_id=1, source_target_pairs={{0,4},{4,0},{8,12},{12,8},{16,20},{20,16},{24,28},{28,24},{1,5},{5... | collective-permute-start | bytes 1081352 | tf_op jit(solution)/shard_map/ppermute | solution.py:369
  66.5 10.1 %collective-permute-start.4 = (bf16[128,1408]{1,0:T(8,128)(2,1)}, bf16[128,1408]{1,0:T(8,128)(2,1)}, u32[]{:S(2)}, u32[]{:S(2)}) collective-permute-start(bf16[128,1408]{1,0:T(8,128)(2,1)} %collective-permute-done.3), channel_id=1, source_target_pairs={{0,4},{4,0},{8,12},{12,8},{16,20},{20,16},{24,28},{28,24},{1,5},{5... | collective-permute-start | bytes 1081352 | tf_op jit(solution)/shard_map/ppermute | solution.py:369
  76.6 7.7 %collective-permute-start.6 = (bf16[128,1408]{1,0:T(8,128)(2,1)}, bf16[128,1408]{1,0:T(8,128)(2,1)}, u32[]{:S(2)}, u32[]{:S(2)}) collective-permute-start(bf16[128,1408]{1,0:T(8,128)(2,1)} %collective-permute-done.5), channel_id=1, source_target_pairs={{0,4},{4,0},{8,12},{12,8},{16,20},{20,16},{24,28},{28,24},{1,5},{5... | collective-permute-start | bytes 1081352 | tf_op jit(solution)/shard_map/ppermute | solution.py:369
  85.7 20.5 %copy-start.6 = (bf16[1024,1408]{0,1:T(8,128)(2,1)}, bf16[1024,1408]{0,1:T(8,128)(2,1)S(1)}, u32[]{:S(2)}) copy-start(bf16[1024,1408]{0,1:T(8,128)(2,1)S(1)} %constant_dynamic-update-slice_fusion.26) | copy-start | bytes 8650756
  88.1 69.8 %reduce-scatter.6.cloned.1.call-start = ((), (), s32[]{:S(2)}) async-start(), calls=%async_computation.6 | async-start | bytes 1310720 | tf_op jit(solution)/shard_map/reduce_scatter | solution.py:412
  90.0 31.8 %copy-start.44 = (f32[512,32]{0,1:T(8,128)}, f32[512,32]{0,1:T(8,128)S(1)}, u32[]{:S(2)}) copy-start(f32[512,32]{0,1:T(8,128)S(1)} %get-tuple-element.293) | copy-start | bytes 196612
  90.0 31.8 %copy-start.46 = (f32[512,32]{0,1:T(8,128)}, f32[512,32]{0,1:T(8,128)S(1)}, u32[]{:S(2)}) copy-start(f32[512,32]{0,1:T(8,128)S(1)} %get-tuple-element.294) | copy-start | bytes 196612
  92.8 24.2 %copy-start.75 = (f32[640]{0:T(1024)}, f32[640]{0:T(1024)S(1)}, u32[]{:S(2)}) copy-start(f32[640]{0:T(1024)S(1)} %get-tuple-element.238) | copy-start | bytes 7684
  92.8 24.2 %copy-start.77 = (f32[640]{0:T(1024)}, f32[640]{0:T(1024)S(1)}, u32[]{:S(2)}) copy-start(f32[640]{0:T(1024)S(1)} %get-tuple-element.239) | copy-start | bytes 7684
  92.8 24.2 %copy-start.79 = (f32[640]{0:T(1024)}, f32[640]{0:T(1024)S(1)}, u32[]{:S(2)}) copy-start(f32[640]{0:T(1024)S(1)} %get-tuple-element.240) | copy-start | bytes 7684
  92.8 24.2 %copy-start.81 = (f32[640]{0:T(1024)}, f32[640]{0:T(1024)S(1)}, u32[]{:S(2)}) copy-start(f32[640]{0:T(1024)S(1)} %get-tuple-element.241) | copy-start | bytes 7684
  95.4 5.7 %collective-permute-start.9 = (bf16[128,512]{1,0:T(8,128)(2,1)}, bf16[128,512]{1,0:T(8,128)(2,1)S(1)}, u32[]{:S(2)}, u32[]{:S(2)}) collective-permute-start(bf16[128,512]{1,0:T(8,128)(2,1)} %collective-permute-done.8), channel_id=1, source_target_pairs={{0,4},{4,0},{8,12},{12,8},{16,20},{20,16},{24,28},{28,24},{1,5},{5... | collective-permute-start | bytes 393224 | tf_op jit(solution)/shard_map/ppermute | solution.py:369
  96.0 7.4 %collective-permute-start.11 = (bf16[128,512]{1,0:T(8,128)(2,1)}, bf16[128,512]{1,0:T(8,128)(2,1)S(1)}, u32[]{:S(2)}, u32[]{:S(2)}) collective-permute-start(bf16[128,512]{1,0:T(8,128)(2,1)} %collective-permute-done.10), channel_id=1, source_target_pairs={{0,4},{4,0},{8,12},{12,8},{16,20},{20,16},{24,28},{28,24},{1,5},{5... | collective-permute-start | bytes 393224 | tf_op jit(solution)/shard_map/ppermute | solution.py:369
  97.4 8.1 %collective-permute-start.13 = (bf16[128,512]{1,0:T(8,128)(2,1)}, bf16[128,512]{1,0:T(8,128)(2,1)S(1)}, u32[]{:S(2)}, u32[]{:S(2)}) collective-permute-start(bf16[128,512]{1,0:T(8,128)(2,1)} %collective-permute-done.12), channel_id=1, source_target_pairs={{0,4},{4,0},{8,12},{12,8},{16,20},{20,16},{24,28},{28,24},{1,5},{5... | collective-permute-start | bytes 393224 | tf_op jit(solution)/shard_map/ppermute | solution.py:369
  134.5 51.5 %all-gather.9.cloned.1.call-start = ((), (), s32[]{:S(2)}) async-start(), calls=%async_computation.9 | async-start | bytes 1310720 | tf_op jit(solution)/shard_map/all_gather | solution.py:401
  135.3 59.8 %all-gather.7.cloned.1.call-start = ((), (), s32[]{:S(2)}) async-start(), calls=%async_computation.7 | async-start | bytes 1310720 | tf_op jit(solution)/shard_map/all_gather | solution.py:401
  139.2 19.8 %copy-start.72 = (f32[1024,1]{0,1:T(1,128)S(1)}, f32[1024,1]{0,1:T(1,128)}, u32[]{:S(2)}) copy-start(f32[1024,1]{0,1:T(1,128)} %get-tuple-element.250) | copy-start | bytes 12292
  139.2 14.2 %collective-permute-start.15 = (bf16[128,1536]{1,0:T(8,128)(2,1)}, bf16[128,1536]{1,0:T(8,128)(2,1)}, u32[]{:S(2)}, u32[]{:S(2)}) collective-permute-start(bf16[128,1536]{1,0:T(8,128)(2,1)} %constant_dynamic-update-slice_fusion.2), channel_id=1, source_target_pairs={{0,8},{4,12},{8,16},{12,20},{16,24},{20,28},{24,0},{28,4},{1,9},{5... | collective-permute-start | bytes 1179656 | tf_op jit(solution)/shard_map/ppermute | solution.py:367
  139.8 15.1 %collective-permute-start.14 = (bf16[128,1536]{1,0:T(8,128)(2,1)}, bf16[128,1536]{1,0:T(8,128)(2,1)S(1)}, u32[]{:S(2)}, u32[]{:S(2)}) collective-permute-start(bf16[128,1536]{1,0:T(8,128)(2,1)} %constant_dynamic-update-slice_fusion.2), channel_id=1, source_target_pairs={{0,4},{4,0},{8,12},{12,8},{16,20},{20,16},{24,28},{28,24},{1,5},{5... | collective-permute-start | bytes 1179656 | tf_op jit(solution)/shard_map/ppermute | solution.py:368
  141.4 24.3 %collective-permute-start.17 = (bf16[128,1536]{1,0:T(8,128)(2,1)}, bf16[128,1536]{1,0:T(8,128)(2,1)}, u32[]{:S(2)}, u32[]{:S(2)}) collective-permute-start(bf16[128,1536]{1,0:T(8,128)(2,1)} %constant_dynamic-update-slice_fusion.2), channel_id=1, source_target_pairs={{0,16},{4,20},{8,24},{12,28},{16,0},{20,4},{24,8},{28,12},{1,17},{... | collective-permute-start | bytes 1179656 | tf_op jit(solution)/shard_map/ppermute | solution.py:367
  141.4 25.8 %collective-permute-start.19 = (bf16[128,1536]{1,0:T(8,128)(2,1)}, bf16[128,1536]{1,0:T(8,128)(2,1)}, u32[]{:S(2)}, u32[]{:S(2)}) collective-permute-start(bf16[128,1536]{1,0:T(8,128)(2,1)} %constant_dynamic-update-slice_fusion.2), channel_id=1, source_target_pairs={{0,24},{4,28},{8,0},{12,4},{16,8},{20,12},{24,16},{28,20},{1,25},{... | collective-permute-start | bytes 1179656 | tf_op jit(solution)/shard_map/ppermute | solution.py:367
  153.4 14.2 %collective-permute-start.16 = (bf16[128,1536]{1,0:T(8,128)(2,1)}, bf16[128,1536]{1,0:T(8,128)(2,1)}, u32[]{:S(2)}, u32[]{:S(2)}) collective-permute-start(bf16[128,1536]{1,0:T(8,128)(2,1)} %collective-permute-done.15), channel_id=1, source_target_pairs={{0,4},{4,0},{8,12},{12,8},{16,20},{20,16},{24,28},{28,24},{1,5},{5... | collective-permute-start | bytes 1179656 | tf_op jit(solution)/shard_map/ppermute | solution.py:369
  159.0 73.9 %copy-start.98 = (f32[128]{0:T(128)}, f32[128]{0:T(128)S(1)}, u32[]{:S(2)}) copy-start(f32[128]{0:T(128)S(1)} %fusion.121) | copy-start | bytes 1540
  160.8 70.8 %reduce-scatter.10.cloned.1.call-start = ((), (), s32[]{:S(2)}) async-start(), calls=%async_computation.10 | async-start | bytes 1310720 | tf_op jit(solution)/shard_map/reduce_scatter | solution.py:412
  165.6 12.2 %collective-permute-start.18 = (bf16[128,1536]{1,0:T(8,128)(2,1)}, bf16[128,1536]{1,0:T(8,128)(2,1)S(1)}, u32[]{:S(2)}, u32[]{:S(2)}) collective-permute-start(bf16[128,1536]{1,0:T(8,128)(2,1)} %collective-permute-done.17), channel_id=1, source_target_pairs={{0,4},{4,0},{8,12},{12,8},{16,20},{20,16},{24,28},{28,24},{1,5},{5... | collective-permute-start | bytes 1179656 | tf_op jit(solution)/shard_map/ppermute | solution.py:369
  167.1 18.1 %collective-permute-start.20 = (bf16[128,1536]{1,0:T(8,128)(2,1)}, bf16[128,1536]{1,0:T(8,128)(2,1)S(1)}, u32[]{:S(2)}, u32[]{:S(2)}) collective-permute-start(bf16[128,1536]{1,0:T(8,128)(2,1)} %collective-permute-done.19), channel_id=1, source_target_pairs={{0,4},{4,0},{8,12},{12,8},{16,20},{20,16},{24,28},{28,24},{1,5},{5... | collective-permute-start | bytes 1179656 | tf_op jit(solution)/shard_map/ppermute | solution.py:369
  206.5 28.5 %copy-start.86 = (f32[2,512]{1,0:T(2,128)S(1)}, f32[2,512]{1,0:T(2,128)}, u32[]{:S(2)}) copy-start(f32[2,512]{1,0:T(2,128)} %copy-done.85) | copy-start | bytes 12292
  206.5 28.5 %copy-start.88 = (f32[2,512]{1,0:T(2,128)S(1)}, f32[2,512]{1,0:T(2,128)}, u32[]{:S(2)}) copy-start(f32[2,512]{1,0:T(2,128)} %copy-done.87) | copy-start | bytes 12292
  206.6 45.3 %all-gather.11.cloned.1.call-start = ((), (), s32[]{:S(2)}) async-start(), calls=%async_computation.11 | async-start | bytes 1310720 | tf_op jit(solution)/shard_map/all_gather | solution.py:401
  235.0 84.7 %reduce-scatter.12.cloned.1.call-start = ((), (), s32[]{:S(2)}) async-start(), calls=%async_computation.12 | async-start | bytes 1310720 | tf_op jit(solution)/shard_map/reduce_scatter | solution.py:412
  294.6 145.7 %reduce-scatter.14.cloned.1.call-start = ((), (), s32[]{:S(2)}) async-start(), calls=%async_computation.13 | async-start | bytes 1638400 | tf_op jit(solution)/shard_map/reduce_scatter | solution.py:698
  303.5 36.7 %collective-permute-start.29 = (bf16[4,128,1536]{2,1,0:T(8,128)(2,1)S(1)}, bf16[4,128,1536]{2,1,0:T(8,128)(2,1)}, u32[]{:S(2)}, u32[]{:S(2)}) collective-permute-start(bf16[4,128,1536]{2,1,0:T(8,128)(2,1)S(1)} %dynamic-slice_bitcast_fusion), channel_id=1, source_target_pairs={{0,4},{4,0},{8,12},{12,8},{16,20},{20,16},{24,28},{28,24},{1,5},{5... | collective-permute-start | bytes 4718600 | tf_op jit(solution)/shard_map/ppermute | solution.py:391
  326.9 153.1 %reduce-scatter.8.cloned.1.call-start = ((), (), s32[]{:S(2)}) async-start(), calls=%async_computation.8 | async-start | bytes 1310720 | tf_op jit(solution)/shard_map/reduce_scatter | solution.py:412
  343.5 14.2 %collective-permute-start.30 = (bf16[128,1536]{1,0:T(8,128)(2,1)}, bf16[128,1536]{1,0:T(8,128)(2,1)S(1)}, u32[]{:S(2)}, u32[]{:S(2)}) collective-permute-start(bf16[128,1536]{1,0:T(8,128)(2,1)} %get-tuple-element.255), channel_id=1, source_target_pairs={{0,8},{4,12},{8,16},{12,20},{16,24},{20,28},{24,0},{28,4},{1,9},{5... | collective-permute-start | bytes 1179656 | tf_op jit(solution)/shard_map/ppermute | solution.py:396
  344.9 28.2 %collective-permute-start.31 = (bf16[128,1536]{1,0:T(8,128)(2,1)}, bf16[128,1536]{1,0:T(8,128)(2,1)}, u32[]{:S(2)}, u32[]{:S(2)}) collective-permute-start(bf16[128,1536]{1,0:T(8,128)(2,1)} %get-tuple-element.257), channel_id=1, source_target_pairs={{0,16},{4,20},{8,24},{12,28},{16,0},{20,4},{24,8},{28,12},{1,17},{... | collective-permute-start | bytes 1179656 | tf_op jit(solution)/shard_map/ppermute | solution.py:396
  347.3 25.8 %collective-permute-start.32 = (bf16[128,1536]{1,0:T(8,128)(2,1)}, bf16[128,1536]{1,0:T(8,128)(2,1)}, u32[]{:S(2)}, u32[]{:S(2)}) collective-permute-start(bf16[128,1536]{1,0:T(8,128)(2,1)} %get-tuple-element.256), channel_id=1, source_target_pairs={{0,24},{4,28},{8,0},{12,4},{16,8},{20,12},{24,16},{28,20},{1,25},{... | collective-permute-start | bytes 1179656 | tf_op jit(solution)/shard_map/ppermute | solution.py:396
  351.9 23.3 %copy-start.95 = (f32[640]{0:T(1024)S(1)}, f32[640]{0:T(1024)}, u32[]{:S(2)}) copy-start(f32[640]{0:T(1024)} %get-tuple-element.231) | copy-start | bytes 7684
  351.9 23.3 %copy-start.94 = (f32[640]{0:T(1024)S(1)}, f32[640]{0:T(1024)}, u32[]{:S(2)}) copy-start(f32[640]{0:T(1024)} %get-tuple-element.227) | copy-start | bytes 7684
  351.9 23.3 %copy-start.93 = (f32[640]{0:T(1024)S(1)}, f32[640]{0:T(1024)}, u32[]{:S(2)}) copy-start(f32[640]{0:T(1024)} %get-tuple-element.229) | copy-start | bytes 7684
  352.0 23.3 %copy-start.92 = (f32[640]{0:T(1024)S(1)}, f32[640]{0:T(1024)}, u32[]{:S(2)}) copy-start(f32[640]{0:T(1024)} %get-tuple-element.228) | copy-start | bytes 7684
  352.0 23.4 %copy-start.112 = (f32[24]{0:T(128)S(1)}, f32[24]{0:T(128)}, u32[]{:S(2)}) copy-start(f32[24]{0:T(128)} %param.35) | copy-start | bytes 292
  352.0 23.4 %copy-start.113 = (f32[6]{0:T(128)S(1)}, f32[6]{0:T(128)}, u32[]{:S(2)}) copy-start(f32[6]{0:T(128)} %get-tuple-element.292) | copy-start | bytes 76
  352.0 23.5 %copy-start.107 = (f32[384]{0:T(512)S(1)}, f32[384]{0:T(512)}, u32[]{:S(2)}) copy-start(f32[384]{0:T(512)} %get-tuple-element.242) | copy-start | bytes 4612
  352.0 23.7 %copy-start.91 = (f32[640]{0:T(1024)S(1)}, f32[640]{0:T(1024)}, u32[]{:S(2)}) copy-start(f32[640]{0:T(1024)} %get-tuple-element.230) | copy-start | bytes 7684
  352.0 23.6 %copy-start.110 = (f32[6]{0:T(128)S(1)}, f32[6]{0:T(128)}, u32[]{:S(2)}) copy-start(f32[6]{0:T(128)} %get-tuple-element.244) | copy-start | bytes 76
  374.3 50.8 %copy-start.20 = (bf16[512,1024]{1,0:T(8,128)(2,1)S(1)}, bf16[512,1024]{1,0:T(8,128)(2,1)}, u32[]{:S(2)}) copy-start(bf16[512,1024]{1,0:T(8,128)(2,1)} %all-gather.11.cloned.1.call-done) | copy-start | bytes 3145732
  431.6 17.4 %collective-permute-start.25 = (bf16[4,128,512]{2,1,0:T(8,128)(2,1)}, bf16[4,128,512]{2,1,0:T(8,128)(2,1)}, u32[]{:S(2)}, u32[]{:S(2)}) collective-permute-start(bf16[4,128,512]{2,1,0:T(8,128)(2,1)} %fusion.63), channel_id=1, source_target_pairs={{0,4},{4,0},{8,12},{12,8},{16,20},{20,16},{24,28},{28,24},{1,5},{5... | collective-permute-start | bytes 1572872 | tf_op jit(solution)/shard_map/ppermute | solution.py:391
  447.0 26.6 %collective-permute-start.21 = (bf16[4,128,1062]{1,0,2:T(4,128)(2,1)}, bf16[4,128,1062]{1,0,2:T(4,128)(2,1)}, u32[]{:S(2)}, u32[]{:S(2)}) collective-permute-start(bf16[4,128,1062]{1,0,2:T(4,128)(2,1)} %copy.360), channel_id=1, source_target_pairs={{0,4},{4,0},{8,12},{12,8},{16,20},{20,16},{24,28},{28,24},{1,5},{5... | collective-permute-start | bytes 3262472 | tf_op jit(solution)/shard_map/ppermute | solution.py:391
  450.3 8.3 %collective-permute-start.26 = (bf16[128,512]{1,0:T(8,128)(2,1)S(1)}, bf16[128,512]{1,0:T(8,128)(2,1)S(1)}, u32[]{:S(2)}, u32[]{:S(2)}) collective-permute-start(bf16[128,512]{1,0:T(8,128)(2,1)S(1)} %get-tuple-element.274), channel_id=1, source_target_pairs={{0,8},{4,12},{8,16},{12,20},{16,24},{20,28},{24,0},{28,4},{1,9},{5... | collective-permute-start | bytes 393224 | tf_op jit(solution)/shard_map/ppermute | solution.py:396
  450.4 12.7 %collective-permute-start.27 = (bf16[128,512]{1,0:T(8,128)(2,1)S(1)}, bf16[128,512]{1,0:T(8,128)(2,1)S(1)}, u32[]{:S(2)}, u32[]{:S(2)}) collective-permute-start(bf16[128,512]{1,0:T(8,128)(2,1)S(1)} %get-tuple-element.276), channel_id=1, source_target_pairs={{0,16},{4,20},{8,24},{12,28},{16,0},{20,4},{24,8},{28,12},{1,17},{... | collective-permute-start | bytes 393224 | tf_op jit(solution)/shard_map/ppermute | solution.py:396
  450.5 12.6 %collective-permute-start.28 = (bf16[128,512]{1,0:T(8,128)(2,1)S(1)}, bf16[128,512]{1,0:T(8,128)(2,1)S(1)}, u32[]{:S(2)}, u32[]{:S(2)}) collective-permute-start(bf16[128,512]{1,0:T(8,128)(2,1)S(1)} %get-tuple-element.275), channel_id=1, source_target_pairs={{0,24},{4,28},{8,0},{12,4},{16,8},{20,12},{24,16},{28,20},{1,25},{... | collective-permute-start | bytes 393224 | tf_op jit(solution)/shard_map/ppermute | solution.py:396
  476.1 11.6 %collective-permute-start.22 = (bf16[128,1062]{0,1:T(8,128)(2,1)}, bf16[128,1062]{0,1:T(8,128)(2,1)S(1)}, u32[]{:S(2)}, u32[]{:S(2)}) collective-permute-start(bf16[128,1062]{0,1:T(8,128)(2,1)} %get-tuple-element.264), channel_id=1, source_target_pairs={{0,8},{4,12},{8,16},{12,20},{16,24},{20,28},{24,0},{28,4},{1,9},{5... | collective-permute-start | bytes 815624 | tf_op jit(solution)/shard_map/ppermute | solution.py:396
  476.1 21.8 %collective-permute-start.23 = (bf16[128,1062]{0,1:T(8,128)(2,1)S(1)}, bf16[128,1062]{0,1:T(8,128)(2,1)S(1)}, u32[]{:S(2)}, u32[]{:S(2)}) collective-permute-start(bf16[128,1062]{0,1:T(8,128)(2,1)S(1)} %get-tuple-element.266), channel_id=1, source_target_pairs={{0,16},{4,20},{8,24},{12,28},{16,0},{20,4},{24,8},{28,12},{1,17},{... | collective-permute-start | bytes 815624 | tf_op jit(solution)/shard_map/ppermute | solution.py:396
  476.1 21.8 %collective-permute-start.24 = (bf16[128,1062]{0,1:T(8,128)(2,1)S(1)}, bf16[128,1062]{0,1:T(8,128)(2,1)}, u32[]{:S(2)}, u32[]{:S(2)}) collective-permute-start(bf16[128,1062]{0,1:T(8,128)(2,1)S(1)} %get-tuple-element.265), channel_id=1, source_target_pairs={{0,24},{4,28},{8,0},{12,4},{16,8},{20,12},{24,16},{28,20},{1,25},{... | collective-permute-start | bytes 815624 | tf_op jit(solution)/shard_map/ppermute | solution.py:396
  (103 other events, 449.0 us)
Sparse Core Ops, SparseCore 0:
  88.2 14.0 all-gather.4
  134.6 23.1 reduce-scatter.5
  159.5 16.7 all-gather.8
  178.3 16.7 all-gather.6
  206.7 24.8 reduce-scatter.9
  235.1 16.7 all-gather.10
  294.7 24.9 reduce-scatter.11
  327.0 26.5 reduce-scatter.13
  356.1 25.0 reduce-scatter.7

commit v3 on v2

--- a/solution.py
+++ b/solution.py
@@ -353,10 +353,25 @@
     return [(index, (index + 2 * steps) % count) for index in range(count)]
 
 
+def gather_far(piece):
+    count = lax.axis_size("dp")
+    if not staged(count):
+        return [piece]
+    far = [lax.ppermute(piece, "dp", shift_pairs(count, steps)) for steps in range(1, count // 2)]
+    near = lax.ppermute(piece, "dp", partner_pairs(count))
+    return [piece, near] + far
+
+
 def gather_dp(piece):
+    return gather_rest(gather_far(piece))
+
+
+def gather_rest(parts):
+    piece = parts[0]
     count = lax.axis_size("dp")
-    if count > 8 or count % 2:
+    if not staged(count):
         return lax.all_gather(piece, "dp", axis=0, tiled=True)
+    near, far = parts[1], parts[2:]
     mine = lax.axis_index("dp")
     rows = piece.shape[0]
     result = jnp.zeros((count * rows,) + piece.shape[1:], piece.dtype)
@@ -364,8 +379,6 @@
     def put(result, block, source):
         return lax.dynamic_update_slice_in_dim(result, block, source * rows, 0)
 
-    far = [lax.ppermute(piece, "dp", shift_pairs(count, steps)) for steps in range(1, count // 2)]
-    near = lax.ppermute(piece, "dp", partner_pairs(count))
     crossed = [lax.ppermute(block, "dp", partner_pairs(count)) for block in far]
     other = mine + 1 - 2 * (mine % 2)
     result = put(result, piece, mine)
@@ -376,20 +389,29 @@
     return result
 
 
-def reduce_dp(partial):
+def staged(count):
+    return count <= 8 and count % 2 == 0
+
+
+def reduce_pair(partial):
     count = lax.axis_size("dp")
+    if not staged(count):
+        return partial
     rows = partial.shape[0] // count
-    if count > 8 or count % 2:
-        return lax.psum_scatter(partial, "dp", scatter_dimension=0, tiled=True).astype(jnp.float32)
-    mine = lax.axis_index("dp")
-    side = mine % 2
-    place = mine // 2
-    half_count = count // 2
-    split = partial.reshape((half_count, 2, rows) + partial.shape[1:])
+    side = lax.axis_index("dp") % 2
+    split = partial.reshape((count // 2, 2, rows) + partial.shape[1:])
     sent = lax.dynamic_index_in_dim(split, 1 - side, 1, keepdims=False)
     kept = lax.dynamic_index_in_dim(split, side, 1, keepdims=False)
     arrived = lax.ppermute(sent, "dp", partner_pairs(count))
-    paired = (kept.astype(jnp.float32) + arrived.astype(jnp.float32)).astype(jnp.bfloat16)
+    return (kept.astype(jnp.float32) + arrived.astype(jnp.float32)).astype(jnp.bfloat16)
+
+
+def reduce_far(paired):
+    count = lax.axis_size("dp")
+    if not staged(count):
+        return lax.psum_scatter(paired, "dp", scatter_dimension=0, tiled=True).astype(jnp.float32)
+    place = lax.axis_index("dp") // 2
+    half_count = count // 2
     total = lax.dynamic_index_in_dim(paired, place, 0, keepdims=False).astype(jnp.float32)
     for steps in range(1, half_count):
         block = lax.dynamic_index_in_dim(paired, (place + steps) % half_count, 0, keepdims=False)
@@ -475,8 +497,15 @@
             [mamba_gate, mamba_input, state_weight, query_weight, key_own, value_own, narrow], 1
         )
     )
-    out_pack = gather_dp(jnp.concatenate([attention_out, mamba_out], 1))
-    mlp_pack = gather_dp(jnp.concatenate([gate_weight, up_weight, down_weight], 1))
+    mix_pack, out_own, mlp_own = lax.optimization_barrier(
+        (
+            mix_pack,
+            jnp.concatenate([attention_out, mamba_out], 1),
+            jnp.concatenate([gate_weight, up_weight, down_weight], 1),
+        )
+    )
+    out_pack = gather_dp(out_own)
+    mlp_parts = gather_far(mlp_own)
 
     def take(pack, widths):
         pieces, start = [], 0
@@ -494,7 +523,6 @@
     mix_gain_all = narrow_all[:, scan_heads]
     mlp_gain_all = narrow_all[:, scan_heads + 1]
     attention_all, mamba_out_all = take(out_pack, (query_width, scan_width))
-    gate_all, up_all, down_all = take(mlp_pack, (unit_count,) * 3)
     full_width = SSM_HEADS * SSM_HEAD_DIM
     kernel_local = jnp.concatenate(
         [
@@ -562,7 +590,10 @@
         step_local,
         skip_local,
     )
-    gated_low = gated_out.astype(jnp.bfloat16)
+    gated_low, mlp_parts = lax.optimization_barrier(
+        (gated_out.astype(jnp.bfloat16), mlp_parts)
+    )
+    gate_all, up_all, down_all = take(gather_rest(mlp_parts), (unit_count,) * 3)
     mixed = summed_rows(((attended_low, attention_all), (gated_low, mamba_out_all)), local_rows)
     hidden = rows_float + mixed
     normed_mlp, second_norm_back = jax.vjp(rms_norm, hidden, mlp_gain_all.astype(jnp.float32))
@@ -584,12 +615,15 @@
     up_grad = (unit_grad * silu_gate).astype(jnp.bfloat16)
     grad_gate = weight_grad(mlp_rows, gate_grad)
     grad_up = weight_grad(mlp_rows, up_grad)
+    low = jnp.bfloat16
+    mlp_paired = reduce_pair(jnp.concatenate([grad_gate, grad_up, grad_down], 1).astype(low))
     mlp_input_grad = summed_rows(((gate_grad, gate_all), (up_grad, up_all)), local_rows)
     hidden_norm_grad, grad_mlp_gain = second_norm_back(mlp_input_grad)
     hidden_grad = cotangent.astype(jnp.float32) + hidden_norm_grad
     mixer_grad_rows = full_rows(hidden_grad.astype(jnp.bfloat16))
     grad_attention = weight_grad(mixer_grad_rows, attended_low)
     grad_mamba_out = weight_grad(mixer_grad_rows, gated_low)
+    out_paired = reduce_pair(jnp.concatenate([grad_attention, grad_mamba_out], 1).astype(low))
     attended_grad = (
         jnp.dot(mixer_grad_rows, attention_all, preferred_element_type=jnp.float32)
         .astype(jnp.bfloat16)
@@ -648,6 +682,11 @@
     input_proj_low = input_proj_grad.astype(jnp.bfloat16)
     state_proj_low = state_proj_grad.astype(jnp.bfloat16)
     step_proj_low = step_proj_grad.astype(jnp.bfloat16)
+    gate_proj_low, input_proj_low, mlp_paired, out_paired = lax.optimization_barrier(
+        (gate_proj_low, input_proj_low, mlp_paired, out_paired)
+    )
+    mlp_sum_pack = reduce_far(mlp_paired)
+    out_sum_pack = reduce_far(out_paired)
     mixer_input_grad = summed_rows(
         (
             (query_low, query_all),
@@ -682,7 +721,6 @@
     grad_step = weight_grad(mixer_rows, step_proj_low)
     count = lax.axis_size("dp")
     tensor_size = lax.axis_size("tensor")
-    low = jnp.bfloat16
     shared = jnp.concatenate(
         [
             grad_key,
@@ -702,9 +740,7 @@
         tiled=True,
     )
     shared = shared.reshape(D, shared_width // tensor_size)
-    mlp_sum_pack = reduce_dp(jnp.concatenate([grad_gate, grad_up, grad_down], 1).astype(low))
-    out_sum_pack = reduce_dp(jnp.concatenate([grad_attention, grad_mamba_out], 1).astype(low))
-    mix_sum_pack = reduce_dp(
+    mix_paired = reduce_pair(
         jnp.concatenate(
             [
                 grad_gate_ssm.astype(low),
@@ -716,6 +752,10 @@
             1,
         )
     )
+    mix_paired, mlp_sum_pack, out_sum_pack = lax.optimization_barrier(
+        (mix_paired, mlp_sum_pack, out_sum_pack)
+    )
+    mix_sum_pack = reduce_far(mix_paired)
     mlp_sums = take(mlp_sum_pack, (unit_count,) * 3)
     attention_sum, mamba_out_sum = take(out_sum_pack, (query_width, scan_width))
     gate_ssm_sum, input_ssm_sum, query_sum, shared_sum, step_sum = take(
@@ -735,10 +775,10 @@
     )
     small_rows = -(-small_own.shape[0] // 1024) * 8
     small_own = jnp.pad(small_own, (0, small_rows * 128 - small_own.shape[0]))
-    small_every = lax.all_gather(
-        small_own.reshape(small_rows, 128), ("dp", "tensor"), axis=0, tiled=True
-    )
-    small_tensor = jnp.sum(small_every.reshape(count, tensor_size, -1), 0)
+    small_every = gather_dp(small_own.reshape(small_rows, 128))
+    small_sum = jnp.sum(small_every.reshape(count, small_rows, 128), 0)
+    small_tensor = lax.all_gather(small_sum, "tensor", axis=0, tiled=True)
+    small_tensor = small_tensor.reshape(tensor_size, -1)
     local_width = kernel_grad.shape[1]
     taps = small_tensor[:, : KCONV * local_width].reshape(tensor_size, KCONV, local_width)
     bias_start = KCONV * local_width

time: 520 us -> 513 us (0.987)
  waiting for transfers between devices: 147 us -> 192 us
  blocking collectives: 48.5 us -> 5.56 us
  local copies, waits for them, and re-layouts: 116 us -> 105 us
  matrix products: 79.4 us -> 71.4 us
  other arithmetic: 34.6 us -> 40.9 us
  starting transfers between devices: 64.1 us -> 69.3 us
    all_gather x1, blocking collectives: 48.5 us -> 5.56 us  [local(): small_tensor = lax.all_gather(small_sum, 'tensor', axis=0, tiled=True)]
    ppermute x33 -> x40, waiting for transfers between devices: 99.5 us -> 139 us  [the longest x3 44.6 us: reduce_pair(): arrived = lax.ppermute(sent, 'dp', partner_pairs(count))]
    reduce_scatter x4, waiting for transfers between devices: 27.4 us -> 42.9 us  [summed_rows(): lax.psum_scatter(running.astype(jnp.bfloat16), 'tensor', scatter_dimensio...]
    all_gather x4, waiting for transfers between devices: 19.6 us -> 8.96 us  [full_rows(): return lax.all_gather(local_piece, 'tensor', axis=0, tiled=True)]
    ppermute x33 -> x40, starting transfers between devices: 62.8 us -> 68.3 us  [the longest x12 24.8 us: gather_far(): lax.ppermute(piece, 'dp', shift_pairs(count, steps))]
    dot_general x12, matrix products: 29 us -> 23.6 us  [summed_rows(): lax.dot_general(left_side, right_side, by_columns, preferred_element_type...]
    dynamic_update_slice x24 -> x32, local copies, waits for them, and re-layouts: 26.9 us -> 23.6 us  [put(): return lax.dynamic_update_slice_in_dim(result, block, source * rows, 0)]
    unnamed x258 -> x199, local copies, waits for them, and re-layouts: 19.3 us -> 16.9 us
  transfers between devices with their start and end apart: 42 -> 49, of which waited for: 20 -> 21; matrix products, arithmetic and copies ran while one was open for 26% -> 28% of each run, Pallas kernels for 0% -> 0%
where the time goes in v3:
time: 513 us; the launch traced here: 506 us
  waiting for transfers between devices  192 us (37%)
  local copies, waits for them, and re-layouts  105 us (20%)
  matrix products  71.4 us (14%)
  starting transfers between devices  69.3 us (14%)
  other arithmetic  40.9 us (8%)
  between operations  16 us (3%)
  blocking collectives  5.56 us (1%)
  Pallas kernels  5.52 us (1%)
    ppermute x3, waiting for transfers between devices, reduce_pair(): arrived = lax.ppermute(sent, 'dp', partner_pairs(count))  44.6 us
    reduce_scatter x4, waiting for transfers between devices, summed_rows(): lax.psum_scatter(running.astype(jnp.bfloat16), 'tensor', scatter_dimensio...  42.9 us
    ppermute x12, waiting for transfers between devices, gather_far(): lax.ppermute(piece, 'dp', shift_pairs(count, steps))  37.1 us
    ppermute x9, waiting for transfers between devices, reduce_far(): lax.ppermute(block, 'dp', shift_pairs(count, steps)).astype(jnp.float32)  35.8 us
    ppermute x12, starting transfers between devices, gather_far(): lax.ppermute(piece, 'dp', shift_pairs(count, steps))  24.8 us
    ppermute x9, starting transfers between devices, reduce_far(): lax.ppermute(block, 'dp', shift_pairs(count, steps)).astype(jnp.float32)  24.1 us
    dynamic_update_slice x32, local copies, waits for them, and re-layouts, put(): return lax.dynamic_update_slice_in_dim(result, block, source * rows, 0)  23.6 us
    dot_general x12, matrix products, summed_rows(): lax.dot_general(left_side, right_side, by_columns, preferred_element_type...  23.6 us
  transfers between devices with their start and end apart: 49, of which 21 were waited for; matrix products, arithmetic and copies ran while one was open for 28% of the time, Pallas kernels for 0%

profile of v3, /device:TPU:0, one launch (start us, length us, event | category | flops | bytes accessed | tf_op | source)
XLA Modules:
  0.0 505.9 jit_solution(17424517107468416001)
XLA Ops:
  11.6 3.0 collective-permute-start
  16.2 2.6 collective-permute-start.3
  29.2 1.9 copy.276
  31.6 10.5 %collective-permute-done.3 = bf16[128,1408]{1,0:T(8,128)(2,1)} collective-permute-done((bf16[128,1408]{1,0:T(8,128)(2,1)S(1)}, bf16[128,1408]{1,0:T(8,128)(2,1)}, u32[]{:S(2)}, u32[]{:S(2)}) %collective-permute-start.3) | collective-permute-done | bytes 360480 | tf_op jit(solution)/shard_map/ppermute | solution.py:360
  42.1 1.9 copy.278
  44.4 1.9 copy.280
  50.4 1.9 copy.277
  55.5 1.9 copy.279
  58.7 3.5 collective-permute-done.6
  66.7 5.0 collective-permute-start.8
  75.7 3.5 collective-permute-start.16
  83.8 25.0 %collective-permute-done.10 = bf16[128,512]{1,0:T(8,128)(2,1)S(1)} collective-permute-done((bf16[128,512]{1,0:T(8,128)(2,1)S(1)}, bf16[128,512]{1,0:T(8,128)(2,1)S(1)}, u32[]{:S(2)}, u32[]{:S(2)}) %collective-permute-start.10) | collective-permute-done | bytes 131104 | tf_op jit(solution)/shard_map/ppermute | solution.py:360
  108.8 1.9 collective-permute-start.12
  114.2 3.4 collective-permute-start.17
  119.5 3.1 collective-permute-done.13
  125.4 1.8 fusion.67
  127.2 2.0 fusion.44
  130.2 1.9 fusion.10
  135.2 3.3 multiply_convert_fusion.3
  140.3 1.9 fusion.37
  148.0 2.4 add_convert_fusion.2
  151.8 1.9 broadcast_in_dim.92
  155.4 1.8 constant_dynamic-update-slice_fusion.14
  157.2 15.5 %reduce-scatter.6.cloned.1.call-done = bf16[128,1024]{1,0:T(8,128)(2,1)} async-done(((bf16[512,1024]{1,0:T(8,128)(2,1)}), bf16[128,1024]{1,0:T(8,128)(2,1)}) %reduce-scatter.6.cloned.1.call-update) | async-done | bytes 262160 | tf_op jit(solution)/shard_map/reduce_scatter | solution.py:434
  181.3 1.9 constant_dynamic-update-slice_fusion.11
  183.1 6.5 %collective-permute-done.19 = bf16[128,1536]{1,0:T(8,128)(2,1)S(1)} collective-permute-done((bf16[128,1536]{1,0:T(8,128)(2,1)}, bf16[128,1536]{1,0:T(8,128)(2,1)S(1)}, u32[]{:S(2)}, u32[]{:S(2)}) %collective-permute-start.19) | collective-permute-done | bytes 393248 | tf_op jit(solution)/shard_map/ppermute | solution.py:382
  190.5 1.8 constant_dynamic-update-slice_fusion.9
  192.3 4.7 collective-permute-done.20
  197.7 3.3 convolution_bitcast_fusion
  201.0 9.0 %all-gather.7.cloned.1.call-done = bf16[512,1024]{1,0:T(8,128)(2,1)} async-done(((bf16[128,1024]{1,0:T(8,128)(2,1)}), bf16[512,1024]{1,0:T(8,128)(2,1)}) %all-gather.7.cloned.1.call-update) | async-done | bytes 1048592 | tf_op jit(solution)/shard_map/all_gather | solution.py:423
  209.9 2.4 fusion.24
  212.3 3.2 multiply_convert_fusion.1
  216.4 2.0 fusion.22
  218.3 2.9 add_convert_fusion.1
  221.4 3.1 fusion.7
  224.5 2.6 concatenate.106
  227.0 3.7 copy.296
  230.7 2.2 convolution_convert_fusion.2
  238.8 7.6 %reduce-scatter.10.cloned.1.call-done = bf16[128,1024]{1,0:T(8,128)(2,1)} async-done(((bf16[512,1024]{1,0:T(8,128)(2,1)}), bf16[128,1024]{1,0:T(8,128)(2,1)}) %reduce-scatter.10.cloned.1.call-update) | async-done | bytes 262160 | tf_op jit(solution)/shard_map/reduce_scatter | solution.py:434
  246.4 1.9 fusion.54
  248.3 2.0 fusion.123
  250.8 23.4 %collective-permute-done.21 = bf16[4,128,1536]{2,1,0:T(8,128)(2,1)} collective-permute-done((bf16[4,128,1536]{2,1,0:T(8,128)(2,1)}, bf16[4,128,1536]{2,1,0:T(8,128)(2,1)}, u32[]{:S(2)}, u32[]{:S(2)}) %collective-permute-start.21) | collective-permute-done | bytes 1572896 | tf_op jit(solution)/shard_map/ppermute | solution.py:405
  274.2 3.5 fusion
  277.6 4.2 multiply_reduce_fusion.4
  281.8 3.9 transpose_jvp___.1
  298.1 1.9 split.11
  305.3 2.7 fusion.81
  308.0 2.8 fusion.73
  315.5 1.8 collective-permute-done.22
  320.4 1.9 add_convert_fusion
  327.6 19.9 %reduce-scatter.12.cloned.1.call-done = bf16[128,1024]{1,0:T(8,128)(2,1)} async-done(((bf16[512,1024]{1,0:T(8,128)(2,1)}), bf16[128,1024]{1,0:T(8,128)(2,1)}) %reduce-scatter.12.cloned.1.call-update) | async-done | bytes 262160 | tf_op jit(solution)/shard_map/reduce_scatter | solution.py:434
  351.0 3.5 concatenate.118
  354.8 3.1 convolution_convert_fusion.3
  361.5 2.4 collective-permute-start.36
  373.3 5.6 %all_gather.19 = f32[128,128]{1,0:T(8,128)S(1)} all-gather(f32[32,128]{1,0:T(8,128)S(1)} %reduce_sum.220), channel_id=1, replica_groups=mesh['dp'=8,'tensor'=4] {'tensor'}, dimensions={0}, use_global_device_ids=true | all-gather | bytes 81920 | tf_op jit(solution)/shard_map/all_gather | solution.py:780
  384.3 2.8 convolution_convert_fusion.4
  392.9 3.3 collective-permute-start.29
  402.2 18.2 %collective-permute-done.29 = bf16[128,512]{1,0:T(8,128)(2,1)S(1)} collective-permute-done((bf16[128,512]{1,0:T(8,128)(2,1)}, bf16[128,512]{1,0:T(8,128)(2,1)S(1)}, u32[]{:S(2)}, u32[]{:S(2)}) %collective-permute-start.29) | collective-permute-done | bytes 131104 | tf_op jit(solution)/shard_map/ppermute | solution.py:418
  420.5 15.8 %collective-permute-start.27 = (bf16[128,512]{1,0:T(8,128)(2,1)}, bf16[128,512]{1,0:T(8,128)(2,1)S(1)}, u32[]{:S(2)}, u32[]{:S(2)}) collective-permute-start(bf16[128,512]{1,0:T(8,128)(2,1)} %get-tuple-element.285), channel_id=1, source_target_pairs={{0,8},{4,12},{8,16},{12,20},{16,24},{20,28},{24,0},{28,4},{1,9},{5... | collective-permute-start | bytes 393224 | tf_op jit(solution)/shard_map/ppermute | solution.py:418
  437.6 4.0 copy.315
  444.5 2.3 fusion.33
  446.9 19.3 %collective-permute-done.23 = bf16[4,128,1062]{1,0,2:T(4,128)(2,1)S(1)} collective-permute-done((bf16[4,128,1062]{1,0,2:T(4,128)(2,1)S(1)}, bf16[4,128,1062]{1,0,2:T(4,128)(2,1)S(1)}, u32[]{:S(2)}, u32[]{:S(2)}) %collective-permute-start.23) | collective-permute-done | bytes 1087520 | tf_op jit(solution)/shard_map/ppermute | solution.py:405
  470.8 2.2 fusion.58
  476.0 16.7 %collective-permute-done.31 = bf16[128,1062]{0,1:T(8,128)(2,1)} collective-permute-done((bf16[128,1062]{0,1:T(8,128)(2,1)}, bf16[128,1062]{0,1:T(8,128)(2,1)}, u32[]{:S(2)}, u32[]{:S(2)}) %collective-permute-start.31) | collective-permute-done | bytes 271904 | tf_op jit(solution)/shard_map/ppermute | solution.py:418
  (466 shorter events, 160.7 us)
Async XLA Ops:
  7.2 116.1 %all-gather.5.cloned.1.call-start = ((), (), s32[]{:S(2)}) async-start(), calls=%async_computation.5 | async-start | bytes 1310720 | tf_op jit(solution)/shard_map/all_gather | solution.py:423
  11.6 36.3 %collective-permute-start = (bf16[128,1408]{1,0:T(8,128)(2,1)S(1)}, bf16[128,1408]{1,0:T(8,128)(2,1)}, u32[]{:S(2)}, u32[]{:S(2)}) collective-permute-start(bf16[128,1408]{1,0:T(8,128)(2,1)S(1)} %concatenate.93), channel_id=1, source_target_pairs={{0,4},{4,0},{8,12},{12,8},{16,20},{20,16},{24,28},{28,24},{1,5},{5... | collective-permute-start | bytes 1081352 | tf_op jit(solution)/shard_map/ppermute | solution.py:361
  14.6 14.5 %collective-permute-start.1 = (bf16[128,1408]{1,0:T(8,128)(2,1)S(1)}, bf16[128,1408]{1,0:T(8,128)(2,1)}, u32[]{:S(2)}, u32[]{:S(2)}) collective-permute-start(bf16[128,1408]{1,0:T(8,128)(2,1)S(1)} %concatenate.93), channel_id=1, source_target_pairs={{0,8},{4,12},{8,16},{12,20},{16,24},{20,28},{24,0},{28,4},{1,9},{5... | collective-permute-start | bytes 1081352 | tf_op jit(solution)/shard_map/ppermute | solution.py:360
  16.2 25.8 %collective-permute-start.3 = (bf16[128,1408]{1,0:T(8,128)(2,1)S(1)}, bf16[128,1408]{1,0:T(8,128)(2,1)}, u32[]{:S(2)}, u32[]{:S(2)}) collective-permute-start(bf16[128,1408]{1,0:T(8,128)(2,1)S(1)} %concatenate.93), channel_id=1, source_target_pairs={{0,16},{4,20},{8,24},{12,28},{16,0},{20,4},{24,8},{28,12},{1,17},{... | collective-permute-start | bytes 1081352 | tf_op jit(solution)/shard_map/ppermute | solution.py:360
  18.8 25.6 %collective-permute-start.5 = (bf16[128,1408]{1,0:T(8,128)(2,1)S(1)}, bf16[128,1408]{1,0:T(8,128)(2,1)}, u32[]{:S(2)}, u32[]{:S(2)}) collective-permute-start(bf16[128,1408]{1,0:T(8,128)(2,1)S(1)} %concatenate.93), channel_id=1, source_target_pairs={{0,24},{4,28},{8,0},{12,4},{16,8},{20,12},{24,16},{28,20},{1,25},{... | collective-permute-start | bytes 1081352 | tf_op jit(solution)/shard_map/ppermute | solution.py:360
  31.1 19.3 %collective-permute-start.2 = (bf16[128,1408]{1,0:T(8,128)(2,1)}, bf16[128,1408]{1,0:T(8,128)(2,1)}, u32[]{:S(2)}, u32[]{:S(2)}) collective-permute-start(bf16[128,1408]{1,0:T(8,128)(2,1)} %collective-permute-done.1), channel_id=1, source_target_pairs={{0,4},{4,0},{8,12},{12,8},{16,20},{20,16},{24,28},{28,24},{1,5},{5... | collective-permute-start | bytes 1081352 | tf_op jit(solution)/shard_map/ppermute | solution.py:382
  43.9 11.6 %collective-permute-start.4 = (bf16[128,1408]{1,0:T(8,128)(2,1)}, bf16[128,1408]{1,0:T(8,128)(2,1)}, u32[]{:S(2)}, u32[]{:S(2)}) collective-permute-start(bf16[128,1408]{1,0:T(8,128)(2,1)} %collective-permute-done.3), channel_id=1, source_target_pairs={{0,4},{4,0},{8,12},{12,8},{16,20},{20,16},{24,28},{28,24},{1,5},{5... | collective-permute-start | bytes 1081352 | tf_op jit(solution)/shard_map/ppermute | solution.py:382
  46.4 15.9 %collective-permute-start.6 = (bf16[128,1408]{1,0:T(8,128)(2,1)}, bf16[128,1408]{1,0:T(8,128)(2,1)}, u32[]{:S(2)}, u32[]{:S(2)}) collective-permute-start(bf16[128,1408]{1,0:T(8,128)(2,1)} %collective-permute-done.5), channel_id=1, source_target_pairs={{0,4},{4,0},{8,12},{12,8},{16,20},{20,16},{24,28},{28,24},{1,5},{5... | collective-permute-start | bytes 1081352 | tf_op jit(solution)/shard_map/ppermute | solution.py:382
  63.6 59.7 %copy-start.6 = (bf16[1024,1408]{0,1:T(8,128)(2,1)}, bf16[1024,1408]{0,1:T(8,128)(2,1)S(1)}, u32[]{:S(2)}) copy-start(bf16[1024,1408]{0,1:T(8,128)(2,1)S(1)} %constant_dynamic-update-slice_fusion.24) | copy-start | bytes 8650756
  64.5 108.2 %reduce-scatter.6.cloned.1.call-start = ((), (), s32[]{:S(2)}) async-start(), calls=%async_computation.6 | async-start | bytes 1310720 | tf_op jit(solution)/shard_map/reduce_scatter | solution.py:434
  66.2 14.7 %collective-permute-start.7 = (bf16[128,512]{1,0:T(8,128)(2,1)}, bf16[128,512]{1,0:T(8,128)(2,1)}, u32[]{:S(2)}, u32[]{:S(2)}) collective-permute-start(bf16[128,512]{1,0:T(8,128)(2,1)} %pad_maximum_fusion.3), channel_id=1, source_target_pairs={{0,4},{4,0},{8,12},{12,8},{16,20},{20,16},{24,28},{28,24},{1,5},{5... | collective-permute-start | bytes 393224 | tf_op jit(solution)/shard_map/ppermute | solution.py:361
  66.7 14.2 %collective-permute-start.8 = (bf16[128,512]{1,0:T(8,128)(2,1)}, bf16[128,512]{1,0:T(8,128)(2,1)S(1)}, u32[]{:S(2)}, u32[]{:S(2)}) collective-permute-start(bf16[128,512]{1,0:T(8,128)(2,1)} %pad_maximum_fusion.3), channel_id=1, source_target_pairs={{0,8},{4,12},{8,16},{12,20},{16,24},{20,28},{24,0},{28,4},{1,9},{5... | collective-permute-start | bytes 393224 | tf_op jit(solution)/shard_map/ppermute | solution.py:360
  72.5 60.6 %copy-start.91 = (f32[6]{0:T(128)}, f32[6]{0:T(128)S(1)}, u32[]{:S(2)}) copy-start(f32[6]{0:T(128)S(1)} %fusion.122) | copy-start | bytes 76
  74.1 61.0 %copy-start.70 = (f32[384]{0:T(512)}, f32[384]{0:T(512)S(1)}, u32[]{:S(2)}) copy-start(f32[384]{0:T(512)S(1)} %mul.722) | copy-start | bytes 4612
  74.2 64.3 %collective-permute-start.14 = (bf16[128,1536]{1,0:T(8,128)(2,1)}, bf16[128,1536]{1,0:T(8,128)(2,1)}, u32[]{:S(2)}, u32[]{:S(2)}) collective-permute-start(bf16[128,1536]{1,0:T(8,128)(2,1)} %pad_maximum_fusion.2), channel_id=1, source_target_pairs={{0,4},{4,0},{8,12},{12,8},{16,20},{20,16},{24,28},{28,24},{1,5},{5... | collective-permute-start | bytes 1179656 | tf_op jit(solution)/shard_map/ppermute | solution.py:361
  75.7 62.7 %collective-permute-start.15 = (bf16[128,1536]{1,0:T(8,128)(2,1)}, bf16[128,1536]{1,0:T(8,128)(2,1)}, u32[]{:S(2)}, u32[]{:S(2)}) collective-permute-start(bf16[128,1536]{1,0:T(8,128)(2,1)} %pad_maximum_fusion.2), channel_id=1, source_target_pairs={{0,8},{4,12},{8,16},{12,20},{16,24},{20,28},{24,0},{28,4},{1,9},{5... | collective-permute-start | bytes 1179656 | tf_op jit(solution)/shard_map/ppermute | solution.py:360
  75.7 62.7 %collective-permute-start.16 = (bf16[128,1536]{1,0:T(8,128)(2,1)}, bf16[128,1536]{1,0:T(8,128)(2,1)}, u32[]{:S(2)}, u32[]{:S(2)}) collective-permute-start(bf16[128,1536]{1,0:T(8,128)(2,1)} %pad_maximum_fusion.2), channel_id=1, source_target_pairs={{0,16},{4,20},{8,24},{12,28},{16,0},{20,4},{24,8},{28,12},{1,17},{... | collective-permute-start | bytes 1179656 | tf_op jit(solution)/shard_map/ppermute | solution.py:360
  81.0 27.8 %collective-permute-start.10 = (bf16[128,512]{1,0:T(8,128)(2,1)S(1)}, bf16[128,512]{1,0:T(8,128)(2,1)S(1)}, u32[]{:S(2)}, u32[]{:S(2)}) collective-permute-start(bf16[128,512]{1,0:T(8,128)(2,1)S(1)} %copy-done.46), channel_id=1, source_target_pairs={{0,16},{4,20},{8,24},{12,28},{16,0},{20,4},{24,8},{28,12},{1,17},{... | collective-permute-start | bytes 393224 | tf_op jit(solution)/shard_map/ppermute | solution.py:360
  81.0 29.7 %collective-permute-start.9 = (bf16[128,512]{1,0:T(8,128)(2,1)S(1)}, bf16[128,512]{1,0:T(8,128)(2,1)S(1)}, u32[]{:S(2)}, u32[]{:S(2)}) collective-permute-start(bf16[128,512]{1,0:T(8,128)(2,1)S(1)} %collective-permute-done.8), channel_id=1, source_target_pairs={{0,4},{4,0},{8,12},{12,8},{16,20},{20,16},{24,28},{28,24},{1,5},{5... | collective-permute-start | bytes 393224 | tf_op jit(solution)/shard_map/ppermute | solution.py:382
  108.8 5.4 %collective-permute-start.12 = (bf16[128,512]{1,0:T(8,128)(2,1)S(1)}, bf16[128,512]{1,0:T(8,128)(2,1)S(1)}, u32[]{:S(2)}, u32[]{:S(2)}) collective-permute-start(bf16[128,512]{1,0:T(8,128)(2,1)S(1)} %copy-done.46), channel_id=1, source_target_pairs={{0,24},{4,28},{8,0},{12,4},{16,8},{20,12},{24,16},{28,20},{1,25},{... | collective-permute-start | bytes 393224 | tf_op jit(solution)/shard_map/ppermute | solution.py:360
  110.7 6.9 %collective-permute-start.11 = (bf16[128,512]{1,0:T(8,128)(2,1)S(1)}, bf16[128,512]{1,0:T(8,128)(2,1)S(1)}, u32[]{:S(2)}, u32[]{:S(2)}) collective-permute-start(bf16[128,512]{1,0:T(8,128)(2,1)S(1)} %collective-permute-done.10), channel_id=1, source_target_pairs={{0,4},{4,0},{8,12},{12,8},{16,20},{20,16},{24,28},{28,24},{1,5},{5... | collective-permute-start | bytes 393224 | tf_op jit(solution)/shard_map/ppermute | solution.py:382
  114.2 24.3 %collective-permute-start.17 = (bf16[128,1536]{1,0:T(8,128)(2,1)}, bf16[128,1536]{1,0:T(8,128)(2,1)}, u32[]{:S(2)}, u32[]{:S(2)}) collective-permute-start(bf16[128,1536]{1,0:T(8,128)(2,1)} %pad_maximum_fusion.2), channel_id=1, source_target_pairs={{0,24},{4,28},{8,0},{12,4},{16,8},{20,12},{24,16},{28,20},{1,25},{... | collective-permute-start | bytes 1179656 | tf_op jit(solution)/shard_map/ppermute | solution.py:360
  117.6 5.0 collective-permute-start.13
  150.4 47.3 %all-gather.9.cloned.1.call-start = ((), (), s32[]{:S(2)}) async-start(), calls=%async_computation.9 | async-start | bytes 1310720 | tf_op jit(solution)/shard_map/all_gather | solution.py:423
  151.1 58.8 %all-gather.7.cloned.1.call-start = ((), (), s32[]{:S(2)}) async-start(), calls=%async_computation.7 | async-start | bytes 1310720 | tf_op jit(solution)/shard_map/all_gather | solution.py:423
  151.2 28.3 %collective-permute-start.18 = (bf16[128,1536]{1,0:T(8,128)(2,1)}, bf16[128,1536]{1,0:T(8,128)(2,1)}, u32[]{:S(2)}, u32[]{:S(2)}) collective-permute-start(bf16[128,1536]{1,0:T(8,128)(2,1)} %collective-permute-done.15), channel_id=1, source_target_pairs={{0,4},{4,0},{8,12},{12,8},{16,20},{20,16},{24,28},{28,24},{1,5},{5... | collective-permute-start | bytes 1179656 | tf_op jit(solution)/shard_map/ppermute | solution.py:382
  173.8 74.4 %copy-start.73 = (f32[128]{0:T(128)}, f32[128]{0:T(128)S(1)}, u32[]{:S(2)}) copy-start(f32[128]{0:T(128)S(1)} %fusion.116) | copy-start | bytes 1540
  175.6 70.8 %reduce-scatter.10.cloned.1.call-start = ((), (), s32[]{:S(2)}) async-start(), calls=%async_computation.10 | async-start | bytes 1310720 | tf_op jit(solution)/shard_map/reduce_scatter | solution.py:434
  177.5 12.2 %collective-permute-start.19 = (bf16[128,1536]{1,0:T(8,128)(2,1)}, bf16[128,1536]{1,0:T(8,128)(2,1)S(1)}, u32[]{:S(2)}, u32[]{:S(2)}) collective-permute-start(bf16[128,1536]{1,0:T(8,128)(2,1)} %collective-permute-done.16), channel_id=1, source_target_pairs={{0,4},{4,0},{8,12},{12,8},{16,20},{20,16},{24,28},{28,24},{1,5},{5... | collective-permute-start | bytes 1179656 | tf_op jit(solution)/shard_map/ppermute | solution.py:382
  178.9 18.0 %collective-permute-start.20 = (bf16[128,1536]{1,0:T(8,128)(2,1)}, bf16[128,1536]{1,0:T(8,128)(2,1)S(1)}, u32[]{:S(2)}, u32[]{:S(2)}) collective-permute-start(bf16[128,1536]{1,0:T(8,128)(2,1)} %collective-permute-done.17), channel_id=1, source_target_pairs={{0,4},{4,0},{8,12},{12,8},{16,20},{20,16},{24,28},{28,24},{1,5},{5... | collective-permute-start | bytes 1179656 | tf_op jit(solution)/shard_map/ppermute | solution.py:382
  221.3 56.3 %all-gather.11.cloned.1.call-start = ((), (), s32[]{:S(2)}) async-start(), calls=%async_computation.11 | async-start | bytes 1310720 | tf_op jit(solution)/shard_map/all_gather | solution.py:423
  237.3 36.8 %collective-permute-start.21 = (bf16[4,128,1536]{2,1,0:T(8,128)(2,1)}, bf16[4,128,1536]{2,1,0:T(8,128)(2,1)}, u32[]{:S(2)}, u32[]{:S(2)}) collective-permute-start(bf16[4,128,1536]{2,1,0:T(8,128)(2,1)} %dynamic-slice_bitcast_fusion), channel_id=1, source_target_pairs={{0,4},{4,0},{8,12},{12,8},{16,20},{20,16},{24,28},{28,24},{1,5},{5... | collective-permute-start | bytes 4718600 | tf_op jit(solution)/shard_map/ppermute | solution.py:405
  248.2 29.4 %copy-start.82 = (f32[128]{0:T(128)}, f32[128]{0:T(128)S(1)}, u32[]{:S(2)}) copy-start(f32[128]{0:T(128)S(1)} %multiply_multiply_fusion.1) | copy-start | bytes 1540
  250.3 97.2 %reduce-scatter.12.cloned.1.call-start = ((), (), s32[]{:S(2)}) async-start(), calls=%async_computation.12 | async-start | bytes 1310720 | tf_op jit(solution)/shard_map/reduce_scatter | solution.py:434
  250.8 26.8 %copy-start.71 = (f32[384]{0:T(512)S(1)}, f32[384]{0:T(512)}, u32[]{:S(2)}) copy-start(f32[384]{0:T(512)} %copy-done.70) | copy-start | bytes 4612
  290.1 24.9 %copy-start.37 = (bf16[512,256]{1,0:T(8,128)(2,1)}, bf16[512,256]{1,0:T(8,128)(2,1)S(1)}, u32[]{:S(2)}) copy-start(bf16[512,256]{1,0:T(8,128)(2,1)S(1)} %add_convert_fusion.4) | copy-start | bytes 786436
  303.8 13.6 %collective-permute-start.22 = (bf16[4,128,512]{2,1,0:T(8,128)(2,1)}, bf16[4,128,512]{2,1,0:T(8,128)(2,1)}, u32[]{:S(2)}, u32[]{:S(2)}) collective-permute-start(bf16[4,128,512]{2,1,0:T(8,128)(2,1)} %fusion.62), channel_id=1, source_target_pairs={{0,4},{4,0},{8,12},{12,8},{16,20},{20,16},{24,28},{28,24},{1,5},{5... | collective-permute-start | bytes 1572872 | tf_op jit(solution)/shard_map/ppermute | solution.py:405
  322.4 76.0 %reduce-scatter.14.cloned.1.call-start = ((), (), s32[]{:S(2)}) async-start(), calls=%async_computation.13 | async-start | bytes 1638400 | tf_op jit(solution)/shard_map/reduce_scatter | solution.py:736
  354.6 116.1 %reduce-scatter.8.cloned.1.call-start = ((), (), s32[]{:S(2)}) async-start(), calls=%async_computation.8 | async-start | bytes 1310720 | tf_op jit(solution)/shard_map/reduce_scatter | solution.py:434
  358.5 23.6 %copy-start.48 = (bf16[512,384]{1,0:T(8,128)(2,1)S(1)}, bf16[512,384]{1,0:T(8,128)(2,1)}, u32[]{:S(2)}) copy-start(bf16[512,384]{1,0:T(8,128)(2,1)} %get-tuple-element.103) | copy-start | bytes 1179652
  358.5 11.7 %collective-permute-start.33 = (f32[32,128]{1,0:T(8,128)S(1)}, f32[32,128]{1,0:T(8,128)S(1)}, u32[]{:S(2)}, u32[]{:S(2)}) collective-permute-start(f32[32,128]{1,0:T(8,128)S(1)} %pad_bitcast_fusion), channel_id=1, source_target_pairs={{0,4},{4,0},{8,12},{12,8},{16,20},{20,16},{24,28},{28,24},{1,5},{5... | collective-permute-start | bytes 49160 | tf_op jit(solution)/shard_map/ppermute | solution.py:361
  360.0 7.6 %collective-permute-start.34 = (f32[32,128]{1,0:T(8,128)S(1)}, f32[32,128]{1,0:T(8,128)S(1)}, u32[]{:S(2)}, u32[]{:S(2)}) collective-permute-start(f32[32,128]{1,0:T(8,128)S(1)} %pad_bitcast_fusion), channel_id=1, source_target_pairs={{0,8},{4,12},{8,16},{12,20},{16,24},{20,28},{24,0},{28,4},{1,9},{5... | collective-permute-start | bytes 49160 | tf_op jit(solution)/shard_map/ppermute | solution.py:360
  361.5 6.6 %collective-permute-start.36 = (f32[32,128]{1,0:T(8,128)S(1)}, f32[32,128]{1,0:T(8,128)S(1)}, u32[]{:S(2)}, u32[]{:S(2)}) collective-permute-start(f32[32,128]{1,0:T(8,128)S(1)} %pad_bitcast_fusion), channel_id=1, source_target_pairs={{0,16},{4,20},{8,24},{12,28},{16,0},{20,4},{24,8},{28,12},{1,17},{... | collective-permute-start | bytes 49160 | tf_op jit(solution)/shard_map/ppermute | solution.py:360
  363.9 5.7 %collective-permute-start.38 = (f32[32,128]{1,0:T(8,128)S(1)}, f32[32,128]{1,0:T(8,128)S(1)}, u32[]{:S(2)}, u32[]{:S(2)}) collective-permute-start(f32[32,128]{1,0:T(8,128)S(1)} %pad_bitcast_fusion), channel_id=1, source_target_pairs={{0,24},{4,28},{8,0},{12,4},{16,8},{20,12},{24,16},{28,20},{1,25},{... | collective-permute-start | bytes 49160 | tf_op jit(solution)/shard_map/ppermute | solution.py:360
  367.6 3.7 collective-permute-start.35
  368.1 3.7 collective-permute-start.37
  369.6 3.7 collective-permute-start.39
  389.6 54.8 %collective-permute-start.26 = (bf16[128,1536]{1,0:T(8,128)(2,1)}, bf16[128,1536]{1,0:T(8,128)(2,1)}, u32[]{:S(2)}, u32[]{:S(2)}) collective-permute-start(bf16[128,1536]{1,0:T(8,128)(2,1)} %get-tuple-element.267), channel_id=1, source_target_pairs={{0,24},{4,28},{8,0},{12,4},{16,8},{20,12},{24,16},{28,20},{1,25},{... | collective-permute-start | bytes 1179656 | tf_op jit(solution)/shard_map/ppermute | solution.py:418
  390.9 53.6 %collective-permute-start.25 = (bf16[128,1536]{1,0:T(8,128)(2,1)}, bf16[128,1536]{1,0:T(8,128)(2,1)}, u32[]{:S(2)}, u32[]{:S(2)}) collective-permute-start(bf16[128,1536]{1,0:T(8,128)(2,1)} %get-tuple-element.268), channel_id=1, source_target_pairs={{0,16},{4,20},{8,24},{12,28},{16,0},{20,4},{24,8},{28,12},{1,17},{... | collective-permute-start | bytes 1179656 | tf_op jit(solution)/shard_map/ppermute | solution.py:418
  391.7 52.8 %collective-permute-start.24 = (bf16[128,1536]{1,0:T(8,128)(2,1)}, bf16[128,1536]{1,0:T(8,128)(2,1)}, u32[]{:S(2)}, u32[]{:S(2)}) collective-permute-start(bf16[128,1536]{1,0:T(8,128)(2,1)} %get-tuple-element.266), channel_id=1, source_target_pairs={{0,8},{4,12},{8,16},{12,20},{16,24},{20,28},{24,0},{28,4},{1,9},{5... | collective-permute-start | bytes 1179656 | tf_op jit(solution)/shard_map/ppermute | solution.py:418
  392.9 27.5 %collective-permute-start.29 = (bf16[128,512]{1,0:T(8,128)(2,1)}, bf16[128,512]{1,0:T(8,128)(2,1)S(1)}, u32[]{:S(2)}, u32[]{:S(2)}) collective-permute-start(bf16[128,512]{1,0:T(8,128)(2,1)} %get-tuple-element.286), channel_id=1, source_target_pairs={{0,24},{4,28},{8,0},{12,4},{16,8},{20,12},{24,16},{28,20},{1,25},{... | collective-permute-start | bytes 393224 | tf_op jit(solution)/shard_map/ppermute | solution.py:418
  396.3 45.3 %collective-permute-start.28 = (bf16[128,512]{1,0:T(8,128)(2,1)}, bf16[128,512]{1,0:T(8,128)(2,1)}, u32[]{:S(2)}, u32[]{:S(2)}) collective-permute-start(bf16[128,512]{1,0:T(8,128)(2,1)} %get-tuple-element.287), channel_id=1, source_target_pairs={{0,16},{4,20},{8,24},{12,28},{16,0},{20,4},{24,8},{28,12},{1,17},{... | collective-permute-start | bytes 393224 | tf_op jit(solution)/shard_map/ppermute | solution.py:418
  420.5 22.3 %collective-permute-start.27 = (bf16[128,512]{1,0:T(8,128)(2,1)}, bf16[128,512]{1,0:T(8,128)(2,1)S(1)}, u32[]{:S(2)}, u32[]{:S(2)}) collective-permute-start(bf16[128,512]{1,0:T(8,128)(2,1)} %get-tuple-element.285), channel_id=1, source_target_pairs={{0,8},{4,12},{8,16},{12,20},{16,24},{20,28},{24,0},{28,4},{1,9},{5... | collective-permute-start | bytes 393224 | tf_op jit(solution)/shard_map/ppermute | solution.py:418
  441.6 24.6 %collective-permute-start.23 = (bf16[4,128,1062]{1,0,2:T(4,128)(2,1)S(1)}, bf16[4,128,1062]{1,0,2:T(4,128)(2,1)S(1)}, u32[]{:S(2)}, u32[]{:S(2)}) collective-permute-start(bf16[4,128,1062]{1,0,2:T(4,128)(2,1)S(1)} %copy.315), channel_id=1, source_target_pairs={{0,4},{4,0},{8,12},{12,8},{16,20},{20,16},{24,28},{28,24},{1,5},{5... | collective-permute-start | bytes 3262472 | tf_op jit(solution)/shard_map/ppermute | solution.py:405
  446.8 23.9 %copy-start.18 = (bf16[128,1024]{1,0:T(8,128)(2,1)S(1)}, bf16[128,1024]{1,0:T(8,128)(2,1)}, u32[]{:S(2)}) copy-start(bf16[128,1024]{1,0:T(8,128)(2,1)} %reduce-scatter.6.cloned.1.call-done) | copy-start | bytes 786436
  446.8 23.9 %copy-start.27 = (bf16[128,1024]{1,0:T(8,128)(2,1)S(1)}, bf16[128,1024]{1,0:T(8,128)(2,1)}, u32[]{:S(2)}) copy-start(bf16[128,1024]{1,0:T(8,128)(2,1)} %param.22) | copy-start | bytes 786436
  446.9 23.9 %copy-start.28 = (bf16[128,1024]{1,0:T(8,128)(2,1)S(1)}, bf16[128,1024]{1,0:T(8,128)(2,1)}, u32[]{:S(2)}) copy-start(bf16[128,1024]{1,0:T(8,128)(2,1)} %reduce-scatter.10.cloned.1.call-done) | copy-start | bytes 786436
  446.9 23.9 %copy-start.34 = (bf16[128,1024]{1,0:T(8,128)(2,1)S(1)}, bf16[128,1024]{1,0:T(8,128)(2,1)}, u32[]{:S(2)}) copy-start(bf16[128,1024]{1,0:T(8,128)(2,1)} %reduce-scatter.12.cloned.1.call-done) | copy-start | bytes 786436
  446.9 23.9 %copy-start.74 = (f32[128]{0:T(128)S(1)}, f32[128]{0:T(128)}, u32[]{:S(2)}) copy-start(f32[128]{0:T(128)} %copy-done.73) | copy-start | bytes 1540
  446.9 23.9 %copy-start.80 = (f32[128]{0:T(128)S(1)}, f32[128]{0:T(128)}, u32[]{:S(2)}) copy-start(f32[128]{0:T(128)} %fusion.115) | copy-start | bytes 1540
  446.9 23.9 %copy-start.83 = (f32[128]{0:T(128)S(1)}, f32[128]{0:T(128)}, u32[]{:S(2)}) copy-start(f32[128]{0:T(128)} %copy-done.82) | copy-start | bytes 1540
  468.7 7.3 %collective-permute-start.32 = (bf16[128,1062]{0,1:T(8,128)(2,1)}, bf16[128,1062]{0,1:T(8,128)(2,1)}, u32[]{:S(2)}, u32[]{:S(2)}) collective-permute-start(bf16[128,1062]{0,1:T(8,128)(2,1)} %get-tuple-element.276), channel_id=1, source_target_pairs={{0,24},{4,28},{8,0},{12,4},{16,8},{20,12},{24,16},{28,20},{1,25},{... | collective-permute-start | bytes 815624 | tf_op jit(solution)/shard_map/ppermute | solution.py:418
  468.7 24.0 %collective-permute-start.31 = (bf16[128,1062]{0,1:T(8,128)(2,1)}, bf16[128,1062]{0,1:T(8,128)(2,1)}, u32[]{:S(2)}, u32[]{:S(2)}) collective-permute-start(bf16[128,1062]{0,1:T(8,128)(2,1)} %get-tuple-element.277), channel_id=1, source_target_pairs={{0,16},{4,20},{8,24},{12,28},{16,0},{20,4},{24,8},{28,12},{1,17},{... | collective-permute-start | bytes 815624 | tf_op jit(solution)/shard_map/ppermute | solution.py:418
  470.4 22.3 %collective-permute-start.30 = (bf16[128,1062]{0,1:T(8,128)(2,1)}, bf16[128,1062]{0,1:T(8,128)(2,1)}, u32[]{:S(2)}, u32[]{:S(2)}) collective-permute-start(bf16[128,1062]{0,1:T(8,128)(2,1)} %get-tuple-element.275), channel_id=1, source_target_pairs={{0,8},{4,12},{8,16},{12,20},{16,24},{20,28},{24,0},{28,4},{1,9},{5... | collective-permute-start | bytes 815624 | tf_op jit(solution)/shard_map/ppermute | solution.py:418
  (80 other events, 337.4 us)
Sparse Core Ops, SparseCore 0:
  64.6 21.4 all-gather.4
  150.5 22.1 reduce-scatter.5
  174.3 16.7 all-gather.8
  193.2 16.7 all-gather.6
  221.4 24.8 reduce-scatter.9
  250.4 16.7 all-gather.10
  322.5 24.9 reduce-scatter.11
  354.7 26.8 reduce-scatter.13
  384.2 24.8 reduce-scatter.7
